TPU v7x, 32 devices: a whole 2x2x4 slice. The times are simulated.
32 devices in a mesh: shard: 4 (over y, core), ctx: 2 (over x), tp: 4 (over z).
Axes of the slice: x: 2, y: 2, z: 4, core: 2. Of those that a mesh axis runs over, the one named last changes fastest.
Arguments:
- inputs: bfloat16 [4, 768, 1024], P('shard', ('ctx', 'tp')), may hold values from -6 to 6
- cotangent: bfloat16 [4, 768, 1024], P('shard', ('ctx', 'tp')), may hold values from -6 to 6
- lengths: int32 [4], P('shard'), may hold values from 576 to 768, as said below
- buckets: int32 [73], replicated, may hold values from 0 to 72, each once
- ffn1_in: bfloat16 [1024, 4096], P(('shard', 'ctx'), 'tp'), may hold values from -0.1875 to 0.1875
- ffn1_out: bfloat16 [1024, 4096], P(('shard', 'ctx'), 'tp'), may hold values from -0.25 to 0.25
- norm_gains: bfloat16 [1024, 5], P(('shard', 'ctx')), may hold values from 0.5 to 1.5
- norm_biases: bfloat16 [1024, 5], P(('shard', 'ctx')), may hold values from -1.5 to 1.5
- qkv_weight: bfloat16 [1024, 3, 1024], P(('shard', 'ctx'), None, 'tp'), may hold values from -0.1875 to 0.1875
- attn_out: bfloat16 [1024, 1024], P(('shard', 'ctx'), 'tp'), may hold values from -0.5 to 0.5
- distance: bfloat16 [64, 73], P(('shard', 'ctx')), may hold values from -6 to 6
- glu_in: bfloat16 [1024, 2, 1024], P(('shard', 'ctx'), None, 'tp'), may hold values from -0.1875 to 0.1875
- depthwise: bfloat16 [1024, 31], P(('tp', 'shard', 'ctx')), may hold values from -1 to 1
- conv_gain: bfloat16 [1024], P(('tp', 'shard', 'ctx')), may hold values from 0.5 to 1.5
- conv_bias: bfloat16 [1024], P(('tp', 'shard', 'ctx')), may hold values from -1.5 to 1.5
- conv_out: bfloat16 [1024, 1024], P(('shard', 'ctx'), 'tp'), may hold values from -0.25 to 0.25
- ffn2_in: bfloat16 [1024, 4096], P(('shard', 'ctx'), 'tp'), may hold values from -0.1875 to 0.1875
- ffn2_out: bfloat16 [1024, 4096], P(('shard', 'ctx'), 'tp'), may hold values from -0.25 to 0.25
Outputs:
- activations: bfloat16 [4, 768, 1024], P('shard', ('ctx', 'tp'))
- input_grad: float32 [4, 768, 1024], P('shard', ('ctx', 'tp'))
- grad_ffn1_in: float32 [1024, 4096], P(('shard', 'ctx'), 'tp')
- grad_ffn1_out: float32 [1024, 4096], P(('shard', 'ctx'), 'tp')
- grad_norm_gains: float32 [1024, 5], P(('shard', 'ctx'))
- grad_norm_biases: float32 [1024, 5], P(('shard', 'ctx'))
- grad_qkv_weight: float32 [1024, 3, 1024], P(('shard', 'ctx'), None, 'tp')
- grad_attn_out: float32 [1024, 1024], P(('shard', 'ctx'), 'tp')
- grad_distance: float32 [64, 73], P(('shard', 'ctx'))
- grad_glu_in: float32 [1024, 2, 1024], P(('shard', 'ctx'), None, 'tp')
- grad_depthwise: float32 [1024, 31], P(('tp', 'shard', 'ctx'))
- grad_conv_gain: float32 [1024], P(('tp', 'shard', 'ctx'))
- grad_conv_bias: float32 [1024], P(('tp', 'shard', 'ctx'))
- grad_conv_out: float32 [1024, 1024], P(('shard', 'ctx'), 'tp')
- grad_ffn2_in: float32 [1024, 4096], P(('shard', 'ctx'), 'tp')
- grad_ffn2_out: float32 [1024, 4096], P(('shard', 'ctx'), 'tp')
Inputs may be any that keep to these rules, and one draw needn't show every extreme that they name: `lengths`: one clip has all 768 frames valid and one clip has exactly 576. `buckets`: each row of the distance table serves exactly one offset.
All inputs are finite; a program needn't handle non-finite values.
Results may differ from a plain program's by a relative error of at most 0.034.
Values may be sent and summed in bfloat16 or wider, within the bound.
No kernel may reach another device: no remote copies, remote signals or barrier semaphores. Data moves between devices by JAX's collectives and lax.ppermute only.
A program may use at most 128 MiB of HBM per device.

v0:
```python
import jax
import jax.numpy as jnp
from jax import lax
from jax.sharding import PartitionSpec as P

D = 1024
HD = 64
KERNEL = 31
LEFT = 64
SPAN = 73


EPSILON = 1e-05
MASKED = -1e30


def extended_2(block, sides, width):
    for axis, dim in sides:
        count = lax.axis_size(axis)
        forward = [(i, i + 1) for i in range(count - 1)]
        backward = [(target, source) for source, target in forward]
        low = lax.ppermute(
            lax.slice_in_dim(block, block.shape[dim] - width, None, axis=dim), axis, forward
        )
        high = lax.ppermute(lax.slice_in_dim(block, 0, width, axis=dim), axis, backward)
        block = jnp.concatenate([low, block, high], axis=dim)
    return block


def from_behind(value, axis, steps):
    count = lax.axis_size(axis)
    initial, last = (max(0, -steps), min(count, count - steps))
    return lax.ppermute(value, axis, [(source, source + steps) for source in range(initial, last)])


def product(left, right):
    return jnp.dot(left, right, preferred_element_type=jnp.float32)


def product_nt(left, right):
    return lax.dot_general(
        left, right, (((1,), (1,)), ((), ())), preferred_element_type=jnp.float32
    )


def product_tn(left, right):
    return lax.dot_general(
        left, right, (((0,), (0,)), ((), ())), preferred_element_type=jnp.float32
    )


def silu_slope(values):
    logistic = jax.nn.sigmoid(values)
    return logistic * (1.0 + values * (1.0 - logistic))


def norm_rows(stream, gain, offset):
    centre = stream - jnp.mean(stream, axis=-1, keepdims=True)
    inverse = lax.rsqrt(jnp.mean(centre * centre, axis=-1, keepdims=True) + EPSILON)
    normal = centre * inverse
    return (normal * gain + offset, normal, inverse)


def norm_back(upstream, normal, inverse, gain):
    scaled = upstream * gain
    inward = inverse * (
        scaled
        - jnp.mean(scaled, axis=-1, keepdims=True)
        - normal * jnp.mean(scaled * normal, axis=-1, keepdims=True)
    )
    return (inward, jnp.sum(upstream * normal, axis=0), jnp.sum(upstream, axis=0))


def skewed(relative, columns):
    height = relative.shape[0]
    padded = jnp.pad(relative, ((0, 0), (0, columns + 1 - relative.shape[1])))
    return padded.reshape(-1)[: height * columns].reshape(height, columns)


def unskewed(grid, span_cols):
    height, columns = grid.shape
    flat = jnp.pad(grid.reshape(-1), (0, height))
    return flat.reshape(height, columns + 1)[:, :span_cols]


def gather_pair(couple):
    return (
        lax.all_gather(couple[0], ("shard", "ctx"), axis=0, tiled=True),
        lax.all_gather(couple[1], ("shard", "ctx"), axis=0, tiled=True),
    )


def gather_five(bundle):
    return (
        lax.all_gather(bundle[0], ("shard", "ctx"), axis=0, tiled=True),
        lax.all_gather(bundle[1], ("shard", "ctx"), axis=0, tiled=True),
        lax.all_gather(bundle[2], ("shard", "ctx"), axis=0, tiled=True),
        lax.all_gather(bundle[3], ("shard", "ctx"), axis=0, tiled=True),
        lax.all_gather(bundle[4], ("shard", "ctx"), axis=0, tiled=True),
    )


def settle_pair(couple):
    return (
        lax.psum_scatter(couple[0], ("shard", "ctx"), scatter_dimension=0, tiled=True),
        lax.psum_scatter(couple[1], ("shard", "ctx"), scatter_dimension=0, tiled=True),
    )


def settle_five(bundle):
    return (
        lax.psum_scatter(bundle[0], ("shard", "ctx"), scatter_dimension=0, tiled=True),
        lax.psum_scatter(bundle[1], ("shard", "ctx"), scatter_dimension=0, tiled=True),
        lax.psum_scatter(bundle[2], ("shard", "ctx"), scatter_dimension=0, tiled=True),
        lax.psum_scatter(bundle[3], ("shard", "ctx"), scatter_dimension=0, tiled=True),
        lax.psum_scatter(bundle[4], ("shard", "ctx"), scatter_dimension=0, tiled=True),
    )


def widen(stream_rows):
    return lax.all_gather(stream_rows, "tp", axis=0, tiled=True)


def narrow(partial_value):
    return lax.psum_scatter(
        partial_value.astype(jnp.bfloat16), "tp", scatter_dimension=0, tiled=True
    ).astype(jnp.float32)


def widen_grad(stream_rows):
    return lax.all_gather(stream_rows, "tp", axis=0, tiled=True)


def narrow_grad(partial_value):
    return lax.psum_scatter(
        partial_value.astype(jnp.bfloat16), "tp", scatter_dimension=0, tiled=True
    ).astype(jnp.float32)


def sum_over_tp(couple):
    return lax.psum((couple[0], couple[1]), "tp")


def head_forward(query_rows, key_rows, value_rows, rel_table, setting):
    columns = key_rows.shape[0]
    scores = (
        product_nt(query_rows, key_rows) + skewed(product(query_rows, rel_table), columns)
    ) * setting["scaling"]
    masked = jnp.where(setting["allowed"], scores, MASKED)
    ceiling = jnp.max(masked, axis=-1, keepdims=True)
    raised = jnp.where(setting["in_band"], jnp.exp(masked - ceiling), 0.0)
    denominator = jnp.sum(raised, axis=-1, keepdims=True)
    weights = (raised / denominator).astype(jnp.bfloat16)
    return (product(weights, value_rows), ceiling, denominator)


def head_backward(
    query_rows, key_rows, value_rows, ceiling, denominator, upstream, rel_table, setting
):
    columns = key_rows.shape[0]
    span_cols = rel_table.shape[1]
    scores = (
        product_nt(query_rows, key_rows) + skewed(product(query_rows, rel_table), columns)
    ) * setting["scaling"]
    masked = jnp.where(setting["allowed"], scores, MASKED)
    chance = jnp.where(setting["in_band"], jnp.exp(masked - ceiling), 0.0) / denominator
    weights = chance.astype(jnp.bfloat16)
    d_chance = product_nt(upstream, value_rows)
    d_value = product_tn(weights, upstream)
    inner_sum = jnp.sum(d_chance * chance, axis=-1, keepdims=True)
    d_scores = jnp.where(setting["allowed"], chance * (d_chance - inner_sum), 0.0).astype(
        jnp.bfloat16
    )
    d_relative = unskewed(d_scores, span_cols)
    d_query = (product(d_scores, key_rows) + product_nt(d_relative, rel_table)) * setting["scaling"]
    d_key = product_tn(d_scores, query_rows) * setting["scaling"]
    d_table = product_tn(query_rows, d_relative) * setting["scaling"]
    return (d_query, d_key, d_value, d_table)


def depth_mix(extended, kernel_taps, height):
    mixed = extended[0:height] * kernel_taps[:, 0]
    for offset in range(1, kernel_taps.shape[1]):
        mixed = mixed + extended[offset : offset + height] * kernel_taps[:, offset]
    return mixed


def ffn_forward(stream, gain, offset, weight_in, weight_out):
    normed, normal, inverse = norm_rows(stream, gain, offset)
    hidden = widen(normed.astype(jnp.bfloat16))
    before = product(hidden, weight_in)
    active = jax.nn.silu(before).astype(jnp.bfloat16)
    result = stream + 0.5 * narrow(product_nt(active, weight_out))
    return (result, (normal, inverse, hidden, before, active))


def ffn_backward(d_stream, gain, stored_ffn, weight_in, weight_out):
    normal, inverse, hidden, before, active = stored_ffn
    d_branch = widen_grad((0.5 * d_stream).astype(jnp.bfloat16))
    d_active = product(d_branch, weight_out)
    grad_out = product_tn(d_branch, active)
    d_before = (d_active * silu_slope(before)).astype(jnp.bfloat16)
    grad_in = product_tn(hidden, d_before)
    d_normed = narrow_grad(product_nt(d_before, weight_in))
    d_input, d_gain, d_offset = norm_back(d_normed, normal, inverse, gain)
    return (d_stream + d_input, d_gain, d_offset, grad_in, grad_out)


def attn_forward(stream, gain, offset, qkv_all, attn_all, table_all, setting):
    normed, normal, inverse = norm_rows(stream, gain, offset)
    hidden = widen(normed.astype(jnp.bfloat16))
    height = hidden.shape[0]
    channels = qkv_all.shape[2]
    local_heads = channels // HD
    project = jnp.einsum("fd,dkc->fkc", hidden, qkv_all, preferred_element_type=jnp.float32).astype(
        jnp.bfloat16
    )
    key_value = project[:, 1:].reshape(height, 2 * channels)
    widened = extended_2(key_value, (("ctx", 0),), LEFT)
    columns = widened.shape[0]
    query_heads = project[:, 0].reshape(height, local_heads, HD).transpose(1, 0, 2)
    key_heads = widened[:, :channels].reshape(columns, local_heads, HD).transpose(1, 0, 2)
    value_heads = widened[:, channels:].reshape(columns, local_heads, HD).transpose(1, 0, 2)
    rel_table = product(table_all, setting["selector"]).astype(jnp.bfloat16)

    def one_head(triple):
        return head_forward(triple[0], triple[1], triple[2], rel_table, setting)

    context, ceiling, denominator = lax.map(one_head, (query_heads, key_heads, value_heads))
    context = context.transpose(1, 0, 2).reshape(height, channels).astype(jnp.bfloat16)
    result = stream + narrow(product_nt(context, attn_all))
    return (
        result,
        (
            normal,
            inverse,
            hidden,
            query_heads,
            key_heads,
            value_heads,
            ceiling,
            denominator,
            context,
            rel_table,
        ),
    )


def attn_backward(d_stream, gain, stored_attn, qkv_all, attn_all, setting):
    (
        normal,
        inverse,
        hidden,
        query_heads,
        key_heads,
        value_heads,
        ceiling,
        denominator,
        context,
        rel_table,
    ) = stored_attn
    height = hidden.shape[0]
    channels = context.shape[1]
    local_heads = query_heads.shape[0]
    columns = key_heads.shape[1]
    d_branch = widen_grad(d_stream.astype(jnp.bfloat16))
    grad_out = product_tn(d_branch, context)
    d_context = product(d_branch, attn_all).astype(jnp.bfloat16)
    d_heads = d_context.reshape(height, local_heads, HD).transpose(1, 0, 2)

    def one_head(bundle):
        return head_backward(
            bundle[0], bundle[1], bundle[2], bundle[3], bundle[4], bundle[5], rel_table, setting
        )

    d_query, d_key, d_value, d_table = lax.map(
        one_head, (query_heads, key_heads, value_heads, ceiling, denominator, d_heads)
    )
    d_pairs = jnp.concatenate(
        [
            d_key.transpose(1, 0, 2).reshape(columns, channels),
            d_value.transpose(1, 0, 2).reshape(columns, channels),
        ],
        1,
    )
    outer_rims = jnp.concatenate([d_pairs[:LEFT], d_pairs[LEFT + height :]], 0)
    returned = extended_2(outer_rims.astype(jnp.bfloat16), (("ctx", 0),), LEFT).astype(
        outer_rims.dtype
    )
    d_pairs = d_pairs[LEFT : LEFT + height]
    d_pairs = d_pairs + jnp.pad(returned[:LEFT], ((0, height - LEFT), (0, 0)))
    d_pairs = d_pairs + jnp.pad(returned[3 * LEFT :], ((height - LEFT, 0), (0, 0)))
    d_project = jnp.concatenate([d_query.transpose(1, 0, 2).reshape(height, channels), d_pairs], 1)
    d_project = d_project.reshape(height, 3, channels).astype(jnp.bfloat16)
    grad_qkv = jnp.einsum("fd,fkc->dkc", hidden, d_project, preferred_element_type=jnp.float32)
    d_normed = narrow_grad(
        jnp.einsum("fkc,dkc->fd", d_project, qkv_all, preferred_element_type=jnp.float32)
    )
    d_input, d_gain, d_offset = norm_back(d_normed, normal, inverse, gain)
    d_rel = jnp.sum(d_table, axis=0)
    grad_table = jnp.dot(
        d_rel, setting["selector"].astype(jnp.float32).T, precision=lax.Precision.HIGHEST
    )
    return (d_stream + d_input, d_gain, d_offset, grad_qkv, grad_out, grad_table)


def conv_forward(stream, gain, offset, conv_set, setting):
    glu_all, depth_all, scale_all, shift_all, out_all = conv_set
    normed, normal, inverse = norm_rows(stream, gain, offset)
    hidden = widen(normed.astype(jnp.bfloat16))
    height = hidden.shape[0]
    halves = jnp.einsum("fd,dkc->kfc", hidden, glu_all, preferred_element_type=jnp.float32)
    logistic = jax.nn.sigmoid(halves[1])
    gated = (halves[0] * logistic * setting["live_rows"]).astype(jnp.bfloat16)
    earlier = from_behind(gated[height - (KERNEL - 1) :], "ctx", 1)
    extended = jnp.concatenate([earlier, gated], 0)
    mixed = depth_mix(extended, depth_all.astype(jnp.float32), height)
    row_sum, square_sum = sum_over_tp((jnp.sum(mixed, axis=1), jnp.sum(mixed * mixed, axis=1)))
    centre_mean = (row_sum / D)[:, None]
    inverse_conv = lax.rsqrt((square_sum / D)[:, None] - centre_mean * centre_mean + EPSILON)
    conv_normal = (mixed - centre_mean) * inverse_conv
    levels = conv_normal * scale_all.astype(jnp.float32) + shift_all.astype(jnp.float32)
    active = jax.nn.silu(levels).astype(jnp.bfloat16)
    result = stream + narrow(product_nt(active, out_all))
    return (
        result,
        (
            normal,
            inverse,
            hidden,
            halves,
            logistic,
            extended,
            conv_normal,
            inverse_conv,
            levels,
            active,
        ),
    )


def conv_backward(d_stream, gain, stored_conv, conv_set, setting):
    glu_all, depth_all, scale_all, shift_all, out_all = conv_set
    (
        normal,
        inverse,
        hidden,
        halves,
        logistic,
        extended,
        conv_normal,
        inverse_conv,
        levels,
        active,
    ) = stored_conv
    height = hidden.shape[0]
    d_branch = widen_grad(d_stream.astype(jnp.bfloat16))
    grad_out = product_tn(d_branch, active)
    d_levels = product(d_branch, out_all) * silu_slope(levels)
    grad_scale = jnp.sum(d_levels * conv_normal, axis=0)
    grad_shift = jnp.sum(d_levels, axis=0)
    scaled = d_levels * scale_all.astype(jnp.float32)
    plain_sum, cross_sum = sum_over_tp(
        (jnp.sum(scaled, axis=1), jnp.sum(scaled * conv_normal, axis=1))
    )
    d_mixed = inverse_conv * (
        scaled - (plain_sum / D)[:, None] - conv_normal * (cross_sum / D)[:, None]
    )
    kernel_taps = depth_all.astype(jnp.float32)
    tap_count = kernel_taps.shape[1]
    d_extended = jnp.zeros((height + tap_count - 1, d_mixed.shape[1]), jnp.float32)
    tap_grads = []
    for offset in range(tap_count):
        d_extended = d_extended + jnp.pad(
            d_mixed * kernel_taps[:, offset], ((offset, tap_count - 1 - offset), (0, 0))
        )
        tap_grads.append(jnp.sum(d_mixed * extended[offset : offset + height], axis=0))
    grad_depth = jnp.stack(tap_grads, axis=1)
    later = from_behind(d_extended[: KERNEL - 1], "ctx", -1)
    d_gated = d_extended[KERNEL - 1 :] + jnp.pad(later, ((height - (KERNEL - 1), 0), (0, 0)))
    d_gated = d_gated * setting["live_rows"]
    d_halves = jnp.stack(
        [d_gated * logistic, d_gated * halves[0] * logistic * (1.0 - logistic)], 0
    ).astype(jnp.bfloat16)
    grad_glu = jnp.einsum("fd,kfc->dkc", hidden, d_halves, preferred_element_type=jnp.float32)
    d_normed = narrow_grad(
        jnp.einsum("kfc,dkc->fd", d_halves, glu_all, preferred_element_type=jnp.float32)
    )
    d_input, d_gain, d_offset = norm_back(d_normed, normal, inverse, gain)
    return (
        d_stream + d_input,
        d_gain,
        d_offset,
        (grad_glu, grad_depth, grad_scale, grad_shift, grad_out),
    )


def run_forward(stream, weights, setting):
    (
        ffn1_in,
        ffn1_out,
        norm_gains,
        norm_biases,
        qkv_weight,
        attn_out,
        distance,
        glu_in,
        depthwise,
        conv_gain,
        conv_bias,
        conv_out,
        ffn2_in,
        ffn2_out,
    ) = weights
    stored = {}
    gains_all, biases_all, qkv_all, attn_all, table_all = gather_five(
        (norm_gains, norm_biases, qkv_weight, attn_out, distance)
    )
    gains_all = gains_all.astype(jnp.float32)
    biases_all = biases_all.astype(jnp.float32)
    first_in, first_out = gather_pair((ffn1_in, ffn1_out))
    stream, stored["ffn_one"] = ffn_forward(
        stream, gains_all[:, 0], biases_all[:, 0], first_in, first_out
    )
    stream, stored["attention"] = attn_forward(
        stream, gains_all[:, 1], biases_all[:, 1], qkv_all, attn_all, table_all, setting
    )
    conv_set = gather_five((glu_in, depthwise, conv_gain, conv_bias, conv_out))
    stream, stored["convolution"] = conv_forward(
        stream, gains_all[:, 2], biases_all[:, 2], conv_set, setting
    )
    second_in, second_out = gather_pair((ffn2_in, ffn2_out))
    stream, stored["ffn_two"] = ffn_forward(
        stream, gains_all[:, 3], biases_all[:, 3], second_in, second_out
    )
    result, final_normal, final_inverse = norm_rows(stream, gains_all[:, 4], biases_all[:, 4])
    stored["final_normal"] = final_normal
    stored["final_inverse"] = final_inverse
    stored["gains"] = gains_all
    stored["first_in"] = first_in
    stored["first_out"] = first_out
    stored["qkv_all"] = qkv_all
    stored["attn_all"] = attn_all
    stored["conv_set"] = conv_set
    stored["second_in"] = second_in
    stored["second_out"] = second_out
    return (result, stored)


def body(
    inputs,
    cotangent,
    lengths,
    buckets,
    ffn1_in,
    ffn1_out,
    norm_gains,
    norm_biases,
    qkv_weight,
    attn_out,
    distance,
    glu_in,
    depthwise,
    conv_gain,
    conv_bias,
    conv_out,
    ffn2_in,
    ffn2_out,
):
    stream = inputs[0].astype(jnp.float32)
    height = stream.shape[0] * lax.axis_size("tp")
    first_frame = lax.axis_index("ctx") * height
    length = lengths[0]
    frame_ids = first_frame + jnp.arange(height, dtype=jnp.int32)
    live_rows = (frame_ids < length).astype(jnp.float32)[:, None]
    ext_ids = jnp.arange(height + 2 * LEFT, dtype=jnp.int32)
    offsets = ext_ids[None, :] - jnp.arange(height, dtype=jnp.int32)[:, None]
    key_frames = (first_frame - LEFT + ext_ids)[None, :]
    in_band = (offsets >= 0) & (offsets < SPAN)
    allowed = in_band & (key_frames >= 0) & (key_frames < length)
    selector = (jnp.arange(SPAN, dtype=jnp.int32)[:, None] == buckets[None, :]).astype(jnp.bfloat16)
    setting = {
        "live_rows": live_rows,
        "in_band": in_band,
        "allowed": allowed,
        "selector": selector,
        "scaling": HD ** (-0.5),
    }
    weights = (
        ffn1_in,
        ffn1_out,
        norm_gains,
        norm_biases,
        qkv_weight,
        attn_out,
        distance,
        glu_in,
        depthwise,
        conv_gain,
        conv_bias,
        conv_out,
        ffn2_in,
        ffn2_out,
    )
    result, stored = run_forward(stream, weights, setting)
    again_stream, again_weights, marker = lax.optimization_barrier((stream, weights, result))
    unused, stored = run_forward(again_stream, again_weights, setting)
    gains_all = stored["gains"]
    d_stream, gain_four, bias_four = norm_back(
        cotangent[0].astype(jnp.float32),
        stored["final_normal"],
        stored["final_inverse"],
        gains_all[:, 4],
    )
    d_stream, gain_three, bias_three, grad_in_two, grad_out_two = ffn_backward(
        d_stream, gains_all[:, 3], stored["ffn_two"], stored["second_in"], stored["second_out"]
    )
    ffn_two_grads = settle_pair((grad_in_two, grad_out_two))
    d_stream, gain_two, bias_two, conv_grads = conv_backward(
        d_stream, gains_all[:, 2], stored["convolution"], stored["conv_set"], setting
    )
    conv_settled = settle_five(conv_grads)
    d_stream, gain_one, bias_one, grad_qkv, grad_attn, grad_table = attn_backward(
        d_stream,
        gains_all[:, 1],
        stored["attention"],
        stored["qkv_all"],
        stored["attn_all"],
        setting,
    )
    d_stream, gain_zero, bias_zero, grad_in_one, grad_out_one = ffn_backward(
        d_stream, gains_all[:, 0], stored["ffn_one"], stored["first_in"], stored["first_out"]
    )
    ffn_one_grads = settle_pair((grad_in_one, grad_out_one))
    grad_gains = jnp.stack([gain_zero, gain_one, gain_two, gain_three, gain_four], axis=1)
    grad_biases = jnp.stack([bias_zero, bias_one, bias_two, bias_three, bias_four], axis=1)
    attn_settled = settle_five((grad_gains, grad_biases, grad_qkv, grad_attn, grad_table))
    norm_sums, table_sum = sum_over_tp(
        (jnp.stack([attn_settled[0], attn_settled[1]], 0), attn_settled[4])
    )
    return (
        result.astype(jnp.bfloat16)[None],
        d_stream[None],
        ffn_one_grads[0],
        ffn_one_grads[1],
        norm_sums[0],
        norm_sums[1],
        attn_settled[2],
        attn_settled[3],
        table_sum,
        conv_settled[0],
        conv_settled[1],
        conv_settled[2],
        conv_settled[3],
        conv_settled[4],
        ffn_two_grads[0],
        ffn_two_grads[1],
    )


def solution(mesh):
    placed = (
        P("shard", ("ctx", "tp"), None),
        P("shard", ("ctx", "tp"), None),
        P("shard"),
        P(),
        P(("shard", "ctx"), "tp"),
        P(("shard", "ctx"), "tp"),
        P(("shard", "ctx"), None),
        P(("shard", "ctx"), None),
        P(("shard", "ctx"), None, "tp"),
        P(("shard", "ctx"), "tp"),
        P(("shard", "ctx"), None),
        P(("shard", "ctx"), None, "tp"),
        P(("tp", "shard", "ctx"), None),
        P(("tp", "shard", "ctx")),
        P(("tp", "shard", "ctx")),
        P(("shard", "ctx"), "tp"),
        P(("shard", "ctx"), "tp"),
        P(("shard", "ctx"), "tp"),
    )
    return jax.shard_map(
        body,
        mesh=mesh,
        in_specs=placed,
        out_specs=(
            P("shard", ("ctx", "tp"), None),
            P("shard", ("ctx", "tp"), None),
            P(("shard", "ctx"), "tp"),
            P(("shard", "ctx"), "tp"),
            P(("shard", "ctx"), None),
            P(("shard", "ctx"), None),
            P(("shard", "ctx"), None, "tp"),
            P(("shard", "ctx"), "tp"),
            P(("shard", "ctx"), None),
            P(("shard", "ctx"), None, "tp"),
            P(("tp", "shard", "ctx"), None),
            P(("tp", "shard", "ctx")),
            P(("tp", "shard", "ctx")),
            P(("shard", "ctx"), "tp"),
            P(("shard", "ctx"), "tp"),
            P(("shard", "ctx"), "tp"),
        ),
        check_vma=False,
    )
```

profile of v0, /device:TPU:0, one launch (start us, length us, event | category | flops | bytes accessed | tf_op | source)
XLA Modules:
  0.0 1528.9 jit_solution(3814069171340883858)
XLA Ops:
  45.1 19.4 %all_gather.122 = bf16[384,1024]{1,0:T(8,128)(2,1)S(1)} all-gather(bf16[96,1024]{1,0:T(8,128)(2,1)S(1)} %add_convert_fusion.7), channel_id=1, replica_groups=mesh['shard'=4,'ctx'=2,'tp'=4] {'tp'}, dimensions={0}, use_global_device_ids=true | all-gather | bytes 983040 | tf_op jit(solution)/shard_map/all_gather | solution.py:121
  92.9 19.1 %all_gather.128 = bf16[1024,256]{1,0:T(8,128)(2,1)} all-gather(bf16[128,256]{1,0:T(8,128)(2,1)S(1)} %copy-done.53), channel_id=1, replica_groups=mesh['shard'=4,'ctx'=2,'tp'=4] {'shard','ctx'}, dimensions={0}, use_global_device_ids=true | all-gather | bytes 589824 | tf_op jit(solution)/shard_map/all_gather | solution.py:98
  115.6 19.9 %all_gather.125 = bf16[384,1024]{1,0:T(8,128)(2,1)S(1)} all-gather(bf16[96,1024]{1,0:T(8,128)(2,1)S(1)} %add_convert_fusion.6), channel_id=1, replica_groups=mesh['shard'=4,'ctx'=2,'tp'=4] {'tp'}, dimensions={0}, use_global_device_ids=true | all-gather | bytes 983040 | tf_op jit(solution)/shard_map/all_gather | solution.py:121
  267.6 19.0 %reduce-scatter.30.cloned.1.call-done = bf16[96,1024]{1,0:T(8,128)(2,1)} async-done(((bf16[384,1024]{1,0:T(8,128)(2,1)}), bf16[96,1024]{1,0:T(8,128)(2,1)}) %reduce-scatter.30.cloned.1.call-update) | async-done | bytes 196624 | tf_op jit(solution)/shard_map/reduce_scatter | solution.py:125
  288.1 18.0 %all_gather.135 = bf16[384,1024]{1,0:T(8,128)(2,1)S(1)} all-gather(bf16[96,1024]{1,0:T(8,128)(2,1)S(1)} %add_convert_fusion.4), channel_id=1, replica_groups=mesh['shard'=4,'ctx'=2,'tp'=4] {'tp'}, dimensions={0}, use_global_device_ids=true | all-gather | bytes 983040 | tf_op jit(solution)/shard_map/all_gather | solution.py:121
  315.7 29.8 %all-gather.23.cloned.1.call-done = bf16[1024,1024]{1,0:T(8,128)(2,1)} async-done(((bf16[128,1024]{1,0:T(8,128)(2,1)}), bf16[1024,1024]{1,0:T(8,128)(2,1)}) %all-gather.23.cloned.1.call-update) | async-done | bytes 2097168 | tf_op jit(solution)/shard_map/all_gather | solution.py:89
  350.6 23.4 %reduce-scatter.32.cloned.1.call-done = bf16[96,1024]{1,0:T(8,128)(2,1)} async-done(((bf16[384,1024]{1,0:T(8,128)(2,1)}), bf16[96,1024]{1,0:T(8,128)(2,1)}) %reduce-scatter.32.cloned.1.call-update) | async-done | bytes 196624 | tf_op jit(solution)/shard_map/reduce_scatter | solution.py:125
  411.6 18.1 %all_gather.140 = bf16[384,1024]{1,0:T(8,128)(2,1)S(1)} all-gather(bf16[96,1024]{1,0:T(8,128)(2,1)S(1)} %add_convert_fusion.3), channel_id=1, replica_groups=mesh['shard'=4,'ctx'=2,'tp'=4] {'tp'}, dimensions={0}, use_global_device_ids=true | all-gather | bytes 983040 | tf_op jit(solution)/shard_map/all_gather | solution.py:121
  463.5 18.0 %all_gather.143 = bf16[384,1024]{1,0:T(8,128)(2,1)S(1)} all-gather(bf16[96,1024]{1,0:T(8,128)(2,1)S(1)} %add_convert_fusion.2), channel_id=1, replica_groups=mesh['shard'=4,'ctx'=2,'tp'=4] {'tp'}, dimensions={0}, use_global_device_ids=true | all-gather | bytes 983040 | tf_op jit(solution)/shard_map/all_gather | solution.py:121
  495.8 20.3 %all_gather.146 = bf16[1024,256]{1,0:T(8,128)(2,1)} all-gather(bf16[128,256]{1,0:T(8,128)(2,1)S(1)} %copy-done.54), channel_id=1, replica_groups=mesh['shard'=4,'ctx'=2,'tp'=4] {'shard','ctx'}, dimensions={0}, use_global_device_ids=true | all-gather | bytes 589824 | tf_op jit(solution)/shard_map/all_gather | solution.py:98
  519.3 18.7 %while.50 = (s32[]{:T(128)}, bf16[4,384,64]{1,2,0:T(8,128)(2,1)S(1)}, f32[4,384,1]{1,2,0:T(1,128)}, f32[4,384,1]{1,2,0:T(1,128)}, bf16[4,384,64]{2,1,0:T(8,128)(...) while((s32[]{:T(128)}, ...), condition=%wide.region_30.31_spmd.clone, body=%wide.region_27.30_spmd.clone.sunk | while | flops 58834176 | bytes 9471113 | solution.py:229
  565.6 18.0 %all_gather.148 = bf16[384,1024]{1,0:T(8,128)(2,1)S(1)} all-gather(bf16[96,1024]{1,0:T(8,128)(2,1)S(1)} %add_convert_fusion.1), channel_id=1, replica_groups=mesh['shard'=4,'ctx'=2,'tp'=4] {'tp'}, dimensions={0}, use_global_device_ids=true | all-gather | bytes 983040 | tf_op jit(solution)/shard_map/all_gather | solution.py:121
  642.1 19.2 %reduce-scatter.38.cloned.1.call-done = bf16[96,1024]{1,0:T(8,128)(2,1)} async-done(((bf16[384,1024]{1,0:T(8,128)(2,1)}), bf16[96,1024]{1,0:T(8,128)(2,1)}) %reduce-scatter.38.cloned.1.call-update) | async-done | bytes 196624 | tf_op jit(solution)/shard_map/reduce_scatter | solution.py:125
  662.7 18.2 %all_gather.153 = bf16[384,1024]{1,0:T(8,128)(2,1)S(1)} all-gather(bf16[96,1024]{1,0:T(8,128)(2,1)S(1)} %add_convert_fusion), channel_id=1, replica_groups=mesh['shard'=4,'ctx'=2,'tp'=4] {'tp'}, dimensions={0}, use_global_device_ids=true | all-gather | bytes 983040 | tf_op jit(solution)/shard_map/all_gather | solution.py:121
  694.0 26.0 %all-gather.35.cloned.1.call-done = bf16[1024,1024]{1,0:T(8,128)(2,1)} async-done(((bf16[128,1024]{1,0:T(8,128)(2,1)}), bf16[1024,1024]{1,0:T(8,128)(2,1)}) %all-gather.35.cloned.1.call-update) | async-done | bytes 2097168 | tf_op jit(solution)/shard_map/all_gather | solution.py:89
  724.1 23.4 %reduce-scatter.40.cloned.1.call-done = bf16[96,1024]{1,0:T(8,128)(2,1)} async-done(((bf16[384,1024]{1,0:T(8,128)(2,1)}), bf16[96,1024]{1,0:T(8,128)(2,1)}) %reduce-scatter.40.cloned.1.call-update) | async-done | bytes 196624 | tf_op jit(solution)/shard_map/reduce_scatter | solution.py:125
  775.0 22.7 %reduce-scatter.42.cloned.1.call-done = bf16[96,1024]{1,0:T(8,128)(2,1)} async-done(((bf16[384,1024]{1,0:T(8,128)(2,1)}), bf16[96,1024]{1,0:T(8,128)(2,1)}) %reduce-scatter.42.cloned.1.call-update) | async-done | bytes 196624 | tf_op jit(solution)/shard_map/reduce_scatter | solution.py:135
  844.0 20.6 %reduce-scatter.44.cloned.1.call-done = bf16[96,1024]{1,0:T(8,128)(2,1)} async-done(((bf16[384,1024]{1,0:T(8,128)(2,1)}), bf16[96,1024]{1,0:T(8,128)(2,1)}) %reduce-scatter.44.cloned.1.call-update) | async-done | bytes 196624 | tf_op jit(solution)/shard_map/reduce_scatter | solution.py:135
  868.2 18.2 %all_gather.158 = bf16[384,1024]{1,0:T(8,128)(2,1)S(1)} all-gather(bf16[96,1024]{1,0:T(8,128)(2,1)S(1)} %get-tuple-element.852), channel_id=1, replica_groups=mesh['shard'=4,'ctx'=2,'tp'=4] {'tp'}, dimensions={0}, use_global_device_ids=true | all-gather | bytes 983040 | tf_op jit(solution)/shard_map/all_gather | solution.py:131
  889.4 43.7 %while.51 = (s32[]{:T(128)}, bf16[4,384,64]{1,2,0:T(8,128)(2,1)}, f32[4,512,64]{1,2,0:T(8,128)}, f32[4,512,64]{1,2,0:T(8,128)}, f32[4,64,73]{2,1,0:T(8,128)}, /*...) while((s32[]{:T(128)}, bf16[4,384,64]{1,2,0:T(8,128)(2,1)}, ...), condition=%wide.region_58.59_spmd.clone, body=%wide.region_56.58_spmd.clone.sunk | while | flops 141594816 | bytes 19051732 | solution.py:276
  948.5 21.8 %reduce-scatter.46.cloned.1.call-done = bf16[96,1024]{1,0:T(8,128)(2,1)} async-done(((bf16[384,1024]{1,0:T(8,128)(2,1)}), bf16[96,1024]{1,0:T(8,128)(2,1)}) %reduce-scatter.46.cloned.1.call-update) | async-done | bytes 196624 | tf_op jit(solution)/shard_map/reduce_scatter | solution.py:135
  1001.8 18.8 %reduce-scatter.48.cloned.1.call-done = bf16[96,1024]{1,0:T(8,128)(2,1)} async-done(((bf16[384,1024]{1,0:T(8,128)(2,1)}), bf16[96,1024]{1,0:T(8,128)(2,1)}) %reduce-scatter.48.cloned.1.call-update) | async-done | bytes 196624 | tf_op jit(solution)/shard_map/reduce_scatter | solution.py:135
  1055.3 24.8 %all-reduce.45 = (f32[64,73]{1,0:T(8,128)S(1)}, f32[256]{0:T(256)S(1)}, f32[256]{0:T(256)S(1)}) all-reduce(f32[64,73]{1,0:T(8,128)S(1)} %fusion.302, f32[256]{0:T(256)S(1)} %copy-done.98, f32[256]{0:T(256)S(1)} %copy-done.99), channel_id=20, replica_groups=mesh['shard'=4,'ctx'=2,'tp'=4] {'shard','ctx'}, use_global_device_ids=true, to_apply=%region_83.84.clone | all-reduce | flops 5184 | bytes 41472
  1099.1 34.2 %reduce-scatter.56.cloned.1.call-done = f32[128,5]{0,1:T(8,128)} async-done(((f32[1024,5]{0,1:T(8,128)}), f32[128,5]{0,1:T(8,128)}) %reduce-scatter.56.cloned.1.call-update) | async-done | bytes 2576 | tf_op jit(solution)/shard_map/reduce_scatter | solution.py:113
  1134.0 19.2 %all-reduce.46 = (f32[2,128,5]{1,2,0:T(8,128)S(1)}, f32[8,73]{1,0:T(8,128)}) all-reduce(f32[2,128,5]{1,2,0:T(8,128)S(1)} %pad_maximum_fusion.9, f32[8,73]{1,0:T(8,128)S(1)} %constant_dynamic-slice_fusion.2), channel_id=1, replica_groups=mesh['shard'=4,'ctx'=2,'tp'=4] {'tp'}, use_global_device_ids=true, to_apply=%region_79.80 | all-reduce | flops 1864 | bytes 14912 | tf_op jit(solution)/shard_map/psum | solution.py:141
  1170.5 39.8 %reduce-scatter.64.cloned.1.call-done = f32[128,256]{1,0:T(8,128)} async-done(((f32[1024,256]{1,0:T(8,128)}), f32[128,256]{1,0:T(8,128)}) %reduce-scatter.64.cloned.1.call-update) | async-done | bytes 131088 | tf_op jit(solution)/shard_map/reduce_scatter | solution.py:116
  1210.3 39.7 %reduce-scatter.60.cloned.1.call-done = f32[128,256]{1,0:T(8,128)} async-done(((f32[1024,256]{1,0:T(8,128)}), f32[128,256]{1,0:T(8,128)}) %reduce-scatter.60.cloned.1.call-update) | async-done | bytes 131088 | tf_op jit(solution)/shard_map/reduce_scatter | solution.py:115
  1250.0 55.3 %reduce-scatter.68.cloned.1.call-done = f32[128,1024]{1,0:T(8,128)} async-done(((f32[1024,1024]{1,0:T(8,128)}), f32[128,1024]{1,0:T(8,128)}) %reduce-scatter.68.cloned.1.call-update) | async-done | bytes 524304 | tf_op jit(solution)/shard_map/reduce_scatter | solution.py:106
  1305.3 55.7 %reduce-scatter.66.cloned.1.call-done = f32[128,1024]{1,0:T(8,128)} async-done(((f32[1024,1024]{1,0:T(8,128)}), f32[128,1024]{1,0:T(8,128)}) %reduce-scatter.66.cloned.1.call-update) | async-done | bytes 524304 | tf_op jit(solution)/shard_map/reduce_scatter | solution.py:105
  1360.9 50.1 %reduce-scatter.58.cloned.1.call-done = f32[128,3,256]{2,0,1:T(8,128)} async-done(((f32[1024,3,256]{2,0,1:T(8,128)}), f32[128,3,256]{2,0,1:T(8,128)}) %reduce-scatter.58.cloned.1.call-update) | async-done | bytes 393232 | tf_op jit(solution)/shard_map/reduce_scatter | solution.py:114
  1411.0 55.6 %reduce-scatter.52.cloned.1.call-done = f32[128,1024]{1,0:T(8,128)} async-done(((f32[1024,1024]{1,0:T(8,128)}), f32[128,1024]{1,0:T(8,128)}) %reduce-scatter.52.cloned.1.call-update) | async-done | bytes 524304 | tf_op jit(solution)/shard_map/reduce_scatter | solution.py:106
  1466.7 55.3 %reduce-scatter.50.cloned.1.call-done = f32[128,1024]{1,0:T(8,128)} async-done(((f32[1024,1024]{1,0:T(8,128)}), f32[128,1024]{1,0:T(8,128)}) %reduce-scatter.50.cloned.1.call-update) | async-done | bytes 524304 | tf_op jit(solution)/shard_map/reduce_scatter | solution.py:105
  (751 shorter events, 683.2 us)
Async XLA Ops:
  7.2 57.3 %all-gather.13.cloned.1.call-start = ((), (), s32[]{:S(2)}) async-start(), calls=%async_computation.23 | async-start | bytes 2359296 | tf_op jit(solution)/shard_map/all_gather | solution.py:88
  7.9 62.5 %all-gather.15.cloned.1.call-start = ((), (), s32[]{:S(2)}) async-start(), calls=%async_computation.24 | async-start | bytes 2359296 | tf_op jit(solution)/shard_map/all_gather | solution.py:89
  8.7 103.6 %reduce-scatter.26.cloned.1.call-start = ((), (), s32[]{:S(2)}) async-start(), calls=%async_computation.25 | async-start | bytes 983040 | tf_op jit(solution)/shard_map/reduce_scatter | solution.py:125
  75.4 60.1 %all-gather.17.cloned.1.call-start = ((), (), s32[]{:S(2)}) async-start(), calls=%async_computation.26 | async-start | bytes 1769472 | tf_op jit(solution)/shard_map/all_gather | solution.py:97
  76.0 113.0 %reduce-scatter.28.cloned.1.call-start = ((), (), s32[]{:S(2)}) async-start(), calls=%async_computation.27 | async-start | bytes 983040 | tf_op jit(solution)/shard_map/reduce_scatter | solution.py:125
  168.1 118.5 %reduce-scatter.30.cloned.1.call-start = ((), (), s32[]{:S(2)}) async-start(), calls=%async_computation.29 | async-start | bytes 983040 | tf_op jit(solution)/shard_map/reduce_scatter | solution.py:125
  266.0 49.7 %all-gather.21.cloned.1.call-start = ((), (), s32[]{:S(2)}) async-start(), calls=%async_computation.30 | async-start | bytes 2359296 | tf_op jit(solution)/shard_map/all_gather | solution.py:88
  266.8 78.7 %all-gather.23.cloned.1.call-start = ((), (), s32[]{:S(2)}) async-start(), calls=%async_computation.31 | async-start | bytes 2359296 | tf_op jit(solution)/shard_map/all_gather | solution.py:89
  267.5 106.5 %reduce-scatter.32.cloned.1.call-start = ((), (), s32[]{:S(2)}) async-start(), calls=%async_computation.32 | async-start | bytes 983040 | tf_op jit(solution)/shard_map/reduce_scatter | solution.py:125
  350.5 79.1 %all-gather.25.cloned.1.call-start = ((), (), s32[]{:S(2)}) async-start(), calls=%async_computation.33 | async-start | bytes 2359296 | tf_op jit(solution)/shard_map/all_gather | solution.py:88
  378.1 57.0 %all-gather.27.cloned.1.call-start = ((), (), s32[]{:S(2)}) async-start(), calls=%async_computation.34 | async-start | bytes 2359296 | tf_op jit(solution)/shard_map/all_gather | solution.py:89
  378.6 83.4 %reduce-scatter.34.cloned.1.call-start = ((), (), s32[]{:S(2)}) async-start(), calls=%async_computation.35 | async-start | bytes 983040 | tf_op jit(solution)/shard_map/reduce_scatter | solution.py:125
  438.6 50.2 %all-gather.29.cloned.1.call-start = ((), (), s32[]{:S(2)}) async-start(), calls=%async_computation.36 | async-start | bytes 1769472 | tf_op jit(solution)/shard_map/all_gather | solution.py:97
  439.1 125.0 %reduce-scatter.36.cloned.1.call-start = ((), (), s32[]{:S(2)}) async-start(), calls=%async_computation.37 | async-start | bytes 983040 | tf_op jit(solution)/shard_map/reduce_scatter | solution.py:125
  541.3 120.0 %reduce-scatter.38.cloned.1.call-start = ((), (), s32[]{:S(2)}) async-start(), calls=%async_computation.39 | async-start | bytes 983040 | tf_op jit(solution)/shard_map/reduce_scatter | solution.py:125
  641.3 78.7 %all-gather.35.cloned.1.call-start = ((), (), s32[]{:S(2)}) async-start(), calls=%async_computation.41 | async-start | bytes 2359296 | tf_op jit(solution)/shard_map/all_gather | solution.py:89
  642.0 105.5 %reduce-scatter.40.cloned.1.call-start = ((), (), s32[]{:S(2)}) async-start(), calls=%async_computation.42 | async-start | bytes 983040 | tf_op jit(solution)/shard_map/reduce_scatter | solution.py:125
  724.1 73.6 %reduce-scatter.42.cloned.1.call-start = ((), (), s32[]{:S(2)}) async-start(), calls=%async_computation.43 | async-start | bytes 983040 | tf_op jit(solution)/shard_map/reduce_scatter | solution.py:135
  774.9 89.7 %reduce-scatter.44.cloned.1.call-start = ((), (), s32[]{:S(2)}) async-start(), calls=%async_computation.44 | async-start | bytes 983040 | tf_op jit(solution)/shard_map/reduce_scatter | solution.py:135
  844.0 126.4 %reduce-scatter.46.cloned.1.call-start = ((), (), s32[]{:S(2)}) async-start(), calls=%async_computation.45 | async-start | bytes 983040 | tf_op jit(solution)/shard_map/reduce_scatter | solution.py:135
  948.5 72.1 %reduce-scatter.48.cloned.1.call-start = ((), (), s32[]{:S(2)}) async-start(), calls=%async_computation.46 | async-start | bytes 983040 | tf_op jit(solution)/shard_map/reduce_scatter | solution.py:135
  997.8 83.4 %reduce-scatter.62.cloned.1.call-start = ((), (), s32[]{:S(2)}) async-start(), calls=%async_computation.53 | async-start | bytes 2359296 | tf_op jit(solution)/shard_map/reduce_scatter | solution.py:112
  1000.1 99.0 %reduce-scatter.54.cloned.1.call-start = ((), (), s32[]{:S(2)}) async-start(), calls=%async_computation.49 | async-start | bytes 36864 | tf_op jit(solution)/shard_map/reduce_scatter | solution.py:112
  1022.4 110.8 %reduce-scatter.56.cloned.1.call-start = ((), (), s32[]{:S(2)}) async-start(), calls=%async_computation.50 | async-start | bytes 36864 | tf_op jit(solution)/shard_map/reduce_scatter | solution.py:113
  1023.5 147.0 %reduce-scatter.70.cloned.1.call-start = ((), (), s32[]{:S(2)}) async-start(), calls=%async_computation.57 | async-start | bytes 147456
  1024.9 185.4 %reduce-scatter.64.cloned.1.call-start = ((), (), s32[]{:S(2)}) async-start(), calls=%async_computation.54 | async-start | bytes 1179648 | tf_op jit(solution)/shard_map/reduce_scatter | solution.py:116
  1027.8 222.1 %reduce-scatter.60.cloned.1.call-start = ((), (), s32[]{:S(2)}) async-start(), calls=%async_computation.52 | async-start | bytes 1179648 | tf_op jit(solution)/shard_map/reduce_scatter | solution.py:115
  1029.7 275.6 %reduce-scatter.68.cloned.1.call-start = ((), (), s32[]{:S(2)}) async-start(), calls=%async_computation.56 | async-start | bytes 4718592 | tf_op jit(solution)/shard_map/reduce_scatter | solution.py:106
  1034.6 326.3 %reduce-scatter.66.cloned.1.call-start = ((), (), s32[]{:S(2)}) async-start(), calls=%async_computation.55 | async-start | bytes 4718592 | tf_op jit(solution)/shard_map/reduce_scatter | solution.py:105
  1039.3 371.7 %reduce-scatter.58.cloned.1.call-start = ((), (), s32[]{:S(2)}) async-start(), calls=%async_computation.51 | async-start | bytes 3538944 | tf_op jit(solution)/shard_map/reduce_scatter | solution.py:114
  1043.1 423.6 %reduce-scatter.52.cloned.1.call-start = ((), (), s32[]{:S(2)}) async-start(), calls=%async_computation.48 | async-start | bytes 4718592 | tf_op jit(solution)/shard_map/reduce_scatter | solution.py:106
  1049.0 472.9 %reduce-scatter.50.cloned.1.call-start = ((), (), s32[]{:S(2)}) async-start(), calls=%async_computation.47 | async-start | bytes 4718592 | tf_op jit(solution)/shard_map/reduce_scatter | solution.py:105
  (157 other events, 2810.0 us)
Sparse Core Ops, SparseCore 0:
  9.9 30.6 all-gather.12
  42.5 27.8 all-gather.14
  75.5 23.2 reduce-scatter.25
  100.6 25.6 all-gather.16
  167.4 21.5 reduce-scatter.27
  191.3 22.7 all-gather.18
  288.5 27.1 all-gather.20
  317.6 27.8 all-gather.22
  350.6 23.3 reduce-scatter.31
  378.2 27.1 all-gather.24
  407.1 27.8 all-gather.26
  438.7 23.3 reduce-scatter.33
  463.8 24.9 all-gather.28
  540.5 23.5 reduce-scatter.35
  566.4 22.8 all-gather.30
  663.0 27.1 all-gather.32
  692.1 27.8 all-gather.34
  724.2 23.2 reduce-scatter.39
  775.1 22.5 reduce-scatter.41
  948.6 21.6 reduce-scatter.45
  997.9 22.5 reduce-scatter.47
  1023.8 40.6 reduce-scatter.61
  1067.7 31.4 reduce-scatter.53
  1101.9 31.2 reduce-scatter.55
  1137.1 33.3 reduce-scatter.69
  1174.3 35.9 reduce-scatter.63
  1213.9 36.0 reduce-scatter.59
  1253.9 51.3 reduce-scatter.67
  1309.6 51.3 reduce-scatter.65
  1364.7 46.2 reduce-scatter.57
  1415.3 51.2 reduce-scatter.51
  1470.6 51.3 reduce-scatter.49
  (3 shorter events, 61.2 us)
where the time goes:
time: 1540 us; the launch traced here: 1530 us
  waiting for transfers between devices  721 us (47%)
  blocking collectives  525 us (34%)
  matrix products  127 us (8%)
  local copies, waits for them, and re-layouts  59.8 us (4%)
  other arithmetic  52.2 us (3%)
  starting transfers between devices  23.5 us (2%)
  between operations  19.1 us (1%)
    all_gather x8, blocking collectives, widen(): return lax.all_gather(stream_rows, 'tp', axis=0, tiled=True)  148 us
    reduce_scatter x2, waiting for transfers between devices, settle_pair(): lax.psum_scatter(couple[0], ('shard', 'ctx'), scatter_dimension=0, tiled=...  111 us
    reduce_scatter x2, waiting for transfers between devices, settle_pair(): lax.psum_scatter(couple[1], ('shard', 'ctx'), scatter_dimension=0, tiled=...  111 us
    reduce_scatter x8, waiting for transfers between devices, narrow(): lax.psum_scatter(partial_value.astype(jnp.bfloat16), 'tp', scatter_dimens...  98.5 us
    reduce_scatter x4, waiting for transfers between devices, narrow_grad(): lax.psum_scatter(partial_value.astype(jnp.bfloat16), 'tp', scatter_dimens...  83.9 us
    all_gather x4, blocking collectives, widen_grad(): return lax.all_gather(stream_rows, 'tp', axis=0, tiled=True)  72.2 us
    all_gather x4, blocking collectives, gather_five(): lax.all_gather(bundle[4], ('shard', 'ctx'), axis=0, tiled=True)  64.5 us
    all_gather x4, waiting for transfers between devices, gather_pair(): lax.all_gather(couple[1], ('shard', 'ctx'), axis=0, tiled=True)  64.2 us
  transfers between devices with their start and end apart: 44, of which 34 were waited for; matrix products, arithmetic and copies ran while one was open for 4% of the time, Pallas kernels for 0%

commit v1 on v0

--- a/solution.py
+++ b/solution.py
@@ -100,21 +100,37 @@
     )
 
 
+def settle_wide(value):
+    count = lax.axis_size("shard") * lax.axis_size("ctx")
+    pieces = value.astype(jnp.bfloat16).reshape((count, value.shape[0] // count) + value.shape[1:])
+    pieces = lax.all_to_all(pieces, ("shard", "ctx"), 0, 0)
+    return jnp.sum(pieces.astype(jnp.float32), axis=0)
+
+
+def settle_narrow(values):
+    count = lax.axis_size("shard") * lax.axis_size("ctx")
+    flat = jnp.concatenate([v.reshape(count, -1) for v in values], axis=1)
+    summed = jnp.sum(lax.all_to_all(flat, ("shard", "ctx"), 0, 0), axis=0)
+    out, start = [], 0
+    for v in values:
+        size = v.size // count
+        out.append(summed[start : start + size].reshape((v.shape[0] // count,) + v.shape[1:]))
+        start += size
+    return out
+
+
 def settle_pair(couple):
-    return (
-        lax.psum_scatter(couple[0], ("shard", "ctx"), scatter_dimension=0, tiled=True),
-        lax.psum_scatter(couple[1], ("shard", "ctx"), scatter_dimension=0, tiled=True),
-    )
-
-
-def settle_five(bundle):
-    return (
-        lax.psum_scatter(bundle[0], ("shard", "ctx"), scatter_dimension=0, tiled=True),
-        lax.psum_scatter(bundle[1], ("shard", "ctx"), scatter_dimension=0, tiled=True),
-        lax.psum_scatter(bundle[2], ("shard", "ctx"), scatter_dimension=0, tiled=True),
-        lax.psum_scatter(bundle[3], ("shard", "ctx"), scatter_dimension=0, tiled=True),
-        lax.psum_scatter(bundle[4], ("shard", "ctx"), scatter_dimension=0, tiled=True),
-    )
+    return (settle_wide(couple[0]), settle_wide(couple[1]))
+
+
+def settle_conv(bundle):
+    small = settle_narrow((bundle[1], bundle[2], bundle[3]))
+    return (settle_wide(bundle[0]), *small, settle_wide(bundle[4]))
+
+
+def settle_attn(bundle):
+    small = settle_narrow((bundle[0], bundle[1], bundle[4]))
+    return (small[0], small[1], settle_wide(bundle[2]), settle_wide(bundle[3]), small[2])
 
 
 def widen(stream_rows):
@@ -122,9 +138,11 @@
 
 
 def narrow(partial_value):
-    return lax.psum_scatter(
-        partial_value.astype(jnp.bfloat16), "tp", scatter_dimension=0, tiled=True
-    ).astype(jnp.float32)
+    count = lax.axis_size("tp")
+    pieces = partial_value.astype(jnp.bfloat16).reshape(
+        count, partial_value.shape[0] // count, partial_value.shape[1]
+    )
+    return jnp.sum(lax.all_to_all(pieces, "tp", 0, 0).astype(jnp.float32), axis=0)
 
 
 def widen_grad(stream_rows):
@@ -132,9 +150,11 @@
 
 
 def narrow_grad(partial_value):
-    return lax.psum_scatter(
-        partial_value.astype(jnp.bfloat16), "tp", scatter_dimension=0, tiled=True
-    ).astype(jnp.float32)
+    count = lax.axis_size("tp")
+    pieces = partial_value.astype(jnp.bfloat16).reshape(
+        count, partial_value.shape[0] // count, partial_value.shape[1]
+    )
+    return jnp.sum(lax.all_to_all(pieces, "tp", 0, 0).astype(jnp.float32), axis=0)
 
 
 def sum_over_tp(couple):
@@ -503,8 +523,6 @@
         ffn2_out,
     )
     result, stored = run_forward(stream, weights, setting)
-    again_stream, again_weights, marker = lax.optimization_barrier((stream, weights, result))
-    unused, stored = run_forward(again_stream, again_weights, setting)
     gains_all = stored["gains"]
     d_stream, gain_four, bias_four = norm_back(
         cotangent[0].astype(jnp.float32),
@@ -519,7 +537,7 @@
     d_stream, gain_two, bias_two, conv_grads = conv_backward(
         d_stream, gains_all[:, 2], stored["convolution"], stored["conv_set"], setting
     )
-    conv_settled = settle_five(conv_grads)
+    conv_settled = settle_conv(conv_grads)
     d_stream, gain_one, bias_one, grad_qkv, grad_attn, grad_table = attn_backward(
         d_stream,
         gains_all[:, 1],
@@ -534,7 +552,7 @@
     ffn_one_grads = settle_pair((grad_in_one, grad_out_one))
     grad_gains = jnp.stack([gain_zero, gain_one, gain_two, gain_three, gain_four], axis=1)
     grad_biases = jnp.stack([bias_zero, bias_one, bias_two, bias_three, bias_four], axis=1)
-    attn_settled = settle_five((grad_gains, grad_biases, grad_qkv, grad_attn, grad_table))
+    attn_settled = settle_attn((grad_gains, grad_biases, grad_qkv, grad_attn, grad_table))
     norm_sums, table_sum = sum_over_tp(
         (jnp.stack([attn_settled[0], attn_settled[1]], 0), attn_settled[4])
     )

time: 1540 us -> 781 us (0.51)
  waiting for transfers between devices: 721 us -> 106 us
  blocking collectives: 525 us -> 357 us
  starting transfers between devices: 23.5 us -> 73.3 us
  matrix products: 127 us -> 106 us
    reduce_scatter x22 -> x0, waiting for transfers between devices: 583 us -> none  [the longest x2 111 us: settle_pair(): lax.psum_scatter(couple[0], ('shard', 'ctx'), scatter_dimension=0, tiled=...]
    all_to_all x0 -> x15, waiting for transfers between devices: none -> 86 us  [the longest x8 51.3 us: settle_wide(): pieces = lax.all_to_all(pieces, ('shard', 'ctx'), 0, 0)]
    all_gather x8 -> x4, blocking collectives: 148 us -> 77.9 us  [widen(): return lax.all_gather(stream_rows, 'tp', axis=0, tiled=True)]
    all_gather x4 -> x2, waiting for transfers between devices: 64.2 us -> 0.05 us  [gather_pair(): lax.all_gather(couple[1], ('shard', 'ctx'), axis=0, tiled=True)]
    all_to_all x0 -> x3, blocking collectives: none -> 59.4 us  [the longest x2 40.3 us: narrow(): lax.all_to_all(pieces, 'tp', 0, 0).astype(jnp.float32)]
    all_to_all x0 -> x15, starting transfers between devices: none -> 58.1 us  [the longest x8 32.5 us: settle_wide(): pieces = lax.all_to_all(pieces, ('shard', 'ctx'), 0, 0)]
    unnamed x3 -> x1, blocking collectives: 52.1 us -> 13.8 us
    all_gather x4 -> x2, blocking collectives: 63.3 us -> 31.2 us  [gather_five(): lax.all_gather(bundle[1], ('shard', 'ctx'), axis=0, tiled=True)]
  transfers between devices with their start and end apart: 44 -> 27, of which waited for: 34 -> 14; matrix products, arithmetic and copies ran while one was open for 4% -> 24% of each run, Pallas kernels for 0% -> 0%
where the time goes in v1:
time: 781 us; the launch traced here: 769 us
  blocking collectives  357 us (46%)
  waiting for transfers between devices  106 us (14%)
  matrix products  106 us (14%)
  starting transfers between devices  73.3 us (9%)
  local copies, waits for them, and re-layouts  53.7 us (7%)
  other arithmetic  52.7 us (7%)
  between operations  18.8 us (2%)
    all_gather x4, blocking collectives, widen(): return lax.all_gather(stream_rows, 'tp', axis=0, tiled=True)  77.9 us
    all_gather x4, blocking collectives, widen_grad(): return lax.all_gather(stream_rows, 'tp', axis=0, tiled=True)  73.9 us
    all_to_all x8, waiting for transfers between devices, settle_wide(): pieces = lax.all_to_all(pieces, ('shard', 'ctx'), 0, 0)  51.3 us
    all_to_all x2, blocking collectives, narrow(): lax.all_to_all(pieces, 'tp', 0, 0).astype(jnp.float32)  40.3 us
    all_gather x2, blocking collectives, gather_five(): lax.all_gather(bundle[4], ('shard', 'ctx'), axis=0, tiled=True)  34.1 us
    all_to_all x8, starting transfers between devices, settle_wide(): pieces = lax.all_to_all(pieces, ('shard', 'ctx'), 0, 0)  32.5 us
    psum x3, blocking collectives, sum_over_tp(): return lax.psum((couple[0], couple[1]), 'tp')  32.4 us
    all_to_all x3, waiting for transfers between devices, narrow_grad(): lax.all_to_all(pieces, 'tp', 0, 0).astype(jnp.float32)  32.4 us
  transfers between devices with their start and end apart: 27, of which 14 were waited for; matrix products, arithmetic and copies ran while one was open for 24% of the time, Pallas kernels for 0%

profile of v1, /device:TPU:0, one launch (start us, length us, event | category | flops | bytes accessed | tf_op | source)
XLA Modules:
  0.0 769.2 jit_solution(9461144593929612758)
XLA Ops:
  13.3 17.3 %all_gather.66 = bf16[1024,5]{0,1:T(8,128)(2,1)S(1)} all-gather(bf16[128,5]{0,1:T(8,128)(2,1)} %param.28), channel_id=1, replica_groups=mesh['shard'=4,'ctx'=2,'tp'=4] {'shard','ctx'}, dimensions={0}, use_global_device_ids=true | all-gather | bytes 11520 | tf_op jit(solution)/shard_map/all_gather | solution.py:95
  30.7 15.6 %all_gather.67 = bf16[1024,5]{0,1:T(8,128)(2,1)S(1)} all-gather(bf16[128,5]{0,1:T(8,128)(2,1)S(1)} %copy-done.179), channel_id=1, replica_groups=mesh['shard'=4,'ctx'=2,'tp'=4] {'shard','ctx'}, dimensions={0}, use_global_device_ids=true | all-gather | bytes 11520 | tf_op jit(solution)/shard_map/all_gather | solution.py:96
  47.1 19.1 %all_gather.68 = bf16[384,1024]{1,0:T(8,128)(2,1)S(1)} all-gather(bf16[96,1024]{1,0:T(8,128)(2,1)S(1)} %fusion.102), channel_id=1, replica_groups=mesh['shard'=4,'ctx'=2,'tp'=4] {'tp'}, dimensions={0}, use_global_device_ids=true | all-gather | bytes 983040 | tf_op jit(solution)/shard_map/all_gather | solution.py:137
  74.4 4.7 all-to-all-start
  80.4 16.4 %all_gather.73 = bf16[64,73]{1,0:T(8,128)(2,1)S(1)} all-gather(bf16[8,73]{1,0:T(8,128)(2,1)S(1)} %copy-done.180), channel_id=1, replica_groups=mesh['shard'=4,'ctx'=2,'tp'=4] {'shard','ctx'}, dimensions={0}, use_global_device_ids=true | all-gather | bytes 10512 | tf_op jit(solution)/shard_map/all_gather | solution.py:99
  96.8 17.3 %all_gather.74 = bf16[1024,256]{1,0:T(8,128)(2,1)S(1)} all-gather(bf16[128,256]{1,0:T(8,128)(2,1)S(1)} %copy-done.60), channel_id=1, replica_groups=mesh['shard'=4,'ctx'=2,'tp'=4] {'shard','ctx'}, dimensions={0}, use_global_device_ids=true | all-gather | bytes 589824 | tf_op jit(solution)/shard_map/all_gather | solution.py:98
  116.3 19.7 %all_gather.71 = bf16[384,1024]{1,0:T(8,128)(2,1)S(1)} all-gather(bf16[96,1024]{1,0:T(8,128)(2,1)S(1)} %add_convert_fusion.3), channel_id=1, replica_groups=mesh['shard'=4,'ctx'=2,'tp'=4] {'tp'}, dimensions={0}, use_global_device_ids=true | all-gather | bytes 983040 | tf_op jit(solution)/shard_map/all_gather | solution.py:137
  144.8 6.8 collective-permute-done.1
  154.0 21.6 %while.36 = (s32[]{:T(128)}, bf16[4,384,64]{1,2,0:T(8,128)(2,1)S(1)}, f32[4,384,1]{1,2,0:T(1,128)}, f32[4,384,1]{1,2,0:T(1,128)}, bf16[4,384,64]{2,1,0:T(8,128)(...) while((s32[]{:T(128)}, ...), condition=%wide.region_8.9_spmd.clone, body=%wide.region_5.8_spmd.clone.sunk | while | flops 58834176 | bytes 9464073 | solution.py:249
  181.0 15.6 %all_gather.77 = bf16[256,31]{1,0:T(8,128)(2,1)S(1)} all-gather(bf16[32,31]{1,0:T(8,128)(2,1)S(1)} %copy-done.153), channel_id=1, replica_groups=mesh['shard'=4,'ctx'=2,'tp'=4] {'shard','ctx'}, dimensions={0}, use_global_device_ids=true | all-gather | bytes 17856 | tf_op jit(solution)/shard_map/all_gather | solution.py:96
  200.0 20.7 %all_gather.75 = bf16[384,1024]{1,0:T(8,128)(2,1)} all-gather(bf16[96,1024]{1,0:T(8,128)(2,1)S(1)} %add_convert_fusion.2), channel_id=1, replica_groups=mesh['shard'=4,'ctx'=2,'tp'=4] {'tp'}, dimensions={0}, use_global_device_ids=true | all-gather | bytes 983040 | tf_op jit(solution)/shard_map/all_gather | solution.py:137
  226.7 17.7 %all_gather.80 = bf16[1024,256]{1,0:T(8,128)(2,1)} all-gather(bf16[128,256]{1,0:T(8,128)(2,1)S(1)} %copy-done.61), channel_id=1, replica_groups=mesh['shard'=4,'ctx'=2,'tp'=4] {'shard','ctx'}, dimensions={0}, use_global_device_ids=true | all-gather | bytes 589824 | tf_op jit(solution)/shard_map/all_gather | solution.py:99
  246.1 13.8 %all-reduce.42 = (bf16[256]{0:T(256)(128)(2,1)S(1)}, bf16[256]{0:T(256)(128)(2,1)S(1)}) all-reduce(bf16[256]{0:T(256)(128)(2,1)S(1)} %dynamic-update-slice.1, bf16[256]{0:T(256)(128)(2,1)S(1)} %dynamic-update-slice), channel_id=1, replica_groups=mesh['shard'=4,'ctx'=2,'tp'=4] {'shard','ctx'}, use_global_device_ids=true, to_apply=%add.38 | all-reduce | flops 512 | bytes 2048
  263.3 10.9 %all-reduce.41 = (f32[384]{0:T(512)S(1)}, f32[384]{0:T(512)S(1)}) all-reduce(f32[384]{0:T(512)S(1)} %get-tuple-element.523, f32[384]{0:T(512)S(1)} %get-tuple-element.522), channel_id=1, replica_groups=mesh['shard'=4,'ctx'=2,'tp'=4] {'tp'}, use_global_device_ids=true, to_apply=%region_15.16 | all-reduce | flops 768 | bytes 6144 | tf_op jit(solution)/shard_map/psum | solution.py:161
  275.7 21.0 %all_to_all.98 = bf16[4,96,1024]{2,1,0:T(8,128)(2,1)S(1)} all-to-all(bf16[4,96,1024]{2,1,0:T(8,128)(2,1)S(1)} %bitcast.465), channel_id=1, replica_groups=mesh['shard'=4,'ctx'=2,'tp'=4] {'tp'}, dimensions={0} | all-to-all | bytes 1572864 | tf_op jit(solution)/shard_map/all_to_all | solution.py:145
  297.6 18.4 %all_gather.81 = bf16[384,1024]{1,0:T(8,128)(2,1)} all-gather(bf16[96,1024]{1,0:T(8,128)(2,1)S(1)} %add_convert_fusion.1), channel_id=1, replica_groups=mesh['shard'=4,'ctx'=2,'tp'=4] {'tp'}, dimensions={0}, use_global_device_ids=true | all-gather | bytes 983040 | tf_op jit(solution)/shard_map/all_gather | solution.py:137
  323.1 19.3 %all_to_all.99 = bf16[4,96,1024]{2,1,0:T(8,128)(2,1)S(1)} all-to-all(bf16[4,96,1024]{2,1,0:T(8,128)(2,1)S(1)} %bitcast.466), channel_id=1, replica_groups=mesh['shard'=4,'ctx'=2,'tp'=4] {'tp'}, dimensions={0} | all-to-all | bytes 1572864 | tf_op jit(solution)/shard_map/all_to_all | solution.py:145
  344.3 17.7 %all_gather.84 = bf16[384,1024]{1,0:T(8,128)(2,1)S(1)} all-gather(bf16[96,1024]{1,0:T(8,128)(2,1)S(1)} %multiply_convert_fusion.7), channel_id=1, replica_groups=mesh['shard'=4,'ctx'=2,'tp'=4] {'tp'}, dimensions={0}, use_global_device_ids=true | all-gather | bytes 983040 | tf_op jit(solution)/shard_map/all_gather | solution.py:149
  365.7 19.1 %all_to_all.100 = bf16[4,96,1024]{2,1,0:T(8,128)(2,1)S(1)} all-to-all(bf16[4,96,1024]{2,1,0:T(8,128)(2,1)S(1)} %bitcast.464), channel_id=1, replica_groups=mesh['shard'=4,'ctx'=2,'tp'=4] {'tp'}, dimensions={0} | all-to-all | bytes 1572864 | tf_op jit(solution)/shard_map/all_to_all | solution.py:157
  387.5 17.4 %all_gather.85 = bf16[384,1024]{1,0:T(8,128)(2,1)S(1)} all-gather(bf16[96,1024]{1,0:T(8,128)(2,1)S(1)} %get-tuple-element.615), channel_id=1, replica_groups=mesh['shard'=4,'ctx'=2,'tp'=4] {'tp'}, dimensions={0}, use_global_device_ids=true | all-gather | bytes 983040 | tf_op jit(solution)/shard_map/all_gather | solution.py:149
  406.8 10.8 %all-reduce.40 = (f32[384]{0:T(512)S(1)}, f32[384]{0:T(512)S(1)}) all-reduce(f32[384]{0:T(512)S(1)} %get-tuple-element.466, f32[384]{0:T(512)S(1)} %get-tuple-element.520), channel_id=1, replica_groups=mesh['shard'=4,'ctx'=2,'tp'=4] {'tp'}, use_global_device_ids=true, to_apply=%region_30.31 | all-reduce | flops 768 | bytes 6144 | tf_op jit(solution)/shard_map/psum | solution.py:161
  459.3 20.2 %all_gather.86 = bf16[384,1024]{1,0:T(8,128)(2,1)S(1)} all-gather(bf16[96,1024]{1,0:T(8,128)(2,1)} %get-tuple-element.613), channel_id=1, replica_groups=mesh['shard'=4,'ctx'=2,'tp'=4] {'tp'}, dimensions={0}, use_global_device_ids=true | all-gather | bytes 983040 | tf_op jit(solution)/shard_map/all_gather | solution.py:149
  481.7 4.5 all-to-all-start.17
  487.0 49.3 %while.37 = (s32[]{:T(128)}, bf16[4,384,64]{1,2,0:T(8,128)(2,1)}, f32[4,512,64]{1,2,0:T(8,128)}, f32[4,512,64]{1,2,0:T(8,128)}, f32[4,64,73]{2,1,0:T(8,128)}, /*...) while((s32[]{:T(128)}, bf16[4,384,64]{1,2,0:T(8,128)(2,1)}, ...), condition=%wide.region_36.37_spmd.clone, body=%wide.region_34.36_spmd.clone.sunk | while | flops 141594816 | bytes 18964864 | solution.py:296
  560.0 15.7 %all-to-all-done.6 = bf16[4,96,1024]{2,1,0:T(8,128)(2,1)S(1)} async-done(((bf16[4,96,1024]{2,1,0:T(8,128)(2,1)}), bf16[4,96,1024]{2,1,0:T(8,128)(2,1)S(1)}, u32[]{:S(2)}, u32[]{:S(2)}) %all-to-all-start.6) | async-done | bytes 786464 | tf_op jit(solution)/shard_map/all_to_all | solution.py:157
  586.3 20.0 %all-to-all-done.16 = bf16[8,128,1024]{2,1,0:T(8,128)(2,1)S(1)} async-done(((bf16[8,128,1024]{2,1,0:T(8,128)(2,1)}), bf16[8,128,1024]{2,1,0:T(8,128)(2,1)S(1)}, u32[]{:S(2)}, u32[]{:S(2)}) %all-to-all-start.16) | async-done | bytes 2097184 | tf_op jit(solution)/shard_map/all_to_all | solution.py:106
  610.8 18.6 %all_gather.87 = bf16[384,1024]{1,0:T(8,128)(2,1)} all-gather(bf16[96,1024]{1,0:T(8,128)(2,1)S(1)} %multiply_convert_fusion.4), channel_id=1, replica_groups=mesh['shard'=4,'ctx'=2,'tp'=4] {'tp'}, dimensions={0}, use_global_device_ids=true | all-gather | bytes 983040 | tf_op jit(solution)/shard_map/all_gather | solution.py:149
  650.6 16.6 %all-to-all-done.7 = bf16[4,96,1024]{2,1,0:T(8,128)(2,1)S(1)} async-done(((bf16[4,96,1024]{2,1,0:T(8,128)(2,1)}), bf16[4,96,1024]{2,1,0:T(8,128)(2,1)S(1)}, u32[]{:S(2)}, u32[]{:S(2)}) %all-to-all-start.7) | async-done | bytes 786464 | tf_op jit(solution)/shard_map/all_to_all | solution.py:157
  667.2 4.5 all-to-all-start.11
  677.7 14.6 %all-to-all-done.11 = bf16[8,128,3,256]{3,1,2,0:T(8,128)(2,1)} async-done(((bf16[8,128,3,256]{3,1,2,0:T(8,128)(2,1)}), bf16[8,128,3,256]{3,1,2,0:T(8,128)(2,1)}, u32[]{:S(2)}, u32[]{:S(2)}) %all-to-all-start.11) | async-done | bytes 1572896 | tf_op jit(solution)/shard_map/all_to_all | solution.py:106
  721.5 9.6 %all-to-all-done.9 = bf16[8,128,1024]{2,1,0:T(8,128)(2,1)} async-done(((bf16[8,128,1024]{2,1,0:T(8,128)(2,1)}), bf16[8,128,1024]{2,1,0:T(8,128)(2,1)}, u32[]{:S(2)}, u32[]{:S(2)}) %all-to-all-start.9) | async-done | bytes 2097184 | tf_op jit(solution)/shard_map/all_to_all | solution.py:106
  741.8 10.7 %all-reduce.39 = (f32[2,128,5]{1,0,2:T(2,128)S(1)}, f32[8,73]{1,0:T(8,128)}) all-reduce(f32[2,128,5]{1,0,2:T(2,128)S(1)} %pad_maximum_fusion.7, f32[8,73]{1,0:T(8,128)S(1)} %reshape.792), channel_id=1, replica_groups=mesh['shard'=4,'ctx'=2,'tp'=4] {'tp'}, use_global_device_ids=true, to_apply=%region_57.58 | all-reduce | flops 1864 | bytes 14912 | tf_op jit(solution)/shard_map/psum | solution.py:161
  (793 shorter events, 295.1 us)
Async XLA Ops:
  7.2 59.0 %all-gather.7.cloned.1.call-start = ((), (), s32[]{:S(2)}) async-start(), calls=%async_computation.18 | async-start | bytes 2359296 | tf_op jit(solution)/shard_map/all_gather | solution.py:88
  7.9 62.5 %all-gather.9.cloned.1.call-start = ((), (), s32[]{:S(2)}) async-start(), calls=%async_computation.19 | async-start | bytes 2359296 | tf_op jit(solution)/shard_map/all_gather | solution.py:89
  8.7 127.3 %all-gather.11.cloned.1.call-start = ((), (), s32[]{:S(2)}) async-start(), calls=%async_computation.20 | async-start | bytes 1769472 | tf_op jit(solution)/shard_map/all_gather | solution.py:97
  9.4 211.4 %all-gather.13.cloned.1.call-start = ((), (), s32[]{:S(2)}) async-start(), calls=%async_computation.21 | async-start | bytes 1179648 | tf_op jit(solution)/shard_map/all_gather | solution.py:95
  30.7 85.5 %copy-start.56 = (f32[1024,1]{0,1:T(1,128)}, f32[1024,1]{0,1:T(1,128)S(1)}, u32[]{:S(2)}) copy-start(f32[1024,1]{0,1:T(1,128)S(1)} %get-tuple-element.678) | copy-start | bytes 12292
  74.4 40.5 %all-to-all-start = ((bf16[4,96,1024]{2,1,0:T(8,128)(2,1)}), bf16[4,96,1024]{2,1,0:T(8,128)(2,1)S(1)}, u32[]{:S(2)}, u32[]{:S(2)}) async-start(bf16[4,96,1024]{2,1,0:T(8,128)(2,1)} %bitcast.3), calls=%async_computation | async-start | bytes 1572864 | tf_op jit(solution)/shard_map/all_to_all | solution.py:145
  79.1 236.9 %all-gather.15.cloned.1.call-start = ((), (), s32[]{:S(2)}) async-start(), calls=%async_computation.22 | async-start | bytes 2359296 | tf_op jit(solution)/shard_map/all_gather | solution.py:88
  138.5 6.1 collective-permute-start
  142.1 9.5 %collective-permute-start.1 = (bf16[64,512]{0,1:T(8,128)(2,1)S(1)}, bf16[64,512]{0,1:T(8,128)(2,1)S(1)}, u32[]{:S(2)}, u32[]{:S(2)}) collective-permute-start(bf16[64,512]{0,1:T(8,128)(2,1)S(1)} %bitcast.477), channel_id=1, source_target_pairs={{4,0},{5,1},{6,2},{7,3},{12,8},{13,9},{14,10},{15,11},{20,16},{21,... | collective-permute-start | bytes 196616 | tf_op jit(solution)/shard_map/ppermute | solution.py:25
  176.9 22.4 %all-to-all-start.1 = ((bf16[4,96,1024]{2,1,0:T(8,128)(2,1)}), bf16[4,96,1024]{2,1,0:T(8,128)(2,1)S(1)}, u32[]{:S(2)}, u32[]{:S(2)}) async-start(bf16[4,96,1024]{2,1,0:T(8,128)(2,1)} %bitcast.20), calls=%async_computation.1 | async-start | bytes 1572864 | tf_op jit(solution)/shard_map/all_to_all | solution.py:145
  180.4 139.7 %all-gather.17.cloned.1.call-start = ((), (), s32[]{:S(2)}) async-start(), calls=%async_computation.23 | async-start | bytes 2359296 | tf_op jit(solution)/shard_map/all_gather | solution.py:89
  197.5 63.5 %copy-start.129 = (f32[256]{0:T(256)}, f32[256]{0:T(256)S(1)}, u32[]{:S(2)}) copy-start(f32[256]{0:T(256)S(1)} %get-tuple-element.544) | copy-start | bytes 3076
  197.5 63.5 %copy-start.130 = (f32[256]{0:T(256)}, f32[256]{0:T(256)S(1)}, u32[]{:S(2)}) copy-start(f32[256]{0:T(256)S(1)} %get-tuple-element.545) | copy-start | bytes 3076
  197.5 63.5 %copy-start.131 = (f32[256]{0:T(256)}, f32[256]{0:T(256)S(1)}, u32[]{:S(2)}) copy-start(f32[256]{0:T(256)S(1)} %get-tuple-element.546) | copy-start | bytes 3076
  197.6 63.5 %copy-start.132 = (f32[256]{0:T(256)}, f32[256]{0:T(256)S(1)}, u32[]{:S(2)}) copy-start(f32[256]{0:T(256)S(1)} %get-tuple-element.547) | copy-start | bytes 3076
  223.0 38.0 %collective-permute-start.2 = (bf16[30,256]{1,0:T(8,128)(2,1)S(1)}, bf16[30,256]{1,0:T(8,128)(2,1)S(1)}, u32[]{:S(2)}, u32[]{:S(2)}) collective-permute-start(bf16[30,256]{1,0:T(8,128)(2,1)S(1)} %slice.499), channel_id=1, source_target_pairs={{0,4},{1,5},{2,6},{3,7},{8,12},{9,13},{10,14},{11,15},{16,20},{17,... | collective-permute-start | bytes 46088 | tf_op jit(solution)/shard_map/ppermute | solution.py:33
  423.4 5.8 collective-permute-start.3
  431.0 16.6 %all-to-all-start.5 = ((bf16[4,96,1024]{2,1,0:T(8,128)(2,1)}), bf16[4,96,1024]{2,1,0:T(8,128)(2,1)S(1)}, u32[]{:S(2)}, u32[]{:S(2)}) async-start(bf16[4,96,1024]{2,1,0:T(8,128)(2,1)} %bitcast.43), calls=%async_computation.5 | async-start | bytes 1572864 | tf_op jit(solution)/shard_map/all_to_all | solution.py:157
  447.6 8.2 %all-to-all-start.14 = ((f32[8,1,1056]{2,1,0:T(1,128)}), f32[8,1,1056]{2,1,0:T(1,128)S(1)}, u32[]{:S(2)}, u32[]{:S(2)}) async-start(f32[8,1,1056]{2,1,0:T(1,128)} %copy.87), calls=%async_computation.14 | async-start | bytes 73728 | tf_op jit(solution)/shard_map/all_to_all | solution.py:113
  455.8 25.1 %all-to-all-start.15 = ((bf16[8,128,256]{2,1,0:T(8,128)(2,1)}), bf16[8,128,256]{2,1,0:T(8,128)(2,1)S(1)}, u32[]{:S(2)}, u32[]{:S(2)}) async-start(bf16[8,128,256]{2,1,0:T(8,128)(2,1)} %bitcast.111), calls=%async_computation.15 | async-start | bytes 1048576 | tf_op jit(solution)/shard_map/all_to_all | solution.py:106
  481.7 70.8 %all-to-all-start.17 = ((bf16[8,128,1024]{2,1,0:T(8,128)(2,1)}), bf16[8,128,1024]{2,1,0:T(8,128)(2,1)}, u32[]{:S(2)}, u32[]{:S(2)}) async-start(bf16[8,128,1024]{2,1,0:T(8,128)(2,1)} %bitcast.447), calls=%async_computation.17 | async-start | bytes 4194304 | tf_op jit(solution)/shard_map/all_to_all | solution.py:106
  537.6 7.0 collective-permute-start.4
  541.6 7.2 collective-permute-start.5
  552.6 23.2 %all-to-all-start.6 = ((bf16[4,96,1024]{2,1,0:T(8,128)(2,1)}), bf16[4,96,1024]{2,1,0:T(8,128)(2,1)S(1)}, u32[]{:S(2)}, u32[]{:S(2)}) async-start(bf16[4,96,1024]{2,1,0:T(8,128)(2,1)} %bitcast.58), calls=%async_computation.6 | async-start | bytes 1572864 | tf_op jit(solution)/shard_map/all_to_all | solution.py:157
  576.6 29.7 %all-to-all-start.16 = ((bf16[8,128,1024]{2,1,0:T(8,128)(2,1)}), bf16[8,128,1024]{2,1,0:T(8,128)(2,1)S(1)}, u32[]{:S(2)}, u32[]{:S(2)}) async-start(bf16[8,128,1024]{2,1,0:T(8,128)(2,1)} %bitcast.450), calls=%async_computation.16 | async-start | bytes 4194304 | tf_op jit(solution)/shard_map/all_to_all | solution.py:106
  606.3 23.1 %all-to-all-start.13 = ((bf16[8,128,2,256]{3,1,2,0:T(8,128)(2,1)}), bf16[8,128,2,256]{3,1,2,0:T(8,128)(2,1)}, u32[]{:S(2)}, u32[]{:S(2)}) async-start(bf16[8,128,2,256]{3,1,2,0:T(8,128)(2,1)} %copy.84), calls=%async_computation.13 | async-start | bytes 2097152 | tf_op jit(solution)/shard_map/all_to_all | solution.py:106
  629.5 13.2 %all-to-all-start.12 = ((bf16[8,128,256]{2,1,0:T(8,128)(2,1)}), bf16[8,128,256]{2,1,0:T(8,128)(2,1)S(1)}, u32[]{:S(2)}, u32[]{:S(2)}) async-start(bf16[8,128,256]{2,1,0:T(8,128)(2,1)} %bitcast.446), calls=%async_computation.12 | async-start | bytes 1048576 | tf_op jit(solution)/shard_map/all_to_all | solution.py:106
  643.5 23.7 %all-to-all-start.7 = ((bf16[4,96,1024]{2,1,0:T(8,128)(2,1)}), bf16[4,96,1024]{2,1,0:T(8,128)(2,1)S(1)}, u32[]{:S(2)}, u32[]{:S(2)}) async-start(bf16[4,96,1024]{2,1,0:T(8,128)(2,1)} %bitcast.463), calls=%async_computation.7 | async-start | bytes 1572864 | tf_op jit(solution)/shard_map/all_to_all | solution.py:157
  667.2 25.1 %all-to-all-start.11 = ((bf16[8,128,3,256]{3,1,2,0:T(8,128)(2,1)}), bf16[8,128,3,256]{3,1,2,0:T(8,128)(2,1)}, u32[]{:S(2)}, u32[]{:S(2)}) async-start(bf16[8,128,3,256]{3,1,2,0:T(8,128)(2,1)} %copy.83), calls=%async_computation.11 | async-start | bytes 3145728 | tf_op jit(solution)/shard_map/all_to_all | solution.py:106
  692.3 8.1 %all-to-all-start.10 = ((f32[8,1,1864]{2,1,0:T(1,128)}), f32[8,1,1864]{2,1,0:T(1,128)S(1)}, u32[]{:S(2)}, u32[]{:S(2)}) async-start(f32[8,1,1864]{2,1,0:T(1,128)} %copy.79), calls=%async_computation.10 | async-start | bytes 122880 | tf_op jit(solution)/shard_map/all_to_all | solution.py:113
  700.4 30.7 %all-to-all-start.9 = ((bf16[8,128,1024]{2,1,0:T(8,128)(2,1)}), bf16[8,128,1024]{2,1,0:T(8,128)(2,1)}, u32[]{:S(2)}, u32[]{:S(2)}) async-start(bf16[8,128,1024]{2,1,0:T(8,128)(2,1)} %bitcast.449), calls=%async_computation.9 | async-start | bytes 4194304 | tf_op jit(solution)/shard_map/all_to_all | solution.py:106
  731.1 29.7 %all-to-all-start.8 = ((bf16[8,128,1024]{2,1,0:T(8,128)(2,1)}), bf16[8,128,1024]{2,1,0:T(8,128)(2,1)S(1)}, u32[]{:S(2)}, u32[]{:S(2)}) async-start(bf16[8,128,1024]{2,1,0:T(8,128)(2,1)} %bitcast.448), calls=%async_computation.8 | async-start | bytes 4194304 | tf_op jit(solution)/shard_map/all_to_all | solution.py:106
  (223 other events, 3490.9 us)
Sparse Core Ops, SparseCore 0:
  9.9 30.6 all-gather.6
  42.5 27.8 all-gather.8
  72.3 25.7 all-gather.10
  100.4 24.3 all-gather.12
  126.6 29.2 all-gather.14
  182.8 28.1 all-gather.16

commit v2 on v0

v2 whole, which is shorter than its diff:
```python
import functools

import jax
import jax.numpy as jnp
from jax import lax
from jax.experimental import pallas as pl
from jax.experimental.pallas import tpu as pltpu
from jax.sharding import Mesh
from jax.sharding import PartitionSpec as P

D = 1024
HD = 64
KERNEL = 31
LEFT = 64
RIGHT = 16
SPAN = 73
PAIR = 128
KEYS = 256
EPSILON = 1e-05
MASKED = -1e30
SCALE = HD**-0.5
F32 = jnp.float32
BF16 = jnp.bfloat16


def product(left, right):
    return jnp.dot(left, right, preferred_element_type=F32)


def product_nt(left, right):
    return lax.dot_general(left, right, (((1,), (1,)), ((), ())), preferred_element_type=F32)


def product_tn(left, right):
    return lax.dot_general(left, right, (((0,), (0,)), ((), ())), preferred_element_type=F32)


def silu_slope(values):
    logistic = jax.nn.sigmoid(values)
    return logistic * (1.0 + values * (1.0 - logistic))


def norm_rows(stream, gain, offset):
    centre = stream - jnp.mean(stream, axis=-1, keepdims=True)
    inverse = lax.rsqrt(jnp.mean(centre * centre, axis=-1, keepdims=True) + EPSILON)
    normal = centre * inverse
    return (normal * gain + offset, normal, inverse)


def norm_back(upstream, normal, inverse, gain):
    scaled = upstream * gain
    inward = inverse * (
        scaled
        - jnp.mean(scaled, axis=-1, keepdims=True)
        - normal * jnp.mean(scaled * normal, axis=-1, keepdims=True)
    )
    return (inward, jnp.sum(upstream * normal, axis=0), jnp.sum(upstream, axis=0))


def bits_of(axis):
    count = lax.axis_size(axis)
    return [1 << k for k in range(count.bit_length() - 1)]


def partner(value, axis, mask):
    count = lax.axis_size(axis)
    return lax.ppermute(value, axis, [(i, i ^ mask) for i in range(count)])


def cube_gather(value, axes):
    value = value[None]
    for axis in axes:
        for mask in bits_of(axis):
            value = jnp.concatenate([value, partner(value, axis, mask)], 0)
    return value


def cube_settle(value, axes):
    for axis in reversed(axes):
        for mask in reversed(bits_of(axis)):
            half = value.shape[0] // 2
            arrived = partner(value[half:].astype(BF16), axis, mask)
            value = value[:half].astype(F32) + arrived.astype(F32)
    return value[0]


def cube_flags(axes):
    return [(lax.axis_index(axis) & mask) != 0 for axis in axes for mask in bits_of(axis)]


def crossed(blocks, axes):
    for k, flag in enumerate(cube_flags(axes)):
        blocks = [jnp.where(flag, blocks[i ^ (1 << k)], blocks[i]) for i in range(len(blocks))]
    return blocks


def position(axes, r, x, c):
    index, width = 0, 1
    for axis in axes:
        index += {"row": r, "ctx": x, "core": c}[axis] * width
        width *= lax.axis_size(axis)
    return index


def places(axes):
    rows, ctxs = lax.axis_size("row"), lax.axis_size("ctx")
    return [
        position(axes, r, x, c) for r in range(rows) for x in range(ctxs) for c in range(2)
    ]


def to_cube(value, axes):
    order = places(axes)
    width = value.shape[-1] // len(order)
    blocks = [None] * len(order)
    for k, place in enumerate(order):
        blocks[place] = value[..., k * width : (k + 1) * width]
    return jnp.concatenate(crossed(blocks, axes), -1)


def from_cube(value, axes):
    order = places(axes)
    width = value.shape[-1] // len(order)
    blocks = [value[..., k * width : (k + 1) * width] for k in range(len(order))]
    blocks = crossed(blocks, axes)
    return jnp.concatenate([blocks[place] for place in order], -1)


def stream_order(value):
    rows, ctxs = lax.axis_size("row"), lax.axis_size("ctx")
    width = value.shape[-1] // (rows * ctxs * 2)
    return jnp.concatenate(
        [
            lax.slice_in_dim(value, j * width, (j + 1) * width, axis=value.ndim - 1)
            for r in range(rows)
            for x in range(ctxs)
            for c in range(2)
            for j in [(r * 2 + c) * ctxs + x]
        ],
        -1,
    )


def natural_order(value):
    rows, ctxs = lax.axis_size("row"), lax.axis_size("ctx")
    width = value.shape[-1] // (rows * ctxs * 2)
    return jnp.concatenate(
        [
            lax.slice_in_dim(value, j * width, (j + 1) * width, axis=value.ndim - 1)
            for r in range(rows)
            for c in range(2)
            for x in range(ctxs)
            for j in [(r * ctxs + x) * 2 + c]
        ],
        -1,
    )


def swap_core(value):
    return lax.ppermute(value, "core", [(0, 1), (1, 0)])


def along(value, step):
    count = lax.axis_size("ctx") * lax.axis_size("tp")
    pairs = [(i, i + step) for i in range(count) if 0 <= i + step < count]
    return lax.ppermute(value, ("ctx", "tp"), pairs)


def widen_tp(rows):
    return lax.all_gather(rows, "tp", axis=0, tiled=True)


def narrow_tp(partial_value):
    count = lax.axis_size("tp")
    pieces = partial_value.astype(BF16).reshape(
        count, partial_value.shape[0] // count, partial_value.shape[1]
    )
    return jnp.sum(lax.all_to_all(pieces, "tp", 0, 0).astype(F32), axis=0)


def widen_core(rows):
    return jnp.concatenate([rows, swap_core(rows)], 0)


def narrow_core(partial_value):
    half = partial_value.shape[0] // 2
    arrived = swap_core(partial_value[half:].astype(BF16))
    return partial_value[:half].astype(F32) + arrived.astype(F32)


def pick(flag, pair_value, axis):
    return jnp.where(
        flag,
        lax.index_in_dim(pair_value, 1, axis, keepdims=False),
        lax.index_in_dim(pair_value, 0, axis, keepdims=False),
    )


def core_weights(matrices, second):
    halves = jnp.concatenate(
        [m.reshape(m.shape[0], 2, 1, m.shape[1] // 2) for m in matrices], 2
    )
    rows, count, half = halves.shape[0], halves.shape[2], halves.shape[3]
    own = pick(second, halves, 1)
    other = swap_core(pick(jnp.logical_not(second), halves, 1))
    own = own.reshape(rows, count * half)
    other = other.reshape(rows, count * half)
    both = jnp.concatenate(
        [jnp.where(second, other, own), jnp.where(second, own, other)], 0
    )
    whole = lax.all_gather(both, ("tp", "row", "ctx"), axis=0, tiled=True)
    whole = whole.reshape(lax.axis_size("tp"), D, count * half)
    return [
        jnp.concatenate([whole[z][:, m * half : (m + 1) * half] for z in range(whole.shape[0])], 1)
        for m in range(count)
    ]


def core_settle(grads, second):
    tp = lax.axis_size("tp")
    group = lax.axis_size("row") * lax.axis_size("ctx")
    count, half = len(grads), grads[0].shape[1] // tp
    columns = [g[:, z * half : (z + 1) * half] for z in range(tp) for g in grads]
    packed = jnp.concatenate(columns, 1).astype(BF16)
    packed = packed.reshape(group, D // group, packed.shape[1])
    total = jnp.sum(lax.all_to_all(packed, ("row", "ctx"), 0, 0).astype(F32), axis=0).astype(BF16)
    width = count * half
    stacked = jnp.stack([total[:, z * width : (z + 1) * width] for z in range(tp)], 0)
    total = jnp.sum(lax.all_to_all(stacked, "tp", 0, 0).astype(F32), axis=0)
    total = total.reshape(2, total.shape[0] // 2, count, half)
    own = pick(second, total, 0)
    other = swap_core(pick(jnp.logical_not(second), total, 0).astype(BF16)).astype(F32)
    whole = jnp.concatenate(
        [jnp.where(second, other, own), jnp.where(second, own, other)], 2
    )
    return [whole[:, m] for m in range(count)]


def window(first_ref, lens_ref, clip, height):
    rows = lax.broadcasted_iota(jnp.int32, (height, KEYS), 0)
    lanes = lax.broadcasted_iota(jnp.int32, (height, KEYS), 1)
    offset = lanes - rows
    frame = lanes + (first_ref[0] - LEFT)
    in_band = (offset >= 0) & (offset < SPAN)
    allowed = in_band & (frame >= 0) & (frame < lens_ref[clip])
    return in_band, allowed


def keys_of(left_ref, own_ref, right_ref, clip, height):
    rest = KEYS - LEFT - RIGHT - height
    return jnp.concatenate(
        [
            left_ref[clip],
            own_ref[clip * height : (clip + 1) * height],
            right_ref[clip],
            jnp.zeros((rest, PAIR), BF16),
        ],
        0,
    )


def attend_kernel(
    height, first_ref, lens_ref, q_ref, k_ref, v_ref, kl_ref, vl_ref, kr_ref, vr_ref,
    rel_ref, out_ref, context_ref, chance_ref, branch_ref, total
):
    step = pl.program_id(0)
    odd = lax.broadcasted_iota(jnp.int32, (1, PAIR), 1) >= HD
    for clip in range(2):
        query = q_ref[clip * height : (clip + 1) * height]
        keys = keys_of(kl_ref, k_ref, kr_ref, clip, height)
        values = keys_of(vl_ref, v_ref, vr_ref, clip, height)
        in_band, allowed = window(first_ref, lens_ref, clip, height)
        context = jnp.zeros((height, PAIR), F32)
        for head in range(2):
            mine = odd if head else jnp.logical_not(odd)
            q_head = jnp.where(mine, query, jnp.zeros_like(query))
            relative = product(q_head, rel_ref[...])
            relative = jnp.concatenate([relative, jnp.zeros((height, KEYS - PAIR), F32)], 1)
            relative = pltpu.roll(relative, 0, 1, stride=1, stride_axis=0)
            score = (product_nt(q_head, keys) + relative) * SCALE
            masked = jnp.where(allowed, score, MASKED)
            ceiling = jnp.max(masked, axis=-1, keepdims=True)
            raised = jnp.where(in_band, jnp.exp(masked - ceiling), 0.0)
            chance = raised / jnp.sum(raised, axis=-1, keepdims=True)
            chance_ref[0, clip, head] = chance
            part = product(chance.astype(BF16), values)
            context = jnp.where(mine, part, context)
        context_ref[clip * height : (clip + 1) * height] = context.astype(BF16)
    branch = product_nt(context_ref[...], out_ref[...])

    @pl.when(step == 0)
    def _():
        total[...] = branch

    @pl.when(step > 0)
    def _():
        total[...] += branch

    @pl.when(step == pl.num_programs(0) - 1)
    def _():
        branch_ref[...] = total[...].astype(BF16)


def attend_back_kernel(
    height, first_ref, lens_ref, up_ref, q_ref, k_ref, v_ref, kl_ref, vl_ref, kr_ref, vr_ref,
    rel_ref, out_ref, chance_ref, dq_ref, own_ref, left_ref, right_ref, table_ref
):
    step = pl.program_id(0)
    odd = lax.broadcasted_iota(jnp.int32, (1, PAIR), 1) >= HD
    d_context = product(up_ref[...], out_ref[...]).astype(BF16)
    table = jnp.zeros((PAIR, PAIR), F32)
    flip = (
        lax.broadcasted_iota(jnp.int32, (height, height), 0)
        + lax.broadcasted_iota(jnp.int32, (height, height), 1)
        == height - 1
    ).astype(BF16)
    for clip in range(2):
        query = q_ref[clip * height : (clip + 1) * height]
        upstream = d_context[clip * height : (clip + 1) * height]
        keys = keys_of(kl_ref, k_ref, kr_ref, clip, height)
        values = keys_of(vl_ref, v_ref, vr_ref, clip, height)
        _, allowed = window(first_ref, lens_ref, clip, height)
        d_query = jnp.zeros((height, PAIR), F32)
        d_keys = jnp.zeros((KEYS, PAIR), F32)
        d_values = jnp.zeros((KEYS, PAIR), F32)
        for head in range(2):
            mine = odd if head else jnp.logical_not(odd)
            q_head = jnp.where(mine, query, jnp.zeros_like(query))
            up_head = jnp.where(mine, upstream, jnp.zeros_like(upstream))
            chance = chance_ref[0, clip, head]
            d_chance = product_nt(up_head, values)
            inner = jnp.sum(d_chance * chance, axis=-1, keepdims=True)
            d_score = jnp.where(allowed, chance * (d_chance - inner), 0.0).astype(BF16)
            d_values += product_tn(chance.astype(BF16), up_head)
            d_keys += product_tn(d_score, q_head)
            relative = pltpu.roll(
                product(flip, d_score), KEYS - height + 1, 1, stride=1, stride_axis=0
            )[:, :PAIR].astype(BF16)
            relative = product(flip, relative).astype(BF16)
            part = product(d_score, keys) + product_nt(relative, rel_ref[...])
            d_query = jnp.where(mine, part, d_query)
            table += product_tn(q_head, relative)
        dq_ref[clip * height : (clip + 1) * height] = (d_query * SCALE).astype(BF16)
        for slot, value in ((0, d_keys * SCALE), (1, d_values)):
            left_ref[slot, clip] = value[:LEFT].astype(BF16)
            own_ref[slot, clip] = value[LEFT : LEFT + height]
            right_ref[slot, clip] = value[LEFT + height : LEFT + height + RIGHT].astype(BF16)

    @pl.when(step == 0)
    def _():
        table_ref[...] = table * SCALE

    @pl.when(step > 0)
    def _():
        table_ref[...] += table * SCALE


def attend_specs(height, channels):
    steps = channels // PAIR
    rows = pl.BlockSpec((2 * height, PAIR), lambda z: (0, z))
    k_own = pl.BlockSpec((2 * height, PAIR), lambda z: (0, steps + z))
    v_own = pl.BlockSpec((2 * height, PAIR), lambda z: (0, 2 * steps + z))
    k_left = pl.BlockSpec((2, LEFT, PAIR), lambda z: (0, 0, z))
    v_left = pl.BlockSpec((2, LEFT, PAIR), lambda z: (0, 0, steps + z))
    k_right = pl.BlockSpec((2, RIGHT, PAIR), lambda z: (0, 0, z))
    v_right = pl.BlockSpec((2, RIGHT, PAIR), lambda z: (0, 0, steps + z))
    table = pl.BlockSpec((PAIR, PAIR), lambda z: (0, 0))
    weight = pl.BlockSpec((D, PAIR), lambda z: (0, z))
    scalar = pl.BlockSpec(memory_space=pltpu.SMEM)
    return steps, rows, k_own, v_own, k_left, v_left, k_right, v_right, table, weight, scalar


def attend(first, lens, project, left, right, rel, out_all):
    height, channels = project.shape[0] // 2, project.shape[1] // 3
    steps, rows, k_own, v_own, k_left, v_left, k_right, v_right, table, weight, scalar = (
        attend_specs(height, channels)
    )
    return pl.pallas_call(
        functools.partial(attend_kernel, height),
        grid=(steps,),
        in_specs=[
            scalar, scalar, rows, k_own, v_own, k_left, v_left, k_right, v_right, table, weight
        ],
        out_specs=[
            rows,
            pl.BlockSpec((1, 2, 2, height, KEYS), lambda z: (z, 0, 0, 0, 0)),
            pl.BlockSpec((2 * height, D), lambda z: (0, 0)),
        ],
        out_shape=[
            jax.ShapeDtypeStruct((2 * height, channels), BF16),
            jax.ShapeDtypeStruct((steps, 2, 2, height, KEYS), F32),
            jax.ShapeDtypeStruct((2 * height, D), BF16),
        ],
        scratch_shapes=[pltpu.VMEM((2 * height, D), F32)],
        compiler_params=pltpu.CompilerParams(vmem_limit_bytes=32 << 20),
        name="attend",
    )(first, lens, project, project, project, left, left, right, right, rel, out_all)


def attend_back(first, lens, upstream, project, left, right, rel, out_all, chance):
    height, channels = project.shape[0] // 2, project.shape[1] // 3
    steps, rows, k_own, v_own, k_left, v_left, k_right, v_right, table, weight, scalar = (
        attend_specs(height, channels)
    )
    sided = lambda n: pl.BlockSpec((2, 2, n, PAIR), lambda z: (0, 0, 0, z))
    return pl.pallas_call(
        functools.partial(attend_back_kernel, height),
        grid=(steps,),
        in_specs=[
            scalar, scalar, pl.BlockSpec((2 * height, D), lambda z: (0, 0)), rows, k_own, v_own,
            k_left, v_left, k_right, v_right, table, weight,
            pl.BlockSpec((1, 2, 2, height, KEYS), lambda z: (z, 0, 0, 0, 0)),
        ],
        out_specs=[rows, sided(height), sided(LEFT), sided(RIGHT), table],
        out_shape=[
            jax.ShapeDtypeStruct((2 * height, channels), BF16),
            jax.ShapeDtypeStruct((2, 2, height, channels), F32),
            jax.ShapeDtypeStruct((2, 2, LEFT, channels), BF16),
            jax.ShapeDtypeStruct((2, 2, RIGHT, channels), BF16),
            jax.ShapeDtypeStruct((PAIR, PAIR), F32),
        ],
        compiler_params=pltpu.CompilerParams(vmem_limit_bytes=32 << 20),
        name="attend_back",
    )(
        first, lens, upstream, project, project, project, left, left, right, right, rel,
        out_all, chance,
    )


def ffn_forward(hidden, weight_in, weight_out):
    before = product(hidden, weight_in)
    active = jax.nn.silu(before).astype(BF16)
    return narrow_tp(product_nt(active, weight_out)), before, active


def ffn_backward(d_branch_in, d_branch_out, before, active, hidden, weight_in, weight_out):
    d_active = product(d_branch_out, weight_out)
    d_before = (d_active * silu_slope(before)).astype(BF16)
    d_hidden = product_nt(d_before, weight_in)
    grad_out = product_tn(d_branch_in, active)
    grad_in = product_tn(hidden, d_before)
    return d_hidden, grad_in, grad_out


def settle_wide(value):
    count = lax.axis_size("row") * lax.axis_size("ctx") * 2
    pieces = value.astype(BF16).reshape(count, value.shape[0] // count, value.shape[1])
    pieces = lax.all_to_all(pieces, ("row", "ctx", "core"), 0, 0)
    return jnp.sum(pieces.astype(F32), axis=0)


def settle_cut(value):
    return jnp.sum(lax.all_to_all(value, ("row", "ctx", "core"), 0, 0), axis=0)


IN_AXES = ("row", "ctx", "core")
OUT_AXES = ("ctx", "row", "core")


def body(
    inputs,
    cotangent,
    lengths,
    buckets,
    ffn1_in,
    ffn1_out,
    norm_gains,
    norm_biases,
    qkv_weight,
    attn_out,
    distance,
    glu_in,
    depthwise,
    conv_gain,
    conv_bias,
    conv_out,
    ffn2_in,
    ffn2_out,
):
    rows, ctxs, tp = lax.axis_size("row"), lax.axis_size("ctx"), lax.axis_size("tp")
    group = rows * ctxs * 2
    second = lax.axis_index("core") == 1
    local = ffn1_in.shape[0]
    height = inputs.shape[1]
    first = (lax.axis_index("ctx") * tp + lax.axis_index("tp")) * height
    lens = widen_core(lengths)
    frame_ids = first + jnp.arange(height, dtype=jnp.int32)
    live = (frame_ids[None, :] < lens[:, None]).astype(F32).reshape(2 * height, 1)

    near = stream_order(inputs[0])
    wide_inputs = widen_tp(near)
    one_in = cube_gather(ffn1_in, IN_AXES).reshape(D, -1)
    one_out = cube_gather(ffn1_out, OUT_AXES).reshape(D, -1)

    small = jnp.concatenate(
        [
            norm_gains.T.reshape(-1),
            norm_biases.T.reshape(-1),
            distance.reshape(-1),
            depthwise.T.reshape(-1),
            conv_gain,
            conv_bias,
        ]
    )
    norm_count, table_count = 10 * local, distance.size
    cube = cube_gather(small, ("core", "row", "ctx"))
    blocks = crossed([cube[k] for k in range(group)], ("core", "row", "ctx"))
    order = [
        (x * rows + r) * 2 + c for r in range(rows) for x in range(ctxs) for c in range(2)
    ]
    norms = jnp.concatenate([blocks[k][:norm_count].reshape(10, local) for k in order], 1)
    norms = norms.astype(F32)
    gains, biases = norms[:5], norms[5:]
    natural = [
        (x * rows + r) * 2 + c for r in range(rows) for c in range(2) for x in range(ctxs)
    ]
    table_all = jnp.concatenate(
        [
            blocks[k][norm_count : norm_count + table_count].reshape(-1, SPAN)
            for k in natural
        ],
        0,
    )
    width = conv_gain.shape[0]
    conv_small = jnp.concatenate(
        [blocks[k][norm_count + table_count :].reshape(KERNEL + 2, width) for k in natural], 1
    )
    half = conv_small.shape[1] // 2
    conv_small = jnp.where(second, conv_small[:, half:], conv_small[:, :half])
    conv_cube = cube_gather(conv_small, ("tp",))
    conv_blocks = crossed([conv_cube[k] for k in range(tp)], ("tp",))
    conv_small = jnp.concatenate(conv_blocks, 1).astype(F32)
    taps, conv_scale, conv_shift = conv_small[:KERNEL], conv_small[KERNEL], conv_small[KERNEL + 1]

    wq, wk, wv, w_attn = core_weights(
        [qkv_weight[:, 0], qkv_weight[:, 1], qkv_weight[:, 2], attn_out], second
    )
    qkv_all = jnp.concatenate([wq, wk, wv], 1)
    w_value, w_gate, w_conv = core_weights([glu_in[:, 0], glu_in[:, 1], conv_out], second)
    glu_all = jnp.concatenate([w_value, w_gate], 1)
    two = lax.all_gather(
        jnp.concatenate([ffn2_in, ffn2_out], 1), ("row", "ctx", "core"), axis=0, tiled=True
    )
    two_in, two_out = two[:, : ffn2_in.shape[1]], two[:, ffn2_in.shape[1] :]

    selector = (jnp.arange(SPAN, dtype=jnp.int32)[:, None] == buckets[None, :]).astype(BF16)
    rel = product(table_all, selector).astype(BF16)
    rel = jnp.pad(jnp.concatenate([rel, rel], 0), ((0, 0), (0, PAIR - SPAN)))

    hidden0, _, _ = norm_rows(wide_inputs.astype(F32), gains[0], biases[0])
    hidden0 = to_cube(hidden0.astype(BF16), IN_AXES)
    stream0 = near.astype(F32)
    branch, before0, active0 = ffn_forward(hidden0, one_in, one_out)
    stream1 = stream0 + 0.5 * from_cube(branch, OUT_AXES)

    normed, normal1, inverse1 = norm_rows(stream1, gains[1], biases[1])
    hidden1 = widen_core(normed.astype(BF16))
    project = product(hidden1, qkv_all).astype(BF16)
    channels = qkv_all.shape[1] // 3
    key_value = project[:, channels:].reshape(2, height, 2 * channels)
    left = along(key_value[:, height - LEFT :], 1)
    right = along(key_value[:, :RIGHT], -1)
    first_ref = first.reshape(1).astype(jnp.int32)
    context, chance, branch = attend(first_ref, lens, project, left, right, rel, w_attn)
    stream2 = stream1 + narrow_core(branch)

    normed, normal2, inverse2 = norm_rows(stream2, gains[2], biases[2])
    hidden2 = widen_core(normed.astype(BF16))
    halves = product(hidden2, glu_all)
    value_half, gate_half = halves[:, :channels], halves[:, channels:]
    logistic = jax.nn.sigmoid(gate_half)
    gated = (value_half * logistic * live).astype(BF16).reshape(2, height, channels)
    tail = KERNEL - 1
    earlier = along(gated[:, height - tail :], 1)
    extended = jnp.concatenate([earlier, gated], 1)
    mixed = extended[:, 0:height] * taps[0]
    for offset in range(1, KERNEL):
        mixed = mixed + extended[:, offset : offset + height] * taps[offset]
    mixed = mixed.reshape(2 * height, channels)
    sums = jnp.stack([jnp.sum(mixed, axis=1), jnp.sum(mixed * mixed, axis=1)], 1)
    sums = (sums + turned(swap_core(sums))) / D
    centre, square = sums[:, :1], sums[:, 1:]
    inverse_conv = lax.rsqrt(square - centre * centre + EPSILON)
    conv_normal = (mixed - centre) * inverse_conv
    levels = conv_normal * conv_scale + conv_shift
    active_conv = jax.nn.silu(levels).astype(BF16)
    stream3 = stream2 + narrow_core(product_nt(active_conv, w_conv))

    normed, normal3, inverse3 = norm_rows(stream3, gains[3], biases[3])
    hidden3 = widen_tp(normed.astype(BF16))
    branch, before3, active3 = ffn_forward(hidden3, two_in, two_out)
    stream4 = stream3 + 0.5 * branch
    result, normal4, inverse4 = norm_rows(stream4, gains[4], biases[4])

    d_stream, gain4, bias4 = norm_back(
        stream_order(cotangent[0]).astype(F32), normal4, inverse4, gains[4]
    )
    d_branch = widen_tp((0.5 * d_stream).astype(BF16))
    d_hidden, grad_two_in, grad_two_out = ffn_backward(
        d_branch, d_branch, before3, active3, hidden3, two_in, two_out
    )
    d_input, gain3, bias3 = norm_back(narrow_tp(d_hidden), normal3, inverse3, gains[3])
    d_stream = d_stream + d_input
    grad_two_in, grad_two_out = settle_wide(grad_two_in), settle_wide(grad_two_out)

    d_branch = widen_core(d_stream.astype(BF16))
    d_levels = product(d_branch, w_conv) * silu_slope(levels)
    grad_w_conv = product_tn(d_branch, active_conv)
    grad_scale = jnp.sum(d_levels * conv_normal, axis=0)
    grad_shift = jnp.sum(d_levels, axis=0)
    scaled = d_levels * conv_scale
    sums = jnp.stack([jnp.sum(scaled, axis=1), jnp.sum(scaled * conv_normal, axis=1)], 1)
    sums = (sums + turned(swap_core(sums))) / D
    d_mixed = inverse_conv * (scaled - sums[:, :1] - conv_normal * sums[:, 1:])
    d_mixed = d_mixed.reshape(2, height, channels)
    d_extended = jnp.zeros((2, height + tail, channels), F32)
    tap_grads = []
    for offset in range(KERNEL):
        d_extended = d_extended + jnp.pad(
            d_mixed * taps[offset], ((0, 0), (offset, tail - offset), (0, 0))
        )
        tap_grads.append(jnp.sum(d_mixed * extended[:, offset : offset + height], axis=(0, 1)))
    later = along(d_extended[:, :tail], -1)
    d_gated = d_extended[:, tail:] + jnp.pad(later, ((0, 0), (height - tail, 0), (0, 0)))
    d_gated = d_gated.reshape(2 * height, channels) * live
    d_halves = jnp.concatenate(
        [d_gated * logistic, d_gated * value_half * logistic * (1.0 - logistic)], 1
    ).astype(BF16)
    d_hidden = narrow_core(product_nt(d_halves, glu_all))
    grad_glu = product_tn(hidden2, d_halves)
    d_input, gain2, bias2 = norm_back(d_hidden, normal2, inverse2, gains[2])
    d_stream = d_stream + d_input
    grad_value, grad_gate, grad_w_conv = core_settle(
        [grad_glu[:, :channels], grad_glu[:, channels:], grad_w_conv], second
    )

    d_branch = widen_core(d_stream.astype(BF16))
    d_query, d_own, d_left, d_right, d_table = attend_back(
        first_ref, lens, d_branch, project, left, right, rel, w_attn, chance
    )
    grad_w_attn = product_tn(d_branch, context)
    from_next = along(d_left, -1).astype(F32)
    from_last = along(d_right, 1).astype(F32)
    d_own = d_own + jnp.pad(from_next, ((0, 0), (0, 0), (height - LEFT, 0), (0, 0)))
    d_own = d_own + jnp.pad(from_last, ((0, 0), (0, 0), (0, height - RIGHT), (0, 0)))
    d_own = d_own.astype(BF16).reshape(2, 2 * height, channels)
    d_project = jnp.concatenate([d_query, d_own[0], d_own[1]], 1)
    d_hidden = narrow_core(product_nt(d_project, qkv_all))
    grad_qkv = product_tn(hidden1, d_project)
    d_input, gain1, bias1 = norm_back(d_hidden, normal1, inverse1, gains[1])
    d_stream = d_stream + d_input
    grad_q, grad_k, grad_v, grad_w_attn = core_settle(
        [
            grad_qkv[:, :channels],
            grad_qkv[:, channels : 2 * channels],
            grad_qkv[:, 2 * channels :],
            grad_w_attn,
        ],
        second,
    )

    _, normal0, inverse0 = norm_rows(stream0, gains[0], biases[0])
    d_branch = widen_tp((0.5 * d_stream).astype(BF16))
    d_branch = to_cube(d_branch, OUT_AXES)
    d_hidden, grad_one_in, grad_one_out = ffn_backward(
        d_branch, d_branch, before0, active0, hidden0, one_in, one_out
    )
    d_hidden = from_cube(narrow_tp(d_hidden), IN_AXES)
    d_input, gain0, bias0 = norm_back(d_hidden, normal0, inverse0, gains[0])
    d_stream = d_stream + d_input
    grad_one_in = cube_settle(grad_one_in.reshape(group, local, -1), IN_AXES)
    grad_one_out = cube_settle(grad_one_out.reshape(group, local, -1), OUT_AXES)

    d_rel = (d_table[:HD] + d_table[HD:])[:, :SPAN]
    grad_table = jnp.dot(d_rel, selector.astype(F32).T, precision=lax.Precision.HIGHEST)
    table_cut = grad_table.reshape(rows, 2, ctxs, table_count).transpose(0, 2, 1, 3)
    conv_cut = jnp.concatenate(
        [jnp.stack(tap_grads, 0), grad_scale[None], grad_shift[None]], 0
    ).reshape(KERNEL + 2, tp, half)
    conv_cut = jnp.where(
        second,
        jnp.concatenate([jnp.zeros_like(conv_cut), conv_cut], 2),
        jnp.concatenate([conv_cut, jnp.zeros_like(conv_cut)], 2),
    )
    conv_cut = conv_cut.reshape(KERNEL + 2, tp, rows, 2, ctxs, width)
    conv_cut = conv_cut.transpose(2, 4, 3, 1, 0, 5)
    packed = jnp.concatenate(
        [table_cut.reshape(group, -1), conv_cut.reshape(group, -1)], 1
    )
    packed = lax.psum(settle_cut(packed), "tp")
    grad_table = packed[:table_count].reshape(distance.shape)
    conv_cut = packed[table_count:].reshape(tp, KERNEL + 2, width)
    conv_cut = lax.dynamic_index_in_dim(conv_cut, lax.axis_index("tp"), 0, keepdims=False)

    norm_grads = jnp.stack(
        [gain0, gain1, gain2, gain3, gain4, bias0, bias1, bias2, bias3, bias4], 0
    )
    norm_grads = norm_grads.reshape(10, group, local).transpose(1, 0, 2)
    norm_grads = lax.psum(settle_cut(norm_grads.reshape(group, -1)), "tp").reshape(10, local)

    return (
        natural_order(result.astype(BF16))[None],
        natural_order(d_stream)[None],
        grad_one_in,
        grad_one_out,
        norm_grads[:5].T,
        norm_grads[5:].T,
        jnp.stack([grad_q, grad_k, grad_v], 1),
        grad_w_attn,
        grad_table,
        jnp.stack([grad_value, grad_gate], 1),
        conv_cut[:KERNEL].T,
        conv_cut[KERNEL],
        conv_cut[KERNEL + 1],
        grad_w_conv,
        grad_two_in,
        grad_two_out,
    )


def turned(sums):
    half = sums.shape[0] // 2
    return jnp.concatenate([sums[half:], sums[:half]], 0)


def solution(mesh):
    shards, ctxs, tp = (mesh.shape[axis] for axis in ("shard", "ctx", "tp"))
    cut = Mesh(mesh.devices.reshape(shards // 2, 2, ctxs, tp), ("row", "core", "ctx", "tp"))
    shard = ("row", "core")
    block = ("row", "core", "ctx")
    every = ("tp", "row", "core", "ctx")
    weight = P(block, "tp")
    narrow = P(block, None)
    deep = P(block, None, "tp")
    frames = P(shard, ("ctx", "tp"), None)
    return jax.shard_map(
        body,
        mesh=cut,
        in_specs=(
            frames, frames, P(shard), P(), weight, weight, narrow, narrow, deep, weight, narrow,
            deep, P(every, None), P(every), P(every), weight, weight, weight,
        ),
        out_specs=(
            frames, frames, weight, weight, narrow, narrow, deep, weight, narrow, deep,
            P(every, None), P(every), P(every), weight, weight, weight,
        ),
        check_vma=False,
    )
```

time: 1540 us -> 677 us (0.44)
  waiting for transfers between devices: 721 us -> 197 us
  blocking collectives: 525 us -> 106 us
  matrix products: 127 us -> 40.2 us
  local copies, waits for them, and re-layouts: 59.8 us -> 120 us
  starting transfers between devices: 23.5 us -> 83.6 us
  other arithmetic: 52.2 us -> 79 us
  Pallas kernels: 0 us -> 21.7 us
    reduce_scatter x22 -> x0, waiting for transfers between devices: 583 us -> none  [the longest x2 111 us: settle_pair(): lax.psum_scatter(couple[0], ('shard', 'ctx'), scatter_dimension=0, tiled=...]
    all_gather x24 -> x4, blocking collectives: 420 us -> 81 us  [widen_tp(): return lax.all_gather(rows, 'tp', axis=0, tiled=True)]
    all_to_all x0 -> x12, waiting for transfers between devices: none -> 114 us  [the longest x4 52.2 us: narrow_tp(): return jnp.sum(lax.all_to_all(pieces, 'tp', 0, 0).astype(F32), axis=0)]
    all_gather x12 -> x3, waiting for transfers between devices: 99.7 us -> 39.4 us  [the longest x2 39.4 us: core_weights(): whole = lax.all_gather(both, ('tp', 'row', 'ctx'), axis=0, tiled=True)]
    unnamed x230 -> x657, local copies, waits for them, and re-layouts: 21.2 us -> 78.3 us
    unnamed x3 -> x0, blocking collectives: 52.1 us -> none
    all_to_all x0 -> x12, starting transfers between devices: none -> 49.4 us  [the longest x4 15.9 us: narrow_tp(): return jnp.sum(lax.all_to_all(pieces, 'tp', 0, 0).astype(F32), axis=0)]
    dot_general x30 -> x7, matrix products: 49.8 us -> 15.2 us  [product_nt(): lax.dot_general(left, right, (((1,), (1,)), ((), ())), preferred_element_...]
  transfers between devices with their start and end apart: 44 -> 53, of which waited for: 34 -> 25; matrix products, arithmetic and copies ran while one was open for 4% -> 30% of each run, Pallas kernels for 0% -> 3%
where the time goes in v2:
time: 677 us; the launch traced here: 667 us
  waiting for transfers between devices  197 us (29%)
  local copies, waits for them, and re-layouts  120 us (18%)
  blocking collectives  106 us (16%)
  starting transfers between devices  83.6 us (12%)
  other arithmetic  79 us (12%)
  matrix products  40.2 us (6%)
  Pallas kernels  21.7 us (3%)
  between operations  19.3 us (3%)
    all_gather x4, blocking collectives, widen_tp(): return lax.all_gather(rows, 'tp', axis=0, tiled=True)  81 us
    unnamed x657, local copies, waits for them, and re-layouts  78.3 us
    all_to_all x4, waiting for transfers between devices, narrow_tp(): return jnp.sum(lax.all_to_all(pieces, 'tp', 0, 0).astype(F32), axis=0)  52.2 us
    all_to_all x2, waiting for transfers between devices, core_settle(): lax.all_to_all(packed, ('row', 'ctx'), 0, 0).astype(F32)  44.7 us
    all_gather x2, waiting for transfers between devices, core_weights(): whole = lax.all_gather(both, ('tp', 'row', 'ctx'), axis=0, tiled=True)  39.4 us
    psum x1, blocking collectives, body(): lax.psum(settle_cut(norm_grads.reshape(group, -1)), 'tp').reshape(10, local)  25 us
    ppermute x17, waiting for transfers between devices, partner(): return lax.ppermute(value, axis, [(i, i ^ mask) for i in range(count)])  23 us
    all_to_all x4, starting transfers between devices, narrow_tp(): return jnp.sum(lax.all_to_all(pieces, 'tp', 0, 0).astype(F32), axis=0)  15.9 us
  transfers between devices with their start and end apart: 53, of which 25 were waited for; matrix products, arithmetic and copies ran while one was open for 30% of the time, Pallas kernels for 3%

profile of v2, /device:TPU:0, one launch (start us, length us, event | category | flops | bytes accessed | tf_op | source)
XLA Modules:
  0.0 666.7 jit_solution(7383835677263263416)
XLA Ops:
  23.4 22.5 %all_gather.21 = bf16[384,1024]{1,0:T(8,128)(2,1)S(1)} all-gather(bf16[96,1024]{1,0:T(8,128)(2,1)S(1)} %constant_dynamic-update-slice_fusion), channel_id=1, replica_groups=mesh['row'=2,'core'=2,'ctx'=2,'tp'=4] {'tp'}, dimensions={0}, use_global_device_ids=true | all-gather | bytes 983040 | tf_op jit(solution)/shard_map/all_gather | solution.py:170
  71.4 15.8 %collective-permute-done.4 = bf16[2,128,1024]{2,1,0:T(8,128)(2,1)S(1)} collective-permute-done((bf16[2,128,1024]{2,1,0:T(8,128)(2,1)}, bf16[2,128,1024]{2,1,0:T(8,128)(2,1)S(1)}, u32[]{:S(2)}, u32[]{:S(2)}) %collective-permute-start.4) | collective-permute-done | bytes 524320 | tf_op jit(solution)/shard_map/ppermute | solution.py:67
  102.4 3.7 all-to-all-start
  111.2 20.7 %all-to-all-done = bf16[4,96,1024]{2,1,0:T(8,128)(2,1)S(1)} async-done(((bf16[4,96,1024]{2,1,0:T(8,128)(2,1)}), bf16[4,96,1024]{2,1,0:T(8,128)(2,1)S(1)}, u32[]{:S(2)}, u32[]{:S(2)}) %all-to-all-start) | async-done | bytes 786464 | tf_op jit(solution)/shard_map/all_to_all | solution.py:178
  142.6 39.4 %all-gather.4.cloned.1.call-done = bf16[4096,512]{1,0:T(8,128)(2,1)} async-done(((bf16[256,512]{1,0:T(8,128)(2,1)}), bf16[4096,512]{1,0:T(8,128)(2,1)}) %all-gather.4.cloned.1.call-update) | async-done | bytes 4194320 | tf_op jit(solution)/shard_map/all_gather | solution.py:211
  202.3 7.2 %collective-permute-done.13.kr_ref.vr_ref = bf16[2,16,1024]{2,1,0:T(8,128)(2,1)S(1)} collective-permute-done((bf16[2,16,1024]{2,1,0:T(8,128)(2,1)S(1)}, bf16[2,16,1024]{2,1,0:T(8,128)(2,1)S(1)}, u32[]{:S(2)}, u32[]{:S(2)}) %collective-permute-start.13) | collective-permute-done | bytes 65568 | tf_op jit(solution)/shard_map/ppermute | solution.py:166
  209.5 8.8 %attend.1 = (bf16[192,512]{1,0:T(8,128)(2,1)S(1)}, f32[4,2,2,96,256]{4,3,2,1,0:T(8,128)S(1)}, bf16[192,1024]{1,0:T(8,128)(2,1)S(1)}) custom-call(s32[1]{0:T(128)} %bitcast.21.first_ref, s32[2]{0:T(128)S(1)} %pad_add_fusion.1.lens_ref, bf16[192,1536]{1,0:T(8,128)(2,1)S(1)} %convolution_convert_fusion.1.q_ref.k_ref.v_ref, ...), custom_call_target="tpu_custom_call" | custom-call | tf_op jit(solution)/shard_map/attend/pallas_call | solution.py:378
  240.9 22.0 %all_gather.24 = bf16[384,1024]{1,0:T(8,128)(2,1)} all-gather(bf16[96,1024]{1,0:T(8,128)(2,1)S(1)} %add_convert_fusion.2), channel_id=1, replica_groups=mesh['row'=2,'core'=2,'ctx'=2,'tp'=4] {'tp'}, dimensions={0}, use_global_device_ids=true | all-gather | bytes 983040 | tf_op jit(solution)/shard_map/all_gather | solution.py:170
  267.8 4.3 all-to-all-start.1
  280.3 10.8 %all-to-all-done.1 = bf16[4,96,1024]{2,1,0:T(8,128)(2,1)} async-done(((bf16[4,96,1024]{2,1,0:T(8,128)(2,1)}), bf16[4,96,1024]{2,1,0:T(8,128)(2,1)}, u32[]{:S(2)}, u32[]{:S(2)}) %all-to-all-start.1) | async-done | bytes 786464 | tf_op jit(solution)/shard_map/all_to_all | solution.py:178
  295.4 18.1 %all_gather.26 = bf16[384,1024]{1,0:T(8,128)(2,1)S(1)} all-gather(bf16[96,1024]{1,0:T(8,128)(2,1)S(1)} %multiply_convert_fusion.7), channel_id=1, replica_groups=mesh['row'=2,'core'=2,'ctx'=2,'tp'=4] {'tp'}, dimensions={0}, use_global_device_ids=true | all-gather | bytes 983040 | tf_op jit(solution)/shard_map/all_gather | solution.py:170
  319.0 4.2 all-to-all-start.2
  323.8 4.1 convolution_convert_fusion.3
  330.6 9.7 %all-to-all-done.2 = bf16[4,96,1024]{2,1,0:T(8,128)(2,1)} async-done(((bf16[4,96,1024]{2,1,0:T(8,128)(2,1)}), bf16[4,96,1024]{2,1,0:T(8,128)(2,1)}, u32[]{:S(2)}, u32[]{:S(2)}) %all-to-all-start.2) | async-done | bytes 786464 | tf_op jit(solution)/shard_map/all_to_all | solution.py:178
  340.4 4.5 all-to-all-start.11
  388.5 6.0 all-to-all-start.10
  398.3 12.8 %attend_back.1 = (bf16[192,512]{1,0:T(8,128)(2,1)S(1)}, f32[2,2,96,512]{3,2,1,0:T(8,128)S(1)}, bf16[2,2,64,512]{3,2,1,0:T(8,128)(2,1)}, bf16[2,2,16,512]{3,2,1,0:T(8,128)(2,1)}, f32[128,128]{1,0:T(8,128)S(1)}) custom-call(s32[1]{0:T(128)} %bitcast.21.first_ref, s32[2]{0:T(128)S(1)} %pad_add_fusion.1.lens_ref, ...), custom_call_target="tpu_custom_call" | custom-call | tf_op jit(solution)/shard_map/attend_back/pallas_call | solution.py:406
  414.1 4.5 collective-permute-start.28
  420.9 4.1 collective-permute-done.27
  432.5 18.5 %all_gather.27 = bf16[384,1024]{1,0:T(8,128)(2,1)S(1)} all-gather(bf16[96,1024]{1,0:T(8,128)(2,1)S(1)} %get-tuple-element.183), channel_id=1, replica_groups=mesh['row'=2,'core'=2,'ctx'=2,'tp'=4] {'tp'}, dimensions={0}, use_global_device_ids=true | all-gather | bytes 983040 | tf_op jit(solution)/shard_map/all_gather | solution.py:170
  454.7 4.0 all-to-all-start.7
  460.6 3.8 all-to-all-done.7
  464.4 3.6 all-to-all-start.3
  477.2 11.0 %all-to-all-done.3 = bf16[4,96,1024]{2,1,0:T(8,128)(2,1)S(1)} async-done(((bf16[4,96,1024]{2,1,0:T(8,128)(2,1)}), bf16[4,96,1024]{2,1,0:T(8,128)(2,1)S(1)}, u32[]{:S(2)}, u32[]{:S(2)}) %all-to-all-start.3) | async-done | bytes 786464 | tf_op jit(solution)/shard_map/all_to_all | solution.py:178
  494.5 4.0 all-to-all-done.4
  498.6 3.7 all-to-all-start.8
  523.9 14.6 %all-to-all-done.8 = bf16[4,256,1536]{2,1,0:T(8,128)(2,1)S(1)} async-done(((bf16[4,256,1536]{2,1,0:T(8,128)(2,1)}), bf16[4,256,1536]{2,1,0:T(8,128)(2,1)S(1)}, u32[]{:S(2)}, u32[]{:S(2)}) %all-to-all-start.8) | async-done | bytes 3145760 | tf_op jit(solution)/shard_map/all_to_all | solution.py:226
  538.5 4.9 all-to-all-start.5
  562.1 30.1 %all-to-all-done.5 = bf16[4,256,2048]{2,1,0:T(8,128)(2,1)} async-done(((bf16[4,256,2048]{2,1,0:T(8,128)(2,1)}), bf16[4,256,2048]{2,1,0:T(8,128)(2,1)}, u32[]{:S(2)}, u32[]{:S(2)}) %all-to-all-start.5) | async-done | bytes 4194336 | tf_op jit(solution)/shard_map/all_to_all | solution.py:226
  597.2 25.0 %all-reduce.37 = (f32[1280]{0:T(1024)S(1)}, f32[4808]{0:T(1024)S(1)}) all-reduce(f32[1280]{0:T(1024)S(1)} %reduce_sum.775, f32[4808]{0:T(1024)S(1)} %reduce_sum.811), channel_id=1, replica_groups=mesh['row'=2,'core'=2,'ctx'=2,'tp'=4] {'tp'}, use_global_device_ids=true, to_apply=%region_41.42 | all-reduce | flops 6088 | bytes 48704 | tf_op jit(solution)/shard_map/psum | solution.py:699
  631.1 3.7 all-to-all-start.6
  647.0 9.3 %all-to-all-done.6 = bf16[4,256,512]{2,1,0:T(8,128)(2,1)S(1)} async-done(((bf16[4,256,512]{2,1,0:T(8,128)(2,1)}), bf16[4,256,512]{2,1,0:T(8,128)(2,1)S(1)}, u32[]{:S(2)}, u32[]{:S(2)}) %all-to-all-start.6) | async-done | bytes 1048608 | tf_op jit(solution)/shard_map/all_to_all | solution.py:229
  (1056 shorter events, 287.9 us)
Async XLA Ops:
  7.2 126.8 %all-gather.6.cloned.1.call-start = ((), (), s32[]{:S(2)}) async-start(), calls=%async_computation.13 | async-start | bytes 3342336 | tf_op jit(solution)/shard_map/all_gather | solution.py:211
  12.4 169.5 %all-gather.4.cloned.1.call-start = ((), (), s32[]{:S(2)}) async-start(), calls=%async_computation.12 | async-start | bytes 4456448 | tf_op jit(solution)/shard_map/all_gather | solution.py:211
  16.2 246.7 %all-gather.8.cloned.1.call-start = ((), (), s32[]{:S(2)}) async-start(), calls=%async_computation.14 | async-start | bytes 4718592 | tf_op jit(solution)/shard_map/all_gather | solution.py:541
  16.2 30.8 %collective-permute-start.9 = (s32[1]{0:T(128)}, s32[1]{0:T(128)}, u32[]{:S(2)}, u32[]{:S(2)}) collective-permute-start(s32[1]{0:T(128)} %param.20), channel_id=1, source_target_pairs={{0,8},{8,0},{1,9},{9,1},{2,10},{10,2},{3,11},{11,3},{4,12},{12,4},... | collective-permute-start | bytes 20 | tf_op jit(solution)/shard_map/ppermute | solution.py:160
  17.0 30.6 %collective-permute-start = (bf16[1,2920]{1,0:T(2,128)(2,1)S(1)}, bf16[1,2920]{1,0:T(2,128)(2,1)S(1)}, u32[]{:S(2)}, u32[]{:S(2)}) collective-permute-start(bf16[1,2920]{1,0:T(2,128)(2,1)S(1)} %broadcast_in_dim.10), channel_id=1, source_target_pairs={{0,8},{8,0},{1,9},{9,1},{2,10},{10,2},{3,11},{11,3},{4,12},{12,4},... | collective-permute-start | bytes 17528 | tf_op jit(solution)/shard_map/ppermute | solution.py:67
  17.3 46.4 %collective-permute-start.3 = (bf16[1,128,1024]{2,1,0:T(8,128)(2,1)S(1)}, bf16[1,128,1024]{2,1,0:T(8,128)(2,1)S(1)}, u32[]{:S(2)}, u32[]{:S(2)}) collective-permute-start(bf16[1,128,1024]{2,1,0:T(8,128)(2,1)S(1)} %bitcast.377), channel_id=1, source_target_pairs={{0,16},{16,0},{1,17},{17,1},{2,18},{18,2},{3,19},{19,3},{4,20},{20... | collective-permute-start | bytes 786440 | tf_op jit(solution)/shard_map/ppermute | solution.py:67
  20.1 47.1 %collective-permute-start.6 = (bf16[1,128,1024]{2,1,0:T(8,128)(2,1)S(1)}, bf16[1,128,1024]{2,1,0:T(8,128)(2,1)S(1)}, u32[]{:S(2)}, u32[]{:S(2)}) collective-permute-start(bf16[1,128,1024]{2,1,0:T(8,128)(2,1)S(1)} %bitcast.381), channel_id=1, source_target_pairs={{0,4},{4,0},{1,5},{5,1},{2,6},{6,2},{3,7},{7,3},{8,12},{12,8},{9,1... | collective-permute-start | bytes 786440 | tf_op jit(solution)/shard_map/ppermute | solution.py:67
  61.5 31.1 %collective-permute-start.18 = (bf16[1,33,128]{2,1,0:T(8,128)(2,1)}, bf16[1,33,128]{2,1,0:T(8,128)(2,1)S(1)}, u32[]{:S(2)}, u32[]{:S(2)}) collective-permute-start(bf16[1,33,128]{2,1,0:T(8,128)(2,1)} %maximum_select_fusion), channel_id=1, source_target_pairs={{0,1},{1,0},{2,3},{3,2},{4,5},{5,4},{6,7},{7,6},{8,9},{9,8},{10,11... | collective-permute-start | bytes 25352 | tf_op jit(solution)/shard_map/ppermute | solution.py:67
  64.9 22.3 %collective-permute-start.4 = (bf16[2,128,1024]{2,1,0:T(8,128)(2,1)}, bf16[2,128,1024]{2,1,0:T(8,128)(2,1)S(1)}, u32[]{:S(2)}, u32[]{:S(2)}) collective-permute-start(bf16[2,128,1024]{2,1,0:T(8,128)(2,1)} %pad_maximum_fusion.9), channel_id=1, source_target_pairs={{0,4},{4,0},{1,5},{5,1},{2,6},{6,2},{3,7},{7,3},{8,12},{12,8},{9,1... | collective-permute-start | bytes 1572872 | tf_op jit(solution)/shard_map/ppermute | solution.py:67
  69.0 20.4 %collective-permute-start.7 = (bf16[2,128,1024]{2,1,0:T(8,128)(2,1)}, bf16[2,128,1024]{2,1,0:T(8,128)(2,1)S(1)}, u32[]{:S(2)}, u32[]{:S(2)}) collective-permute-start(bf16[2,128,1024]{2,1,0:T(8,128)(2,1)} %pad_maximum_fusion.10), channel_id=1, source_target_pairs={{0,16},{16,0},{1,17},{17,1},{2,18},{18,2},{3,19},{19,3},{4,20},{20... | collective-permute-start | bytes 1572872 | tf_op jit(solution)/shard_map/ppermute | solution.py:67
  93.3 12.9 %collective-permute-start.19 = (bf16[2,33,128]{2,1,0:T(8,128)(2,1)S(1)}, bf16[2,33,128]{2,1,0:T(8,128)(2,1)S(1)}, u32[]{:S(2)}, u32[]{:S(2)}) collective-permute-start(bf16[2,33,128]{2,1,0:T(8,128)(2,1)S(1)} %pad_maximum_fusion.37), channel_id=1, source_target_pairs={{0,2},{1,3},{2,0},{3,1},{4,6},{5,7},{6,4},{7,5},{8,10},{9,11},{10,... | collective-permute-start | bytes 50696 | tf_op jit(solution)/shard_map/ppermute | solution.py:67
  102.4 29.5 %all-to-all-start = ((bf16[4,96,1024]{2,1,0:T(8,128)(2,1)}), bf16[4,96,1024]{2,1,0:T(8,128)(2,1)S(1)}, u32[]{:S(2)}, u32[]{:S(2)}) async-start(bf16[4,96,1024]{2,1,0:T(8,128)(2,1)} %bitcast.20), calls=%async_computation | async-start | bytes 1572864 | tf_op jit(solution)/shard_map/all_to_all | solution.py:178
  133.9 60.7 %collective-permute-start.10 = (bf16[96,1024]{1,0:T(8,128)(2,1)S(1)}, bf16[96,1024]{1,0:T(8,128)(2,1)S(1)}, u32[]{:S(2)}, u32[]{:S(2)}) collective-permute-start(bf16[96,1024]{1,0:T(8,128)(2,1)S(1)} %add_convert_fusion.4), channel_id=1, source_target_pairs={{0,8},{8,0},{1,9},{9,1},{2,10},{10,2},{3,11},{11,3},{4,12},{12,4},... | collective-permute-start | bytes 589832 | tf_op jit(solution)/shard_map/ppermute | solution.py:160
  196.5 12.9 %collective-permute-start.12 = (bf16[2,64,1024]{2,1,0:T(8,128)(2,1)S(1)}, bf16[2,64,1024]{2,1,0:T(8,128)(2,1)S(1)}, u32[]{:S(2)}, u32[]{:S(2)}) collective-permute-start(bf16[2,64,1024]{2,1,0:T(8,128)(2,1)S(1)} %slice.1544), channel_id=1, source_target_pairs={{0,1},{1,2},{2,3},{3,4},{4,5},{5,6},{6,7},{8,9},{9,10},{10,11},{11... | collective-permute-start | bytes 786440 | tf_op jit(solution)/shard_map/ppermute | solution.py:166
  267.8 23.3 %all-to-all-start.1 = ((bf16[4,96,1024]{2,1,0:T(8,128)(2,1)}), bf16[4,96,1024]{2,1,0:T(8,128)(2,1)}, u32[]{:S(2)}, u32[]{:S(2)}) async-start(bf16[4,96,1024]{2,1,0:T(8,128)(2,1)} %bitcast.423), calls=%async_computation.1 | async-start | bytes 1572864 | tf_op jit(solution)/shard_map/all_to_all | solution.py:178
  319.0 21.3 %all-to-all-start.2 = ((bf16[4,96,1024]{2,1,0:T(8,128)(2,1)}), bf16[4,96,1024]{2,1,0:T(8,128)(2,1)}, u32[]{:S(2)}, u32[]{:S(2)}) async-start(bf16[4,96,1024]{2,1,0:T(8,128)(2,1)} %bitcast.422), calls=%async_computation.2 | async-start | bytes 1572864 | tf_op jit(solution)/shard_map/all_to_all | solution.py:178
  340.4 48.1 %all-to-all-start.11 = ((bf16[8,128,1024]{2,1,0:T(8,128)(2,1)}), bf16[8,128,1024]{2,1,0:T(8,128)(2,1)}, u32[]{:S(2)}, u32[]{:S(2)}) async-start(bf16[8,128,1024]{2,1,0:T(8,128)(2,1)} %bitcast.391), calls=%async_computation.11 | async-start | bytes 4194304 | tf_op jit(solution)/shard_map/all_to_all | solution.py:448
  360.6 10.5 %collective-permute-start.24 = (f32[2,30,512]{2,1,0:T(8,128)}, f32[2,30,512]{2,1,0:T(8,128)}, u32[]{:S(2)}, u32[]{:S(2)}) collective-permute-start(f32[2,30,512]{2,1,0:T(8,128)} %slice.1676), channel_id=1, source_target_pairs={{1,0},{2,1},{3,2},{4,3},{5,4},{6,5},{7,6},{9,8},{10,9},{11,10},{12... | collective-permute-start | bytes 368648 | tf_op jit(solution)/shard_map/ppermute | solution.py:166
  376.0 10.8 %collective-permute-start.25 = (bf16[96,1024]{1,0:T(8,128)(2,1)S(1)}, bf16[96,1024]{1,0:T(8,128)(2,1)S(1)}, u32[]{:S(2)}, u32[]{:S(2)}) collective-permute-start(bf16[96,1024]{1,0:T(8,128)(2,1)S(1)} %slice.2500), channel_id=1, source_target_pairs={{0,8},{8,0},{1,9},{9,1},{2,10},{10,2},{3,11},{11,3},{4,12},{12,4},... | collective-permute-start | bytes 589832 | tf_op jit(solution)/shard_map/ppermute | solution.py:160
  388.5 66.2 %all-to-all-start.10 = ((bf16[8,128,1024]{2,1,0:T(8,128)(2,1)}), bf16[8,128,1024]{2,1,0:T(8,128)(2,1)}, u32[]{:S(2)}, u32[]{:S(2)}) async-start(bf16[8,128,1024]{2,1,0:T(8,128)(2,1)} %bitcast.390), calls=%async_computation.10 | async-start | bytes 4194304 | tf_op jit(solution)/shard_map/all_to_all | solution.py:448
  412.7 12.3 %collective-permute-start.27 = (bf16[2,2,64,512]{3,2,1,0:T(8,128)(2,1)}, bf16[2,2,64,512]{3,2,1,0:T(8,128)(2,1)S(1)}, u32[]{:S(2)}, u32[]{:S(2)}) collective-permute-start(bf16[2,2,64,512]{3,2,1,0:T(8,128)(2,1)} %get-tuple-element.28), channel_id=1, source_target_pairs={{1,0},{2,1},{3,2},{4,3},{5,4},{6,5},{7,6},{9,8},{10,9},{11,10},{12... | collective-permute-start | bytes 786440 | tf_op jit(solution)/shard_map/ppermute | solution.py:166
  454.7 9.7 %all-to-all-start.7 = ((f32[8,1,4808]{2,1,0:T(1,128)}), f32[8,1,4808]{2,1,0:T(1,128)S(1)}, u32[]{:S(2)}, u32[]{:S(2)}) async-start(f32[8,1,4808]{2,1,0:T(1,128)} %copy.100), calls=%async_computation.7 | async-start | bytes 311296 | tf_op jit(solution)/shard_map/all_to_all | solution.py:453
  464.4 23.8 %all-to-all-start.3 = ((bf16[4,96,1024]{2,1,0:T(8,128)(2,1)}), bf16[4,96,1024]{2,1,0:T(8,128)(2,1)S(1)}, u32[]{:S(2)}, u32[]{:S(2)}) async-start(bf16[4,96,1024]{2,1,0:T(8,128)(2,1)} %bitcast.90), calls=%async_computation.3 | async-start | bytes 1572864 | tf_op jit(solution)/shard_map/all_to_all | solution.py:178
  498.6 39.9 %all-to-all-start.8 = ((bf16[4,256,1536]{2,1,0:T(8,128)(2,1)}), bf16[4,256,1536]{2,1,0:T(8,128)(2,1)S(1)}, u32[]{:S(2)}, u32[]{:S(2)}) async-start(bf16[4,256,1536]{2,1,0:T(8,128)(2,1)} %constant_dynamic-update-slice_fusion.155), calls=%async_computation.8 | async-start | bytes 6291456 | tf_op jit(solution)/shard_map/all_to_all | solution.py:226
  514.9 28.5 %collective-permute-start.33 = (bf16[4,128,1024]{2,1,0:T(8,128)(2,1)}, bf16[4,128,1024]{2,1,0:T(8,128)(2,1)}, u32[]{:S(2)}, u32[]{:S(2)}) collective-permute-start(bf16[4,128,1024]{2,1,0:T(8,128)(2,1)} %bitcast.96), channel_id=1, source_target_pairs={{0,8},{8,0},{1,9},{9,1},{2,10},{10,2},{3,11},{11,3},{4,12},{12,4},... | collective-permute-start | bytes 3145736 | tf_op jit(solution)/shard_map/ppermute | solution.py:67
  517.9 30.7 %collective-permute-start.30 = (bf16[4,128,1024]{2,1,0:T(8,128)(2,1)}, bf16[4,128,1024]{2,1,0:T(8,128)(2,1)}, u32[]{:S(2)}, u32[]{:S(2)}) collective-permute-start(bf16[4,128,1024]{2,1,0:T(8,128)(2,1)} %bitcast.93), channel_id=1, source_target_pairs={{0,8},{8,0},{1,9},{9,1},{2,10},{10,2},{3,11},{11,3},{4,12},{12,4},... | collective-permute-start | bytes 3145736 | tf_op jit(solution)/shard_map/ppermute | solution.py:67
  538.5 53.7 %all-to-all-start.5 = ((bf16[4,256,2048]{2,1,0:T(8,128)(2,1)}), bf16[4,256,2048]{2,1,0:T(8,128)(2,1)}, u32[]{:S(2)}, u32[]{:S(2)}) async-start(bf16[4,256,2048]{2,1,0:T(8,128)(2,1)} %constant_dynamic-update-slice_fusion.106), calls=%async_computation.5 | async-start | bytes 8388608 | tf_op jit(solution)/shard_map/all_to_all | solution.py:226
  546.7 76.3 %collective-permute-start.34 = (bf16[2,128,1024]{2,1,0:T(8,128)(2,1)}, bf16[2,128,1024]{2,1,0:T(8,128)(2,1)}, u32[]{:S(2)}, u32[]{:S(2)}) collective-permute-start(bf16[2,128,1024]{2,1,0:T(8,128)(2,1)} %slice.2495), channel_id=1, source_target_pairs={{0,16},{16,0},{1,17},{17,1},{2,18},{18,2},{3,19},{19,3},{4,20},{20... | collective-permute-start | bytes 1572872 | tf_op jit(solution)/shard_map/ppermute | solution.py:67
  552.6 82.1 %collective-permute-start.31 = (bf16[2,128,1024]{2,1,0:T(8,128)(2,1)}, bf16[2,128,1024]{2,1,0:T(8,128)(2,1)}, u32[]{:S(2)}, u32[]{:S(2)}) collective-permute-start(bf16[2,128,1024]{2,1,0:T(8,128)(2,1)} %slice.2496), channel_id=1, source_target_pairs={{0,4},{4,0},{1,5},{5,1},{2,6},{6,2},{3,7},{7,3},{8,12},{12,8},{9,1... | collective-permute-start | bytes 1572872 | tf_op jit(solution)/shard_map/ppermute | solution.py:67
  592.2 38.0 %all-to-all-start.9 = ((bf16[4,256,384]{2,1,0:T(8,128)(2,1)}), bf16[4,256,384]{2,1,0:T(8,128)(2,1)S(1)}, u32[]{:S(2)}, u32[]{:S(2)}) async-start(bf16[4,256,384]{2,1,0:T(8,128)(2,1)} %pad_maximum_fusion.7), calls=%async_computation.9 | async-start | bytes 1572864 | tf_op jit(solution)/shard_map/all_to_all | solution.py:229
  625.3 14.2 %collective-permute-start.35 = (bf16[1,128,1024]{2,1,0:T(8,128)(2,1)}, bf16[1,128,1024]{2,1,0:T(8,128)(2,1)S(1)}, u32[]{:S(2)}, u32[]{:S(2)}) collective-permute-start(bf16[1,128,1024]{2,1,0:T(8,128)(2,1)} %slice.2497), channel_id=1, source_target_pairs={{0,4},{4,0},{1,5},{5,1},{2,6},{6,2},{3,7},{7,3},{8,12},{12,8},{9,1... | collective-permute-start | bytes 786440 | tf_op jit(solution)/shard_map/ppermute | solution.py:67
  631.1 25.2 %all-to-all-start.6 = ((bf16[4,256,512]{2,1,0:T(8,128)(2,1)}), bf16[4,256,512]{2,1,0:T(8,128)(2,1)S(1)}, u32[]{:S(2)}, u32[]{:S(2)}) async-start(bf16[4,256,512]{2,1,0:T(8,128)(2,1)} %pad_maximum_fusion.6), calls=%async_computation.6 | async-start | bytes 2097152 | tf_op jit(solution)/shard_map/all_to_all | solution.py:229
  (286 other events, 1739.6 us)
Sparse Core Ops, SparseCore 0:
  12.6 83.2 all-gather.5
  99.2 82.7 all-gather.3
  184.4 35.5 all-gather.7

commit v3 on v2

v3 whole, which is shorter than its diff:
```python
import functools

import jax
import jax.numpy as jnp
from jax import lax
from jax.experimental import pallas as pl
from jax.experimental.pallas import tpu as pltpu
from jax.sharding import Mesh
from jax.sharding import PartitionSpec as P

D = 1024
HD = 64
KERNEL = 31
LEFT = 64
RIGHT = 16
SPAN = 73
PAIR = 128
KEYS = 256
EPSILON = 1e-05
MASKED = -1e30
SCALE = HD**-0.5
F32 = jnp.float32
BF16 = jnp.bfloat16


def product(left, right):
    return jnp.dot(left, right, preferred_element_type=F32)


def product_nt(left, right):
    return lax.dot_general(left, right, (((1,), (1,)), ((), ())), preferred_element_type=F32)


def product_tn(left, right):
    return lax.dot_general(left, right, (((0,), (0,)), ((), ())), preferred_element_type=F32)


def silu_slope(values):
    logistic = jax.nn.sigmoid(values)
    return logistic * (1.0 + values * (1.0 - logistic))


def bits_of(axis):
    count = lax.axis_size(axis)
    return [1 << k for k in range(count.bit_length() - 1)]


def stream_places():
    rows, ctxs = lax.axis_size("row"), lax.axis_size("ctx")
    return [(0, b, a) for b in range(ctxs) for a in range(rows)] + [
        (1, b, a) for a in range(rows) for b in range(ctxs)
    ]


def ffn_places(core, kind):
    rows, ctxs = lax.axis_size("row"), lax.axis_size("ctx")
    if kind == "in":
        return [(e ^ core, b, a) for e in range(2) for b in range(ctxs) for a in range(rows)]
    return [(e ^ core, b, a) for e in range(2) for a in range(rows) for b in range(ctxs)]


def reorder(value, source, target):
    width = value.shape[-1] // len(source)
    where = {place: k for k, place in enumerate(source)}
    return jnp.concatenate(
        [value[..., where[p] * width : (where[p] + 1) * width] for p in target], -1
    )


def to_ffn(value, kind, second):
    source = stream_places()
    return jnp.where(
        second,
        reorder(value, source, ffn_places(1, kind)),
        reorder(value, source, ffn_places(0, kind)),
    )


def from_ffn(value, kind, second):
    target = stream_places()
    return jnp.where(
        second,
        reorder(value, ffn_places(1, kind), target),
        reorder(value, ffn_places(0, kind), target),
    )


def crossed(blocks):
    rows = lax.axis_size("row")
    flags = [((lax.axis_index("row") & m) != 0, m) for m in bits_of("row")]
    flags += [((lax.axis_index("ctx") & m) != 0, m * rows) for m in bits_of("ctx")]
    for flag, mask in flags:
        blocks = [jnp.where(flag, blocks[i ^ mask], blocks[i]) for i in range(len(blocks))]
    return blocks


def natural_places():
    rows, ctxs = lax.axis_size("row"), lax.axis_size("ctx")
    return [(c, b, a) for a in range(rows) for c in range(2) for b in range(ctxs)]


def from_natural(value):
    rows, ctxs = lax.axis_size("row"), lax.axis_size("ctx")
    grid = [(c, b, a) for c in range(2) for b in range(ctxs) for a in range(rows)]
    value = reorder(value, natural_places(), grid)
    width = value.shape[-1] // len(grid)
    blocks = [value[..., k * width : (k + 1) * width] for k in range(len(grid))]
    half = len(grid) // 2
    value = jnp.concatenate(crossed(blocks[:half]) + crossed(blocks[half:]), -1)
    return reorder(value, grid, stream_places())


def to_natural(value):
    rows, ctxs = lax.axis_size("row"), lax.axis_size("ctx")
    grid = [(c, b, a) for c in range(2) for b in range(ctxs) for a in range(rows)]
    value = reorder(value, stream_places(), grid)
    width = value.shape[-1] // len(grid)
    blocks = [value[..., k * width : (k + 1) * width] for k in range(len(grid))]
    half = len(grid) // 2
    value = jnp.concatenate(crossed(blocks[:half]) + crossed(blocks[half:]), -1)
    return reorder(value, grid, natural_places())


def partner(value, axis, mask):
    count = lax.axis_size(axis)
    return lax.ppermute(value, axis, [(i, i ^ mask) for i in range(count)])


def swap_core(value):
    return partner(value, "core", 1)


def stages_of(axes):
    return [(axis, mask) for axis in axes for mask in bits_of(axis)]


def cube_pair(value, axes):
    value = value[None]
    stages = stages_of(axes)
    for axis, mask in stages[:-1]:
        value = jnp.concatenate([value, partner(value, axis, mask)], 0)
    return value, partner(value, *stages[-1])


def cube_settle(near, far, axes):
    stages = stages_of(axes)[::-1]
    total = near.astype(F32) + partner(far, *stages[0]).astype(F32)
    for axis, mask in stages[1:]:
        half = total.shape[0] // 2
        arrived = partner(total[half:].astype(BF16), axis, mask)
        total = total[:half] + arrived.astype(F32)
    return total[0]


def ffn_weight(weight, axes):
    near, far = cube_pair(weight, axes)
    return [near, far, swap_core(near), swap_core(far)]


def ffn_settle(chunks, axes):
    near = chunks[0].astype(F32) + swap_core(chunks[2]).astype(F32)
    far = chunks[1].astype(F32) + swap_core(chunks[3]).astype(F32)
    return cube_settle(near, far.astype(BF16), axes)


A_AXES = ("row", "ctx")
B_AXES = ("ctx", "row")


def tp_joined(own, arrived, mask, axis):
    upper = (lax.axis_index("tp") & mask) != 0
    return jnp.concatenate(
        [jnp.where(upper, arrived, own), jnp.where(upper, own, arrived)], axis
    )


def tp_halves(value, mask, axis):
    upper = (lax.axis_index("tp") & mask) != 0
    half = value.shape[axis] // 2
    low = lax.slice_in_dim(value, 0, half, axis=axis)
    high = lax.slice_in_dim(value, half, 2 * half, axis=axis)
    return jnp.where(upper, high, low), jnp.where(upper, low, high)


def core_shares(matrices, second):
    halves = jnp.concatenate(
        [m.reshape(m.shape[0], 2, 1, m.shape[1] // 2) for m in matrices], 2
    )
    own, other = halves[:, 0], halves[:, 1]
    own, other = jnp.where(second, other, own), jnp.where(second, own, other)
    own = own.reshape(own.shape[0], -1)
    other = swap_core(other.reshape(own.shape))
    value = jnp.stack([jnp.where(second, other, own), jnp.where(second, own, other)], 0)[:, None]
    for mask in bits_of("tp"):
        value = tp_joined(value, partner(value, "tp", mask), mask, 1)
    return value


def core_weight(value):
    return [*cube_pair(value[0], A_AXES), *cube_pair(value[1], B_AXES)]


def core_settle(chunks, second, count):
    total = jnp.stack(
        [
            cube_settle(chunks[0], chunks[1], A_AXES),
            cube_settle(chunks[2], chunks[3], B_AXES),
        ],
        0,
    )
    for mask in bits_of("tp")[::-1]:
        kept, sent = tp_halves(total, mask, 1)
        total = kept + partner(sent.astype(BF16), "tp", mask).astype(F32)
    total = total[:, 0]
    own = jnp.where(second, total[1], total[0])
    other = swap_core(jnp.where(second, total[0], total[1]).astype(BF16)).astype(F32)
    own = own.reshape(own.shape[0], count, -1)
    other = other.reshape(own.shape)
    whole = jnp.concatenate(
        [jnp.where(second, other, own), jnp.where(second, own, other)], 2
    )
    return [whole[:, m] for m in range(count)]


def along(value, step):
    count = lax.axis_size("ctx") * lax.axis_size("tp")
    pairs = [(i, i + step) for i in range(count) if 0 <= i + step < count]
    return lax.ppermute(value, ("ctx", "tp"), pairs)


def widen_tp(rows):
    return lax.all_gather(rows, "tp", axis=0, tiled=True)


def widen_early(rows):
    count = lax.axis_size("tp")
    index = lax.axis_index("tp")
    parts = [rows] + [
        lax.ppermute(rows, "tp", [(i, i ^ k) for i in range(count)]) for k in range(1, count)
    ]
    for mask in bits_of("tp"):
        flag = (index & mask) != 0
        parts = [jnp.where(flag, parts[k ^ mask], parts[k]) for k in range(count)]
    return jnp.concatenate(parts, 0)


def exchange_tp(partial_value):
    count = lax.axis_size("tp")
    pieces = partial_value.reshape(
        count, partial_value.shape[0] // count, partial_value.shape[1]
    )
    return lax.all_to_all(pieces, "tp", 0, 0)


def widen_core(rows):
    return jnp.concatenate([rows, swap_core(rows)], 0)


def exchange_core(partial_value):
    half = partial_value.shape[0] // 2
    return [partial_value[:half], swap_core(partial_value[half:])]


PARAMS = pltpu.CompilerParams(vmem_limit_bytes=48 << 20)
VMEM = pl.BlockSpec(memory_space=pltpu.VMEM)
SMEM = pl.BlockSpec(memory_space=pltpu.SMEM)


def run(kernel, name, outs, *args, smem=0, scratch=()):
    return pl.pallas_call(
        kernel,
        in_specs=[SMEM] * smem + [VMEM] * (len(args) - smem),
        out_specs=[VMEM] * len(outs),
        out_shape=[jax.ShapeDtypeStruct(shape, dtype) for shape, dtype in outs],
        scratch_shapes=list(scratch),
        compiler_params=PARAMS,
        name=name,
    )(*args)


def stacked(refs):
    return jnp.concatenate([r[...].reshape(-1, r.shape[-1]) for r in refs], 0)


def heads_of(refs, start, stop):
    return jnp.concatenate(
        [
            jnp.concatenate(
                [r[:, z, :, start:stop].reshape(-1, stop - start) for r in refs], 0
            )
            for z in range(refs[0].shape[1])
        ],
        1,
    )


def block_order(value, source, target, width):
    where = {place: k for k, place in enumerate(source)}
    return jnp.concatenate(
        [value[:, where[p] * width : (where[p] + 1) * width] for p in target], 1
    )


def by_core(value, kind, second, inverse=False):
    places, width = stream_places(), D // len(stream_places())
    options = []
    for core in range(2):
        other = ffn_places(core, kind)
        options.append(
            block_order(value, other, places, width)
            if inverse
            else block_order(value, places, other, width)
        )
    return jnp.where(second, options[1], options[0])


def normal_of(stream):
    centre = stream - jnp.mean(stream, axis=-1, keepdims=True)
    inverse = lax.rsqrt(jnp.mean(centre * centre, axis=-1, keepdims=True) + EPSILON)
    return centre * inverse, inverse


def summed(refs):
    total = None
    for ref in refs:
        value = ref[...].astype(F32)
        value = jnp.sum(value, axis=0) if value.ndim == 3 else value
        total = value if total is None else total + value
    return total


def back_through(upstream, normal, inverse, gain, grads_ref):
    scaled = upstream * gain
    grads_ref[0:1] = jnp.sum(upstream * normal, axis=0, keepdims=True)
    grads_ref[1:2] = jnp.sum(upstream, axis=0, keepdims=True)
    return inverse * (
        scaled
        - jnp.mean(scaled, axis=-1, keepdims=True)
        - normal * jnp.mean(scaled * normal, axis=-1, keepdims=True)
    )


def onward_kernel(count, scale, source, target, core_ref, *refs):
    pieces, stream_ref, norm_ref = refs[:count], refs[count], refs[count + 1]
    next_ref, hidden_ref = refs[count + 2 :]
    second = core_ref[0] == 1
    total = summed(pieces)
    if source:
        total = by_core(total, source, second, inverse=True)
    stream = stream_ref[...] + scale * total
    next_ref[...] = stream
    hidden = normal_of(stream)[0] * norm_ref[0:1] + norm_ref[1:2]
    if target:
        hidden = by_core(hidden, target, second)
    hidden_ref[...] = hidden.astype(BF16)


def onward(core, pieces, stream, norm, scale, source, target):
    return run(
        functools.partial(onward_kernel, len(pieces), scale, source, target),
        "onward",
        [(stream.shape, F32), (stream.shape, BF16)],
        core,
        *pieces,
        stream,
        norm,
        smem=1,
    )


def turn_kernel(count, core_ref, *refs):
    pieces, stream_ref, up_ref, norm_ref = refs[:count], *refs[count : count + 3]
    result_ref, back_ref, branch_ref, grads_ref = refs[count + 3 :]
    second = core_ref[0] == 1
    total = by_core(summed(pieces), "out", second, inverse=True)
    normal, inverse = normal_of(stream_ref[...] + 0.5 * total)
    result_ref[...] = (normal * norm_ref[0:1] + norm_ref[1:2]).astype(BF16)
    back = back_through(up_ref[...].astype(F32), normal, inverse, norm_ref[0:1], grads_ref)
    back_ref[...] = back
    branch_ref[...] = by_core(0.5 * back, "out", second).astype(BF16)


def turn(core, pieces, stream, upstream, norm):
    shape = stream.shape
    return run(
        functools.partial(turn_kernel, len(pieces)),
        "turn",
        [(shape, BF16), (shape, F32), (shape, BF16), ((2, D), F32)],
        core,
        *pieces,
        stream,
        upstream,
        norm,
        smem=1,
    )


def return_kernel(count, scale, source, target, core_ref, *refs):
    pieces, stream_ref, up_ref, norm_ref = refs[:count], *refs[count : count + 3]
    back_ref, branch_ref, grads_ref = refs[count + 3 :]
    second = core_ref[0] == 1
    total = summed(pieces)
    if source:
        total = by_core(total, source, second, inverse=True)
    normal, inverse = normal_of(stream_ref[...].astype(F32))
    back = up_ref[...] + back_through(total, normal, inverse, norm_ref[0:1], grads_ref)
    back_ref[...] = back
    branch = scale * back
    if target:
        branch = by_core(branch, target, second)
    branch_ref[...] = branch.astype(BF16)


def returning(core, pieces, stream, upstream, norm, scale, source, target):
    shape = stream.shape
    return run(
        functools.partial(return_kernel, len(pieces), scale, source, target),
        "returning",
        [(shape, F32), (shape, BF16), ((2, D), F32)],
        core,
        *pieces,
        stream,
        upstream,
        norm,
        smem=1,
    )


def first_kernel(wide_ref, norm_ref, *refs):
    hidden_ref = refs[8]
    hidden = normal_of(wide_ref[...].astype(F32))[0] * norm_ref[0:1] + norm_ref[1:2]
    hidden_ref[...] = hidden.astype(BF16)
    ffn_forward_kernel(hidden_ref, *refs[:8], *refs[9:])


def ffn_forward_kernel(rows_ref, *refs):
    ins, outs = refs[:4], refs[4:8]
    before_ref, active_ref, branch_ref = refs[8:]
    before = product(rows_ref[...], stacked(ins))
    before_ref[...] = before
    active = (before * jax.nn.sigmoid(before)).astype(BF16)
    active_ref[...] = active
    branch_ref[...] = product_nt(active, stacked(outs)).astype(BF16)


def ffn_outs(height, width):
    return [((height, width), F32), ((height, width), BF16), ((height, D), BF16)]


def ffn_first(wide, norm, ins, outs):
    height, width = wide.shape[0], ins[0].shape[-1]
    return run(
        first_kernel, "ffn_first", [((height, D), BF16), *ffn_outs(height, width)],
        wide, norm, *ins, *outs,
    )


def ffn_forward(hidden, ins, outs):
    height, width = hidden.shape[0], ins[0].shape[-1]
    return run(
        ffn_forward_kernel, "ffn_forward", ffn_outs(height, width), hidden, *ins, *outs
    )


def ffn_backward_kernel(rows_ref, before_ref, *refs):
    ins, outs = refs[:4], refs[4:8]
    d_before_ref, branch_ref = refs[8:]
    d_active = product(rows_ref[...], stacked(outs))
    d_before = (d_active * silu_slope(before_ref[...])).astype(BF16)
    d_before_ref[...] = d_before
    branch_ref[...] = product_nt(d_before, stacked(ins)).astype(BF16)


def ffn_backward(upstream, before, ins, outs):
    height, width = before.shape
    return run(
        ffn_backward_kernel, "ffn_backward", [((height, width), BF16), ((height, D), BF16)],
        upstream, before, *ins, *outs,
    )


def scatter_rows(value, refs):
    rows = value.shape[0] // len(refs)
    for j, ref in enumerate(refs):
        ref[...] = value[j * rows : (j + 1) * rows].reshape(ref.shape)


def ffn_grads_kernel(hidden_ref, d_before_ref, up_ref, active_ref, *outs):
    scatter_rows(product_tn(hidden_ref[...], d_before_ref[...]).astype(BF16), outs[:4])
    scatter_rows(product_tn(up_ref[...], active_ref[...]).astype(BF16), outs[4:])


def ffn_grads(hidden, d_before, upstream, active, like):
    grads = run(
        ffn_grads_kernel, "ffn_grads", [(like.shape, BF16)] * 8,
        hidden, d_before, upstream, active,
    )
    return grads[:4], grads[4:]


def project_kernel(rows_ref, *refs):
    chunks, outs = refs[:4], refs[4:]
    value = product(rows_ref[...], heads_of(chunks, 0, 3 * PAIR)).astype(BF16)
    for z in range(chunks[0].shape[1]):
        for m in range(3):
            outs[m][:, z * PAIR : (z + 1) * PAIR] = value[
                :, (3 * z + m) * PAIR : (3 * z + m + 1) * PAIR
            ]


def project_heads(hidden, chunks):
    shape = (hidden.shape[0], chunks[0].shape[1] * PAIR)
    return run(project_kernel, "project_heads", [(shape, BF16)] * 3, hidden, *chunks)


def core_grads_kernel(count, hidden_ref, up_ref, *refs):
    values, last_ref, outs = refs[:count], refs[count], refs[count + 1 :]
    tp = outs[0].shape[1]
    grads = [product_tn(hidden_ref[...], v[...]).astype(BF16) for v in values]
    grads.append(product_tn(up_ref[...], last_ref[...]).astype(BF16))
    for m, grad in enumerate(grads):
        rows = D // len(outs)
        for j, ref in enumerate(outs):
            for z in range(tp):
                piece = grad[j * rows : (j + 1) * rows, z * PAIR : (z + 1) * PAIR]
                ref[:, z, :, m * PAIR : (m + 1) * PAIR] = piece.reshape(
                    ref.shape[0], ref.shape[2], PAIR
                )


def core_grads(hidden, upstream, values, last, like):
    return run(
        functools.partial(core_grads_kernel, len(values)), "core_grads",
        [(like.shape, BF16)] * 4, hidden, upstream, *values, last,
    )


def interleaved(values):
    tp = values[0].shape[1] // PAIR
    return jnp.concatenate(
        [v[:, z * PAIR : (z + 1) * PAIR] for z in range(tp) for v in values], 1
    )


def window(first, length, height):
    rows = lax.broadcasted_iota(jnp.int32, (height, KEYS), 0)
    lanes = lax.broadcasted_iota(jnp.int32, (height, KEYS), 1)
    offset = lanes - rows
    frame = lanes + (first - LEFT)
    in_band = (offset >= 0) & (offset < SPAN)
    allowed = in_band & (frame >= 0) & (frame < length)
    return in_band, allowed


def both(mask):
    return jnp.concatenate([mask, mask], 0)


def window_of(left_ref, own_ref, right_ref, clip, z, side, height):
    channels = own_ref.shape[1]
    lanes = slice(z * PAIR, (z + 1) * PAIR)
    far = slice(side * channels + z * PAIR, side * channels + (z + 1) * PAIR)
    return jnp.concatenate(
        [
            left_ref[clip, :, far],
            own_ref[clip * height : (clip + 1) * height, lanes],
            right_ref[clip, :, far],
            jnp.zeros((KEYS - LEFT - RIGHT - height, PAIR), BF16),
        ],
        0,
    )


def split_heads(value, odd):
    zero = jnp.zeros_like(value)
    return jnp.concatenate([jnp.where(odd, zero, value), jnp.where(odd, value, zero)], 0)


def merge_heads(value, odd):
    height = value.shape[0] // 2
    return jnp.where(odd, value[height:], value[:height])


def attend_kernel(
    height, first_ref, lens_ref, q_ref, k_ref, v_ref, left_ref, right_ref, rel_ref,
    c0, c1, c2, c3, context_ref, chance_ref, branch_ref
):
    odd = lax.broadcasted_iota(jnp.int32, (1, PAIR), 1) >= HD
    for clip in range(2):
        rows = slice(clip * height, (clip + 1) * height)
        in_band, allowed = window(first_ref[0], lens_ref[clip], height)
        in_band, allowed = both(in_band), both(allowed)
        for z in range(c0.shape[1]):
            lanes = slice(z * PAIR, (z + 1) * PAIR)
            query = split_heads(q_ref[rows, lanes], odd)
            keys = window_of(left_ref, k_ref, right_ref, clip, z, 0, height)
            values = window_of(left_ref, v_ref, right_ref, clip, z, 1, height)
            relative = product(query, rel_ref[...])
            relative = jnp.concatenate([relative, jnp.zeros((2 * height, KEYS - PAIR), F32)], 1)
            relative = jnp.concatenate(
                [
                    pltpu.roll(relative[:height], 0, 1, stride=1, stride_axis=0),
                    pltpu.roll(relative[height:], 0, 1, stride=1, stride_axis=0),
                ],
                0,
            )
            score = (product_nt(query, keys) + relative) * SCALE
            masked = jnp.where(allowed, score, MASKED)
            ceiling = jnp.max(masked, axis=-1, keepdims=True)
            raised = jnp.where(in_band, jnp.exp(masked - ceiling), 0.0)
            chance = raised * (1.0 / jnp.sum(raised, axis=-1, keepdims=True))
            chance_ref[clip, z] = chance
            context = merge_heads(product(chance.astype(BF16), values), odd)
            context_ref[rows, lanes] = context.astype(BF16)
    weight = heads_of((c0, c1, c2, c3), 3 * PAIR, 4 * PAIR)
    branch_ref[...] = product_nt(context_ref[...], weight).astype(BF16)


def attend(first, lens, heads, left, right, rel, chunks):
    height, channels, tp = heads[0].shape[0] // 2, heads[0].shape[1], chunks[0].shape[1]
    return run(
        functools.partial(attend_kernel, height),
        "attend",
        [
            ((2 * height, channels), BF16),
            ((2, tp, 2 * height, KEYS), F32),
            ((2 * height, D), BF16),
        ],
        first, lens, *heads, left, right, rel, *chunks,
        smem=2,
    )


def attend_back_kernel(
    height, first_ref, lens_ref, up_ref, q_ref, k_ref, v_ref, left_ref, right_ref, rel_ref,
    c0, c1, c2, c3, chance_ref, dq_ref, own_ref, d_left_ref, d_right_ref, table_ref
):
    odd = lax.broadcasted_iota(jnp.int32, (1, PAIR), 1) >= HD
    weight = heads_of((c0, c1, c2, c3), 3 * PAIR, 4 * PAIR)
    d_context = product(up_ref[...], weight).astype(BF16)
    table = jnp.zeros((PAIR, PAIR), F32)
    flip = (
        lax.broadcasted_iota(jnp.int32, (height, height), 0)
        + lax.broadcasted_iota(jnp.int32, (height, height), 1)
        == height - 1
    ).astype(BF16)
    for clip in range(2):
        rows = slice(clip * height, (clip + 1) * height)
        allowed = both(window(first_ref[0], lens_ref[clip], height)[1])
        for z in range(c0.shape[1]):
            lanes = slice(z * PAIR, (z + 1) * PAIR)
            query = split_heads(q_ref[rows, lanes], odd)
            upstream = split_heads(d_context[rows, lanes], odd)
            keys = window_of(left_ref, k_ref, right_ref, clip, z, 0, height)
            values = window_of(left_ref, v_ref, right_ref, clip, z, 1, height)
            chance = chance_ref[clip, z]
            d_chance = product_nt(upstream, values)
            inner = jnp.sum(d_chance * chance, axis=-1, keepdims=True)
            d_score = jnp.where(allowed, chance * (d_chance - inner), 0.0).astype(BF16)
            d_values = product_tn(chance.astype(BF16), upstream)
            d_keys = product_tn(d_score, query) * SCALE
            relative = []
            for head in range(2):
                turned_rows = product(flip, d_score[head * height : (head + 1) * height])
                rolled = pltpu.roll(
                    turned_rows, KEYS - height + 1, 1, stride=1, stride_axis=0
                )[:, :PAIR].astype(BF16)
                relative.append(product(flip, rolled).astype(BF16))
            relative = jnp.concatenate(relative, 0)
            d_query = product(d_score, keys) + product_nt(relative, rel_ref[...])
            dq_ref[rows, lanes] = (merge_heads(d_query, odd) * SCALE).astype(BF16)
            table += product_tn(query, relative)
            for slot, value in ((0, d_keys), (1, d_values)):
                d_left_ref[slot, clip, :, lanes] = value[:LEFT].astype(BF16)
                own_ref[slot, rows, lanes] = value[LEFT : LEFT + height]
                d_right_ref[slot, clip, :, lanes] = value[
                    LEFT + height : LEFT + height + RIGHT
                ].astype(BF16)
    table_ref[...] = table * SCALE


def attend_back(first, lens, upstream, heads, left, right, rel, chunks, chance):
    height, channels = heads[0].shape[0] // 2, heads[0].shape[1]
    return run(
        functools.partial(attend_back_kernel, height),
        "attend_back",
        [
            ((2 * height, channels), BF16),
            ((2, 2 * height, channels), F32),
            ((2, 2, LEFT, channels), BF16),
            ((2, 2, RIGHT, channels), BF16),
            ((PAIR, PAIR), F32),
        ],
        first, lens, upstream, *heads, left, right, rel, *chunks, chance,
        smem=2,
    )


def heads_in_kernel(height, dq_ref, own_ref, left_ref, right_ref, *refs):
    chunks, dk_ref, dv_ref, branch_ref = refs[:4], *refs[4:]
    for slot, out_ref in ((0, dk_ref), (1, dv_ref)):
        for clip in range(2):
            start = clip * height
            own = own_ref[slot, start : start + height]
            top = own[:RIGHT] + right_ref[slot, clip].astype(F32)
            own = jnp.concatenate([top, own[RIGHT:]], 0)
            low = own[height - LEFT :] + left_ref[slot, clip].astype(F32)
            own = jnp.concatenate([own[: height - LEFT], low], 0)
            out_ref[start : start + height] = own.astype(BF16)
    value = interleaved([dq_ref[...], dk_ref[...], dv_ref[...]])
    branch_ref[...] = product_nt(value, heads_of(chunks, 0, 3 * PAIR)).astype(BF16)


def heads_in(d_query, own, from_next, from_last, chunks):
    shape = d_query.shape
    return run(
        functools.partial(heads_in_kernel, shape[0] // 2), "heads_in",
        [(shape, BF16), (shape, BF16), ((shape[0], D), BF16)],
        d_query, own, from_next, from_last, *chunks,
    )


REACH = 32


def gate_kernel(rows_ref, live_ref, *refs):
    chunks, value_ref, logistic_ref, gated_ref = refs[:4], *refs[4:]
    value = product(rows_ref[...], heads_of(chunks, 0, 2 * PAIR))
    for z in range(chunks[0].shape[1]):
        lanes = slice(z * PAIR, (z + 1) * PAIR)
        linear = value[:, 2 * z * PAIR : (2 * z + 1) * PAIR]
        logistic = jax.nn.sigmoid(value[:, (2 * z + 1) * PAIR : (2 * z + 2) * PAIR])
        value_ref[:, lanes] = linear
        logistic_ref[:, lanes] = logistic
        gated_ref[:, lanes] = (linear * logistic * live_ref[...]).astype(BF16)


def gate_channels(hidden, live, chunks):
    shape = (hidden.shape[0], chunks[0].shape[1] * PAIR)
    return run(
        gate_kernel, "gate_channels", [(shape, F32), (shape, F32), (shape, BF16)],
        hidden, live, *chunks,
    )


def extend(earlier_ref, own_ref, wide, height):
    for clip in range(2):
        wide[clip, :REACH] = earlier_ref[clip].astype(F32)
        wide[clip, REACH : REACH + height] = own_ref[
            clip * height : (clip + 1) * height
        ].astype(F32)


def mix_kernel(height, gated_ref, earlier_ref, taps_ref, mixed_ref, sums_ref, wide):
    extend(earlier_ref, gated_ref, wide, height)
    lead = REACH - (KERNEL - 1)
    for clip in range(2):
        rows = slice(clip * height, (clip + 1) * height)
        first = second = jnp.zeros((height, 1), F32)
        for z in range(gated_ref.shape[1] // PAIR):
            lanes = slice(z * PAIR, (z + 1) * PAIR)
            mixed = wide[clip, lead : lead + height, lanes] * taps_ref[0:1, lanes]
            for j in range(1, KERNEL):
                mixed += wide[clip, lead + j : lead + j + height, lanes] * taps_ref[j : j + 1, lanes]
            mixed_ref[rows, lanes] = mixed
            first += jnp.sum(mixed, axis=1, keepdims=True)
            second += jnp.sum(mixed * mixed, axis=1, keepdims=True)
        sums_ref[rows] = jnp.concatenate([first, second], 1)


def mix_channels(gated, earlier, taps):
    height, channels = gated.shape[0] // 2, gated.shape[1]
    return run(
        functools.partial(mix_kernel, height), "mix_channels",
        [((2 * height, channels), F32), ((2 * height, 2), F32)],
        gated, earlier, taps,
        scratch=[pltpu.VMEM((2, height + REACH, channels), F32)],
    )


def paired(own_ref, other_ref):
    half = own_ref.shape[0] // 2
    other = other_ref[...]
    return (own_ref[...] + jnp.concatenate([other[half:], other[:half]], 0)) * (1.0 / D)


def conv_norm(mixed_ref, sums_ref, other_ref):
    means = paired(sums_ref, other_ref)
    centre, square = means[:, 0:1], means[:, 1:2]
    inverse = lax.rsqrt(square - centre * centre + EPSILON)
    return (mixed_ref[...] - centre) * inverse, inverse


def conv_out_kernel(mixed_ref, sums_ref, other_ref, affine_ref, *refs):
    chunks, active_ref, branch_ref = refs[:4], *refs[4:]
    normal, _ = conv_norm(mixed_ref, sums_ref, other_ref)
    levels = normal * affine_ref[0:1] + affine_ref[1:2]
    active = (levels * jax.nn.sigmoid(levels)).astype(BF16)
    active_ref[...] = active
    weight = heads_of(chunks, 2 * PAIR, 3 * PAIR)
    branch_ref[...] = product_nt(active, weight).astype(BF16)


def conv_forward(mixed, sums, other, affine, chunks):
    return run(
        conv_out_kernel, "conv_forward", [(mixed.shape, BF16), ((mixed.shape[0], D), BF16)],
        mixed, sums, other, affine, *chunks,
    )


def conv_level_kernel(up_ref, mixed_ref, sums_ref, other_ref, affine_ref, *refs):
    chunks, scaled_ref, totals_ref, affine_grad_ref = refs[:4], *refs[4:]
    normal, _ = conv_norm(mixed_ref, sums_ref, other_ref)
    levels = normal * affine_ref[0:1] + affine_ref[1:2]
    weight = heads_of(chunks, 2 * PAIR, 3 * PAIR)
    d_levels = product(up_ref[...], weight) * silu_slope(levels)
    scaled = d_levels * affine_ref[0:1]
    scaled_ref[...] = scaled
    totals_ref[...] = jnp.concatenate(
        [
            jnp.sum(scaled, axis=1, keepdims=True),
            jnp.sum(scaled * normal, axis=1, keepdims=True),
        ],
        1,
    )
    affine_grad_ref[0:1] = jnp.sum(d_levels * normal, axis=0, keepdims=True)
    affine_grad_ref[1:2] = jnp.sum(d_levels, axis=0, keepdims=True)


def conv_levels_back(upstream, mixed, sums, other, affine, chunks):
    return run(
        conv_level_kernel, "conv_levels_back",
        [(mixed.shape, F32), (sums.shape, F32), ((2, mixed.shape[1]), F32)],
        upstream, mixed, sums, other, affine, *chunks,
    )


def unmix_kernel(
    height, scaled_ref, totals_ref, far_totals_ref, mixed_ref, sums_ref, other_ref, taps_ref,
    d_mixed_ref, own_ref, earlier_ref, wide
):
    normal, inverse = conv_norm(mixed_ref, sums_ref, other_ref)
    means = paired(totals_ref, far_totals_ref)
    d_mixed = inverse * (scaled_ref[...] - means[:, 0:1] - normal * means[:, 1:2])
    d_mixed_ref[...] = d_mixed
    for clip in range(2):
        rows = slice(clip * height, (clip + 1) * height)
        wide[clip, :REACH] = jnp.zeros((REACH, d_mixed.shape[1]), F32)
        wide[clip, REACH : REACH + height] = d_mixed[rows]
        wide[clip, REACH + height :] = jnp.zeros((REACH, d_mixed.shape[1]), F32)
        last = REACH + KERNEL - 1
        for z in range(d_mixed.shape[1] // PAIR):
            lanes = slice(z * PAIR, (z + 1) * PAIR)
            own = wide[clip, last : last + height, lanes] * taps_ref[0:1, lanes]
            for j in range(1, KERNEL):
                own += wide[clip, last - j : last - j + height, lanes] * taps_ref[j : j + 1, lanes]
            own_ref[rows, lanes] = own
            early = wide[clip, KERNEL - 1 : KERNEL - 1 + REACH, lanes] * taps_ref[0:1, lanes]
            for j in range(1, KERNEL):
                start = KERNEL - 1 - j
                early += wide[clip, start : start + REACH, lanes] * taps_ref[j : j + 1, lanes]
            earlier_ref[clip, :, lanes] = early


def unmix_channels(scaled, totals, far_totals, mixed, sums, other, taps):
    height, channels = mixed.shape[0] // 2, mixed.shape[1]
    return run(
        functools.partial(unmix_kernel, height), "unmix_channels",
        [(mixed.shape, F32), (mixed.shape, F32), ((2, REACH, channels), F32)],
        scaled, totals, far_totals, mixed, sums, other, taps,
        scratch=[pltpu.VMEM((2, height + 2 * REACH, channels), F32)],
    )


def gate_back_kernel(height, own_ref, later_ref, value_ref, logistic_ref, live_ref, *refs):
    chunks, d_value_ref, d_gate_ref, branch_ref = refs[:4], *refs[4:]
    for clip in range(2):
        rows = slice(clip * height, (clip + 1) * height)
        own = own_ref[rows]
        low = own[height - REACH :] + later_ref[clip]
        own = jnp.concatenate([own[: height - REACH], low], 0) * live_ref[rows]
        logistic = logistic_ref[rows]
        d_value_ref[rows] = (own * logistic).astype(BF16)
        d_gate_ref[rows] = (own * value_ref[rows] * logistic * (1.0 - logistic)).astype(BF16)
    value = interleaved([d_value_ref[...], d_gate_ref[...]])
    branch_ref[...] = product_nt(value, heads_of(chunks, 0, 2 * PAIR)).astype(BF16)


def gate_back(own, later, value_half, logistic, live, chunks):
    shape = own.shape
    return run(
        functools.partial(gate_back_kernel, shape[0] // 2), "gate_back",
        [(shape, BF16), (shape, BF16), ((shape[0], D), BF16)],
        own, later, value_half, logistic, live, *chunks,
    )


def tap_kernel(height, d_mixed_ref, gated_ref, earlier_ref, taps_ref, wide):
    extend(earlier_ref, gated_ref, wide, height)
    lead = REACH - (KERNEL - 1)
    for z in range(gated_ref.shape[1] // PAIR):
        lanes = slice(z * PAIR, (z + 1) * PAIR)
        for j in range(KERNEL):
            total = jnp.zeros((1, PAIR), F32)
            for clip in range(2):
                total += jnp.sum(
                    d_mixed_ref[clip * height : (clip + 1) * height, lanes]
                    * wide[clip, lead + j : lead + j + height, lanes],
                    axis=0,
                    keepdims=True,
                )
            taps_ref[j : j + 1, lanes] = total


def tap_grads_of(d_mixed, gated, earlier):
    height, channels = gated.shape[0] // 2, gated.shape[1]
    return run(
        functools.partial(tap_kernel, height), "tap_grads", [((KERNEL, channels), F32)],
        d_mixed, gated, earlier,
        scratch=[pltpu.VMEM((2, height + REACH, channels), F32)],
    )[0]


def norm_grads_settle(grads, second):
    rows = lax.axis_size("row")
    width = grads.shape[1] // len(stream_places())
    where = {place: k for k, place in enumerate(stream_places())}
    cut = lambda p: grads[:, where[p] * width : (where[p] + 1) * width]
    order = [(b, a) for b in range(lax.axis_size("ctx")) for a in range(rows)]
    halves = [jnp.stack([cut((c, b, a)) for b, a in order], 0) for c in range(2)]
    own = jnp.where(second, halves[1], halves[0])
    total = own + swap_core(jnp.where(second, halves[0], halves[1]))
    for axis, mask in stages_of(A_AXES)[::-1]:
        count = total.shape[0] // 2
        total = total[:count] + partner(total[count:], axis, mask)
    return total[0]


def body(
    inputs,
    cotangent,
    lengths,
    buckets,
    ffn1_in,
    ffn1_out,
    norm_gains,
    norm_biases,
    qkv_weight,
    attn_out,
    distance,
    glu_in,
    depthwise,
    conv_gain,
    conv_bias,
    conv_out,
    ffn2_in,
    ffn2_out,
):
    rows, ctxs, tp = lax.axis_size("row"), lax.axis_size("ctx"), lax.axis_size("tp")
    second = lax.axis_index("core") == 1
    core = lax.axis_index("core").reshape(1).astype(jnp.int32)
    local = ffn1_in.shape[0]
    height = inputs.shape[1]
    first = (lax.axis_index("ctx") * tp + lax.axis_index("tp")) * height
    lens = widen_core(lengths)
    frame_ids = first + jnp.arange(height, dtype=jnp.int32)
    live = (frame_ids[None, :] < lens[:, None]).astype(F32).reshape(2 * height, 1)

    near = from_natural(inputs[0])
    wide_inputs = widen_early(to_ffn(near, "in", second))
    one_in, one_out = ffn_weight(ffn1_in, A_AXES), ffn_weight(ffn1_out, B_AXES)

    padded = lambda v: jnp.pad(v, ((0, 0), (0, PAIR - v.shape[1])))
    table_rows, width = distance.shape[0], conv_gain.shape[0]
    small = jnp.concatenate(
        [
            padded(norm_gains.T),
            padded(norm_biases.T),
            padded(depthwise.T),
            padded(conv_gain[None]),
            padded(conv_bias[None]),
            padded(distance),
        ],
        0,
    )
    cube = jnp.stack([small, swap_core(small)], 0)[None]
    for axis, mask in stages_of(A_AXES):
        cube = jnp.concatenate([cube, partner(cube, axis, mask)], 0)
    take = lambda c, k: jnp.where(second, cube[k, 1 - c], cube[k, c])
    norms = jnp.concatenate(
        [take(c, b * rows + a)[:10, :local] for c, b, a in stream_places()], 1
    ).astype(F32)
    norm = [jnp.stack([norms[k], norms[5 + k]], 0) for k in range(5)]
    blocks = [
        crossed([take(c, k)[10:] for k in range(rows * ctxs)]) for c in range(2)
    ]
    natural = [blocks[c][b * rows + a] for c, b, a in natural_places()]
    table_all = jnp.concatenate([n[KERNEL + 2 :, :SPAN] for n in natural], 0)
    conv_small = jnp.concatenate([n[: KERNEL + 2, :width] for n in natural], 1)
    half = conv_small.shape[1] // 2
    conv_small = jnp.where(second, conv_small[:, half:], conv_small[:, :half])
    for mask in bits_of("tp"):
        conv_small = tp_joined(conv_small, partner(conv_small, "tp", mask), mask, 1)
    conv_small = conv_small.astype(F32)
    taps, affine = conv_small[:KERNEL], conv_small[KERNEL:]

    w_attn = core_weight(
        core_shares([qkv_weight[:, 0], qkv_weight[:, 1], qkv_weight[:, 2], attn_out], second)
    )
    w_conv = core_weight(core_shares([glu_in[:, 0], glu_in[:, 1], conv_out], second))
    two_in, two_out = ffn_weight(ffn2_in, A_AXES), ffn_weight(ffn2_out, B_AXES)

    selector = (jnp.arange(SPAN, dtype=jnp.int32)[:, None] == buckets[None, :]).astype(BF16)
    rel = product(table_all, selector).astype(BF16)
    rel = jnp.pad(jnp.concatenate([rel, rel], 0), ((0, 0), (0, PAIR - SPAN)))

    hidden0, before0, active0, branch = ffn_first(
        wide_inputs, to_ffn(norm[0], "in", second), one_in, one_out
    )
    stream1, hidden1 = onward(
        core, [exchange_tp(branch)], near.astype(F32), norm[1], 0.5, "out", None
    )

    hidden1 = widen_core(hidden1)
    heads = project_heads(hidden1, w_attn)
    channels = heads[0].shape[1]
    key_value = [h.reshape(2, height, channels) for h in heads[1:]]
    left = along(jnp.concatenate([h[:, height - LEFT :] for h in key_value], 2), 1)
    right = along(jnp.concatenate([h[:, :RIGHT] for h in key_value], 2), -1)
    first_ref = first.reshape(1).astype(jnp.int32)
    context, chance, branch = attend(first_ref, lens, heads, left, right, rel, w_attn)
    stream2, hidden2 = onward(core, exchange_core(branch), stream1, norm[2], 1.0, None, None)

    hidden2 = widen_core(hidden2)
    value_half, logistic, gated = gate_channels(hidden2, live, w_conv)
    earlier = along(gated.reshape(2, height, channels)[:, height - REACH :], 1)
    mixed, sums = mix_channels(gated, earlier, taps)
    other = swap_core(sums)
    active_conv, branch = conv_forward(mixed, sums, other, affine, w_conv)
    stream3, hidden3 = onward(core, exchange_core(branch), stream2, norm[3], 1.0, None, "in")

    hidden3 = widen_tp(hidden3)
    before3, active3, branch = ffn_forward(hidden3, two_in, two_out)
    result, d_stream, d_branch, grads4 = turn(
        core, [exchange_tp(branch)], stream3, from_natural(cotangent[0]), norm[4]
    )

    d_branch = widen_tp(d_branch)
    d_before, branch = ffn_backward(d_branch, before3, two_in, two_out)
    grad_in, grad_out = ffn_grads(hidden3, d_before, d_branch, active3, two_in[0])
    grad_two_in, grad_two_out = ffn_settle(grad_in, A_AXES), ffn_settle(grad_out, B_AXES)
    d_stream, d_branch, grads3 = returning(
        core, [exchange_tp(branch)], stream3, d_stream, norm[3], 1.0, "in", None
    )

    d_branch = widen_core(d_branch)
    scaled, totals, affine_grads = conv_levels_back(d_branch, mixed, sums, other, affine, w_conv)
    d_mixed, d_own, d_earlier = unmix_channels(
        scaled, totals, swap_core(totals), mixed, sums, other, taps
    )
    later = along(d_earlier, -1)
    d_value, d_gate, branch = gate_back(d_own, later, value_half, logistic, live, w_conv)
    grads = core_grads(hidden2, d_branch, (d_value, d_gate), active_conv, w_conv[0])
    tap_grads = tap_grads_of(d_mixed, gated, earlier)
    grad_value, grad_gate, grad_w_conv = core_settle(grads, second, 3)
    d_stream, d_branch, grads2 = returning(
        core, exchange_core(branch), stream2, d_stream, norm[2], 1.0, None, None
    )

    d_branch = widen_core(d_branch)
    d_query, d_own, d_left, d_right, d_table = attend_back(
        first_ref, lens, d_branch, heads, left, right, rel, w_attn, chance
    )
    d_key, d_val, branch = heads_in(d_query, d_own, along(d_left, -1), along(d_right, 1), w_attn)
    grads = core_grads(hidden1, d_branch, (d_query, d_key, d_val), context, w_attn[0])
    grad_q, grad_k, grad_v, grad_w_attn = core_settle(grads, second, 4)
    d_stream, d_branch, grads1 = returning(
        core, exchange_core(branch), stream1, d_stream, norm[1], 0.5, None, "out"
    )

    d_branch = widen_tp(d_branch)
    d_before, branch = ffn_backward(d_branch, before0, one_in, one_out)
    grad_in, grad_out = ffn_grads(hidden0, d_before, d_branch, active0, one_in[0])
    grad_one_in, grad_one_out = ffn_settle(grad_in, A_AXES), ffn_settle(grad_out, B_AXES)
    d_stream, _, grads0 = returning(
        core, [exchange_tp(branch)], near, d_stream, norm[0], 1.0, "in", None
    )

    d_rel = (d_table[:HD] + d_table[HD:])[:, :SPAN]
    grad_table = jnp.dot(d_rel, selector.astype(F32).T, precision=lax.Precision.HIGHEST)
    early = jnp.concatenate([tap_grads, affine_grads], 0)
    for mask in bits_of("tp")[::-1]:
        kept, sent = tp_halves(early, mask, 1)
        early = kept + partner(sent, "tp", mask)
    early = jnp.concatenate([early, padded(grad_table)], 0)
    for axis, mask in stages_of(A_AXES):
        early = early + partner(early, axis, mask)
    far_early = swap_core(early)
    grad_table = (early + far_early)[KERNEL + 2 :, :SPAN]
    conv_cut = jnp.concatenate(
        [jnp.where(second, far_early, early), jnp.where(second, early, far_early)], 1
    )[: KERNEL + 2]
    place = (lax.axis_index("row") * 2 + lax.axis_index("core")) * ctxs + lax.axis_index("ctx")
    conv_cut = lax.dynamic_slice_in_dim(conv_cut, place * width, width, 1)
    grad_table = lax.dynamic_slice_in_dim(grad_table, place * table_rows, table_rows, 0)

    norm_grads = jnp.concatenate([grads0, grads1, grads2, grads3, grads4], 0)
    norm_grads = norm_grads_settle(norm_grads, second)
    final = jnp.concatenate([padded(norm_grads), padded(grad_table)], 0)
    for mask in bits_of("tp"):
        final = final + partner(final, "tp", mask)
    norm_grads = final[:10, :local].reshape(5, 2, local)
    grad_table = final[10:, :SPAN]

    return (
        to_natural(result)[None],
        to_natural(d_stream)[None],
        grad_one_in,
        grad_one_out,
        norm_grads[:, 0].T,
        norm_grads[:, 1].T,
        jnp.stack([grad_q, grad_k, grad_v], 1),
        grad_w_attn,
        grad_table,
        jnp.stack([grad_value, grad_gate], 1),
        conv_cut[:KERNEL].T,
        conv_cut[KERNEL],
        conv_cut[KERNEL + 1],
        grad_w_conv,
        grad_two_in,
        grad_two_out,
    )


def solution(mesh):
    shards, ctxs, tp = (mesh.shape[axis] for axis in ("shard", "ctx", "tp"))
    cut = Mesh(mesh.devices.reshape(shards // 2, 2, ctxs, tp), ("row", "core", "ctx", "tp"))
    shard = ("row", "core")
    block = ("row", "core", "ctx")
    every = ("tp", "row", "core", "ctx")
    weight = P(block, "tp")
    narrow = P(block, None)
    deep = P(block, None, "tp")
    frames = P(shard, ("ctx", "tp"), None)
    return jax.shard_map(
        body,
        mesh=cut,
        in_specs=(
            frames, frames, P(shard), P(), weight, weight, narrow, narrow, deep, weight, narrow,
            deep, P(every, None), P(every), P(every), weight, weight, weight,
        ),
        out_specs=(
            frames, frames, weight, weight, narrow, narrow, deep, weight, narrow, deep,
            P(every, None), P(every), P(every), weight, weight, weight,
        ),
        check_vma=False,
    )
```

time: 677 us -> 535 us (0.79)
  local copies, waits for them, and re-layouts: 120 us -> 50.1 us
  blocking collectives: 106 us -> 60.4 us
  Pallas kernels: 21.7 us -> 64.1 us
  matrix products: 40.2 us -> 0.31 us
  other arithmetic: 79 us -> 60.4 us
  starting transfers between devices: 83.6 us -> 101 us
  between operations: 19.3 us -> 5.05 us
  waiting for transfers between devices: 197 us -> 183 us
    ppermute x17 -> x86, waiting for transfers between devices: 23 us -> 150 us  [partner(): return lax.ppermute(value, axis, [(i, i ^ mask) for i in range(count)])]
    all_to_all x12 -> x4, waiting for transfers between devices: 114 us -> 16.7 us  [exchange_tp(): return lax.all_to_all(pieces, 'tp', 0, 0)]
    ppermute x17 -> x86, starting transfers between devices: 15.6 us -> 64.6 us  [partner(): return lax.ppermute(value, axis, [(i, i ^ mask) for i in range(count)])]
    pallas_call x2 -> x27, Pallas kernels: 21.7 us -> 64.1 us  [run(): pl.pallas_call(kernel, in_specs=[SMEM] * smem + [VMEM] * (len(args) - sme...]
    unnamed x657 -> x409, local copies, waits for them, and re-layouts: 78.3 us -> 37.6 us
    all_gather x3 -> x0, waiting for transfers between devices: 39.4 us -> none  [the longest x2 39.4 us: core_weights(): whole = lax.all_gather(both, ('tp', 'row', 'ctx'), axis=0, tiled=True)]
    all_to_all x12 -> x4, starting transfers between devices: 49.4 us -> 16.7 us  [exchange_tp(): return lax.all_to_all(pieces, 'tp', 0, 0)]
    dot_general x15 -> x0, matrix products: 28.6 us -> none  [the longest x7 15.2 us: product_nt(): lax.dot_general(left, right, (((1,), (1,)), ((), ())), preferred_element_...]
  transfers between devices with their start and end apart: 53 -> 99, of which waited for: 25 -> 34; matrix products, arithmetic and copies ran while one was open for 30% -> 13% of each run, Pallas kernels for 3% -> 10%
where the time goes in v3:
time: 535 us; the launch traced here: 525 us
  waiting for transfers between devices  183 us (34%)
  starting transfers between devices  101 us (19%)
  Pallas kernels  64.1 us (12%)
  other arithmetic  60.4 us (11%)
  blocking collectives  60.4 us (11%)
  local copies, waits for them, and re-layouts  50.1 us (9%)
    ppermute x86, waiting for transfers between devices, partner(): return lax.ppermute(value, axis, [(i, i ^ mask) for i in range(count)])  150 us
    ppermute x86, starting transfers between devices, partner(): return lax.ppermute(value, axis, [(i, i ^ mask) for i in range(count)])  64.6 us
    pallas_call x27, Pallas kernels, run(): pl.pallas_call(kernel, in_specs=[SMEM] * smem + [VMEM] * (len(args) - sme...  64.1 us
    all_gather x3, blocking collectives, widen_tp(): return lax.all_gather(rows, 'tp', axis=0, tiled=True)  60.4 us
    unnamed x409, local copies, waits for them, and re-layouts  37.6 us
    all_to_all x4, waiting for transfers between devices, exchange_tp(): return lax.all_to_all(pieces, 'tp', 0, 0)  16.7 us
    all_to_all x4, starting transfers between devices, exchange_tp(): return lax.all_to_all(pieces, 'tp', 0, 0)  16.7 us
    ppermute x6, waiting for transfers between devices, along(): return lax.ppermute(value, ('ctx', 'tp'), pairs)  16 us
  transfers between devices with their start and end apart: 99, of which 34 were waited for; matrix products, arithmetic and copies ran while one was open for 13% of the time, Pallas kernels for 10%

profile of v3, /device:TPU:0, one launch (start us, length us, event | category | flops | bytes accessed | tf_op | source)
XLA Modules:
  0.0 524.8 jit_solution(3836142737038932053)
XLA Ops:
  10.0 3.1 collective-permute-start.3
  35.6 5.9 %collective-permute-done.17 = bf16[2,1,128,512]{3,2,1,0:T(8,128)(2,1)S(1)} collective-permute-done((bf16[2,1,128,512]{3,2,1,0:T(8,128)(2,1)S(1)}, bf16[2,1,128,512]{3,2,1,0:T(8,128)(2,1)S(1)}, u32[]{:S(2)}, u32[]{:S(2)}) %collective-permute-start.17) | collective-permute-done | bytes 262176 | tf_op jit(solution)/shard_map/ppermute | solution.py:126
  43.0 4.8 collective-permute-done.11
  53.6 19.6 %collective-permute-done.18 = bf16[2,2,128,512]{3,2,1,0:T(8,128)(2,1)S(1)} collective-permute-done((bf16[2,2,128,512]{3,2,1,0:T(8,128)(2,1)S(1)}, bf16[2,2,128,512]{3,2,1,0:T(8,128)(2,1)S(1)}, u32[]{:S(2)}, u32[]{:S(2)}) %collective-permute-start.18) | collective-permute-done | bytes 524320 | tf_op jit(solution)/shard_map/ppermute | solution.py:126
  83.6 4.5 ffn_first.1
  90.0 4.2 all-to-all-start
  103.5 26.9 %collective-permute-done.29 = bf16[2,2,128,384]{3,2,1,0:T(8,128)(2,1)S(1)} collective-permute-done((bf16[2,2,128,384]{3,2,1,0:T(8,128)(2,1)S(1)}, bf16[2,2,128,384]{3,2,1,0:T(8,128)(2,1)S(1)}, u32[]{:S(2)}, u32[]{:S(2)}) %collective-permute-start.29) | collective-permute-done | bytes 393248 | tf_op jit(solution)/shard_map/ppermute | solution.py:126
  139.7 4.1 collective-permute-done.32
  148.2 6.3 %collective-permute-done.24.right_ref = bf16[2,16,1024]{2,1,0:T(8,128)(2,1)S(1)} collective-permute-done((bf16[2,16,1024]{2,1,0:T(8,128)(2,1)S(1)}, bf16[2,16,1024]{2,1,0:T(8,128)(2,1)S(1)}, u32[]{:S(2)}, u32[]{:S(2)}) %collective-permute-start.24) | collective-permute-done | bytes 65568 | tf_op jit(solution)/shard_map/ppermute | solution.py:228
  157.0 5.8 %attend.1 = (bf16[192,512]{1,0:T(8,128)(2,1)S(1)}, f32[2,4,192,256]{3,2,1,0:T(8,128)}, bf16[192,1024]{1,0:T(8,128)(2,1)S(1)}) custom-call(s32[1]{0:T(128)} %bitcast.1.first_ref, s32[2]{0:T(128)S(1)} %copy-done.138, bf16[192,512]{1,0:T(8,128)(2,1)S(1)} %get-tuple-element.104.q_ref, bf16[192,512]{1,0:T(8,128)(2,1)S(1)} %get-tuple-element.105.k_ref, ...), custom_call_target="tpu_custom_call" | custom-call | tf_op jit(solution)/shard_map/attend/pallas_call | solution.py:270
  168.1 5.2 collective-permute-done.31.refs_1_
  188.0 21.7 %all_gather.9.rows_ref.hidden_ref = bf16[384,1024]{1,0:T(8,128)(2,1)} all-gather(bf16[96,1024]{1,0:T(8,128)(2,1)S(1)} %get-tuple-element.115), channel_id=1, replica_groups=mesh['row'=2,'core'=2,'ctx'=2,'tp'=4] {'tp'}, dimensions={0}, use_global_device_ids=true | all-gather | bytes 983040 | tf_op jit(solution)/shard_map/all_gather | solution.py:232
  209.8 4.0 ffn_forward.1
  215.6 4.3 all-to-all-start.1
  223.5 15.4 %all-to-all-done.1.refs_0_ = bf16[4,96,1024]{2,1,0:T(8,128)(2,1)} async-done(((bf16[4,96,1024]{2,1,0:T(8,128)(2,1)}), bf16[4,96,1024]{2,1,0:T(8,128)(2,1)}, u32[]{:S(2)}, u32[]{:S(2)}) %all-to-all-start.1) | async-done | bytes 786464 | tf_op jit(solution)/shard_map/all_to_all | solution.py:252
  243.9 18.2 %all_gather.10.rows_ref.up_ref = bf16[384,1024]{1,0:T(8,128)(2,1)} all-gather(bf16[96,1024]{1,0:T(8,128)(2,1)S(1)} %get-tuple-element.119), channel_id=1, replica_groups=mesh['row'=2,'core'=2,'ctx'=2,'tp'=4] {'tp'}, dimensions={0}, use_global_device_ids=true | all-gather | bytes 983040 | tf_op jit(solution)/shard_map/all_gather | solution.py:232
  265.3 3.5 ffn_backward.2
  270.6 4.5 all-to-all-start.2
  278.0 3.7 ffn_grads.3
  315.1 5.3 %collective-permute-done.49.later_ref = f32[2,32,512]{2,1,0:T(8,128)S(1)} collective-permute-done((f32[2,32,512]{2,1,0:T(8,128)S(1)}, f32[2,32,512]{2,1,0:T(8,128)S(1)}, u32[]{:S(2)}, u32[]{:S(2)}) %collective-permute-start.49) | collective-permute-done | bytes 131104 | tf_op jit(solution)/shard_map/ppermute | solution.py:228
  325.5 8.3 %attend_back.1 = (bf16[192,512]{1,0:T(8,128)(2,1)S(1)}, f32[2,192,512]{2,1,0:T(8,128)S(1)}, bf16[2,2,64,512]{3,2,1,0:T(8,128)(2,1)}, bf16[2,2,16,512]{3,2,1,0:T(8,128)(2,1)}, f32[128,128]{1,0:T(8,128)S(1)}) custom-call(s32[1]{0:T(128)} %bitcast.1.first_ref, s32[2]{0:T(128)S(1)} %copy-done.139, ...), custom_call_target="tpu_custom_call" | custom-call | tf_op jit(solution)/shard_map/attend_back/pallas_call | solution.py:270
  340.4 4.4 collective-permute-done.69
  351.8 4.5 collective-permute-start.53
  383.9 20.5 %all_gather.11.rows_ref.up_ref = bf16[384,1024]{1,0:T(8,128)(2,1)} all-gather(bf16[96,1024]{1,0:T(8,128)(2,1)S(1)} %get-tuple-element.140), channel_id=1, replica_groups=mesh['row'=2,'core'=2,'ctx'=2,'tp'=4] {'tp'}, dimensions={0}, use_global_device_ids=true | all-gather | bytes 983040 | tf_op jit(solution)/shard_map/all_gather | solution.py:232
  404.4 4.4 ffn_backward.3
  408.8 3.6 all-to-all-start.3
  412.4 4.7 ffn_grads.2
  420.4 2.9 collective-permute-start.84
  425.5 20.5 %collective-permute-done.84 = bf16[2,2,128,384]{3,2,1,0:T(8,128)(2,1)S(1)} collective-permute-done((bf16[2,2,128,384]{3,2,1,0:T(8,128)(2,1)S(1)}, bf16[2,2,128,384]{3,2,1,0:T(8,128)(2,1)S(1)}, u32[]{:S(2)}, u32[]{:S(2)}) %collective-permute-start.84) | collective-permute-done | bytes 393248 | tf_op jit(solution)/shard_map/ppermute | solution.py:126
  472.4 7.7 %collective-permute-done.64 = f32[2,10,128]{2,1,0:T(8,128)S(1)} collective-permute-done((f32[2,10,128]{2,1,0:T(8,128)S(1)}, f32[2,10,128]{2,1,0:T(8,128)S(1)}, u32[]{:S(2)}, u32[]{:S(2)}) %collective-permute-start.64) | collective-permute-done | bytes 10272 | tf_op jit(solution)/shard_map/ppermute | solution.py:126
  490.4 21.6 %collective-permute-done.72 = f32[18,128]{1,0:T(8,128)S(1)} collective-permute-done((f32[18,128]{1,0:T(8,128)S(1)}, f32[18,128]{1,0:T(8,128)S(1)}, u32[]{:S(2)}, u32[]{:S(2)}) %collective-permute-start.72) | collective-permute-done | bytes 9248 | tf_op jit(solution)/shard_map/ppermute | solution.py:126
  517.8 3.5 collective-permute-done.78
  (821 shorter events, 242.0 us)
Async XLA Ops:
  10.0 38.9 %collective-permute-start.3 = (bf16[96,1024]{1,0:T(8,128)(2,1)S(1)}, bf16[96,1024]{1,0:T(8,128)(2,1)}, u32[]{:S(2)}, u32[]{:S(2)}) collective-permute-start(bf16[96,1024]{1,0:T(8,128)(2,1)S(1)} %broadcast_select_fusion.8), channel_id=1, source_target_pairs={{0,1},{1,0},{2,3},{3,2},{4,5},{5,4},{6,7},{7,6},{8,9},{9,8},{10,11... | collective-permute-start | bytes 589832 | tf_op jit(solution)/shard_map/ppermute | solution.py:239
  13.1 38.0 %collective-permute-start.2 = (bf16[96,1024]{1,0:T(8,128)(2,1)S(1)}, bf16[96,1024]{1,0:T(8,128)(2,1)}, u32[]{:S(2)}, u32[]{:S(2)}) collective-permute-start(bf16[96,1024]{1,0:T(8,128)(2,1)S(1)} %broadcast_select_fusion.8), channel_id=1, source_target_pairs={{0,2},{1,3},{2,0},{3,1},{4,6},{5,7},{6,4},{7,5},{8,10},{9,11},{10,... | collective-permute-start | bytes 589832 | tf_op jit(solution)/shard_map/ppermute | solution.py:239
  20.0 28.4 %collective-permute-start.27 = (bf16[128,384]{1,0:T(8,128)(2,1)S(1)}, bf16[128,384]{1,0:T(8,128)(2,1)S(1)}, u32[]{:S(2)}, u32[]{:S(2)}) collective-permute-start(bf16[128,384]{1,0:T(8,128)(2,1)S(1)} %copy.62), channel_id=1, source_target_pairs={{0,8},{8,0},{1,9},{9,1},{2,10},{10,2},{3,11},{11,3},{4,12},{12,4},... | collective-permute-start | bytes 294920 | tf_op jit(solution)/shard_map/ppermute | solution.py:126
  47.8 25.4 %collective-permute-start.18 = (bf16[2,2,128,512]{3,2,1,0:T(8,128)(2,1)S(1)}, bf16[2,2,128,512]{3,2,1,0:T(8,128)(2,1)S(1)}, u32[]{:S(2)}, u32[]{:S(2)}) collective-permute-start(bf16[2,2,128,512]{3,2,1,0:T(8,128)(2,1)S(1)} %pad_maximum_fusion.10), channel_id=1, source_target_pairs={{0,2},{1,3},{2,0},{3,1},{4,6},{5,7},{6,4},{7,5},{8,10},{9,11},{10,... | collective-permute-start | bytes 1572872 | tf_op jit(solution)/shard_map/ppermute | solution.py:126
  48.2 29.6 %collective-permute-start.13 = (bf16[2,128,1024]{2,1,0:T(8,128)(2,1)S(1)}, bf16[2,128,1024]{2,1,0:T(8,128)(2,1)S(1)}, u32[]{:S(2)}, u32[]{:S(2)}) collective-permute-start(bf16[2,128,1024]{2,1,0:T(8,128)(2,1)S(1)} %pad_maximum_fusion.9.refs_4_), channel_id=1, source_target_pairs={{0,8},{8,0},{1,9},{9,1},{2,10},{10,2},{3,11},{11,3},{4,12},{12,4},... | collective-permute-start | bytes 1572872 | tf_op jit(solution)/shard_map/ppermute | solution.py:126
  82.3 80.7 %collective-permute-start.39 = (bf16[1,128,1024]{2,1,0:T(8,128)(2,1)}, bf16[1,128,1024]{2,1,0:T(8,128)(2,1)}, u32[]{:S(2)}, u32[]{:S(2)}) collective-permute-start(bf16[1,128,1024]{2,1,0:T(8,128)(2,1)} %bitcast.44), channel_id=1, source_target_pairs={{0,16},{16,0},{1,17},{17,1},{2,18},{18,2},{3,19},{19,3},{4,20},{20... | collective-permute-start | bytes 786440 | tf_op jit(solution)/shard_map/ppermute | solution.py:126
  90.0 42.0 %all-to-all-start = ((bf16[4,96,1024]{2,1,0:T(8,128)(2,1)}), bf16[4,96,1024]{2,1,0:T(8,128)(2,1)}, u32[]{:S(2)}, u32[]{:S(2)}) async-start(bf16[4,96,1024]{2,1,0:T(8,128)(2,1)} %bitcast.205), calls=%async_computation | async-start | bytes 1572864 | tf_op jit(solution)/shard_map/all_to_all | solution.py:252
  95.3 35.1 %collective-permute-start.29 = (bf16[2,2,128,384]{3,2,1,0:T(8,128)(2,1)S(1)}, bf16[2,2,128,384]{3,2,1,0:T(8,128)(2,1)S(1)}, u32[]{:S(2)}, u32[]{:S(2)}) collective-permute-start(bf16[2,2,128,384]{3,2,1,0:T(8,128)(2,1)S(1)} %pad_maximum_fusion.14), channel_id=1, source_target_pairs={{0,2},{1,3},{2,0},{3,1},{4,6},{5,7},{6,4},{7,5},{8,10},{9,11},{10,... | collective-permute-start | bytes 1179656 | tf_op jit(solution)/shard_map/ppermute | solution.py:126
  99.4 36.6 %collective-permute-start.20 = (bf16[2,4,128,512]{3,2,1,0:T(8,128)(2,1)S(1)}, bf16[2,4,128,512]{3,2,1,0:T(8,128)(2,1)S(1)}, u32[]{:S(2)}, u32[]{:S(2)}) collective-permute-start(bf16[2,4,128,512]{3,2,1,0:T(8,128)(2,1)S(1)} %pad_maximum_fusion.1.refs_0_.c0), channel_id=1, source_target_pairs={{0,4},{4,0},{1,5},{5,1},{2,6},{6,2},{3,7},{7,3},{8,12},{12,8},{9,1... | collective-permute-start | bytes 3145736 | tf_op jit(solution)/shard_map/ppermute | solution.py:126
  101.3 36.3 %collective-permute-start.22 = (bf16[2,4,128,512]{3,2,1,0:T(8,128)(2,1)S(1)}, bf16[2,4,128,512]{3,2,1,0:T(8,128)(2,1)}, u32[]{:S(2)}, u32[]{:S(2)}) collective-permute-start(bf16[2,4,128,512]{3,2,1,0:T(8,128)(2,1)S(1)} %pad_maximum_fusion.2.refs_2_.c2), channel_id=1, source_target_pairs={{0,16},{16,0},{1,17},{17,1},{2,18},{18,2},{3,19},{19,3},{4,20},{20... | collective-permute-start | bytes 3145736 | tf_op jit(solution)/shard_map/ppermute | solution.py:126
  136.0 26.8 %collective-permute-start.43 = (bf16[1,128,1024]{2,1,0:T(8,128)(2,1)S(1)}, bf16[1,128,1024]{2,1,0:T(8,128)(2,1)S(1)}, u32[]{:S(2)}, u32[]{:S(2)}) collective-permute-start(bf16[1,128,1024]{2,1,0:T(8,128)(2,1)S(1)} %bitcast.219), channel_id=1, source_target_pairs={{0,4},{4,0},{1,5},{5,1},{2,6},{6,2},{3,7},{7,3},{8,12},{12,8},{9,1... | collective-permute-start | bytes 786440 | tf_op jit(solution)/shard_map/ppermute | solution.py:126
  137.5 29.0 %collective-permute-start.36 = (bf16[33,256]{1,0:T(8,128)(2,1)S(1)}, bf16[33,256]{1,0:T(8,128)(2,1)S(1)}, u32[]{:S(2)}, u32[]{:S(2)}) collective-permute-start(bf16[33,256]{1,0:T(8,128)(2,1)S(1)} %pad_maximum_fusion.25), channel_id=1, source_target_pairs={{0,2},{1,3},{2,0},{3,1},{4,6},{5,7},{6,4},{7,5},{8,10},{9,11},{10,... | collective-permute-start | bytes 50696 | tf_op jit(solution)/shard_map/ppermute | solution.py:126
  183.1 26.6 %collective-permute-start.45 = (bf16[2,128,1024]{2,1,0:T(8,128)(2,1)S(1)}, bf16[2,128,1024]{2,1,0:T(8,128)(2,1)S(1)}, u32[]{:S(2)}, u32[]{:S(2)}) collective-permute-start(bf16[2,128,1024]{2,1,0:T(8,128)(2,1)S(1)} %pad_maximum_fusion.12.refs_4_), channel_id=1, source_target_pairs={{0,8},{8,0},{1,9},{9,1},{2,10},{10,2},{3,11},{11,3},{4,12},{12,4},... | collective-permute-start | bytes 1572872 | tf_op jit(solution)/shard_map/ppermute | solution.py:126
  183.7 26.0 %collective-permute-start.41 = (bf16[2,128,1024]{2,1,0:T(8,128)(2,1)S(1)}, bf16[2,128,1024]{2,1,0:T(8,128)(2,1)S(1)}, u32[]{:S(2)}, u32[]{:S(2)}) collective-permute-start(bf16[2,128,1024]{2,1,0:T(8,128)(2,1)S(1)} %pad_maximum_fusion.11.refs_0_), channel_id=1, source_target_pairs={{0,8},{8,0},{1,9},{9,1},{2,10},{10,2},{3,11},{11,3},{4,12},{12,4},... | collective-permute-start | bytes 1572872 | tf_op jit(solution)/shard_map/ppermute | solution.py:126
  183.7 25.9 %collective-permute-start.46 = (bf16[2,128,1024]{2,1,0:T(8,128)(2,1)S(1)}, bf16[2,128,1024]{2,1,0:T(8,128)(2,1)S(1)}, u32[]{:S(2)}, u32[]{:S(2)}) collective-permute-start(bf16[2,128,1024]{2,1,0:T(8,128)(2,1)S(1)} %collective-permute-done.44.refs_5_), channel_id=1, source_target_pairs={{0,8},{8,0},{1,9},{9,1},{2,10},{10,2},{3,11},{11,3},{4,12},{12,4},... | collective-permute-start | bytes 1572872 | tf_op jit(solution)/shard_map/ppermute | solution.py:126
  184.2 25.5 %collective-permute-start.42 = (bf16[2,128,1024]{2,1,0:T(8,128)(2,1)S(1)}, bf16[2,128,1024]{2,1,0:T(8,128)(2,1)S(1)}, u32[]{:S(2)}, u32[]{:S(2)}) collective-permute-start(bf16[2,128,1024]{2,1,0:T(8,128)(2,1)S(1)} %collective-permute-done.40.refs_1_), channel_id=1, source_target_pairs={{0,8},{8,0},{1,9},{9,1},{2,10},{10,2},{3,11},{11,3},{4,12},{12,4},... | collective-permute-start | bytes 1572872 | tf_op jit(solution)/shard_map/ppermute | solution.py:126
  297.5 37.7 %collective-permute-start.91 = (bf16[2,128,1024]{2,1,0:T(8,128)(2,1)}, bf16[2,128,1024]{2,1,0:T(8,128)(2,1)S(1)}, u32[]{:S(2)}, u32[]{:S(2)}) collective-permute-start(bf16[2,128,1024]{2,1,0:T(8,128)(2,1)} %copy-done.140), channel_id=1, source_target_pairs={{0,8},{8,0},{1,9},{9,1},{2,10},{10,2},{3,11},{11,3},{4,12},{12,4},... | collective-permute-start | bytes 1572872 | tf_op jit(solution)/shard_map/ppermute | solution.py:126
  349.7 27.8 %collective-permute-start.80 = (bf16[2,4,128,384]{3,2,1,0:T(8,128)(2,1)}, bf16[2,4,128,384]{3,2,1,0:T(8,128)(2,1)}, u32[]{:S(2)}, u32[]{:S(2)}) collective-permute-start(bf16[2,4,128,384]{3,2,1,0:T(8,128)(2,1)} %get-tuple-element.175), channel_id=1, source_target_pairs={{0,4},{4,0},{1,5},{5,1},{2,6},{6,2},{3,7},{7,3},{8,12},{12,8},{9,1... | collective-permute-start | bytes 2359304 | tf_op jit(solution)/shard_map/ppermute | solution.py:126
  351.0 29.7 %collective-permute-start.82 = (bf16[2,4,128,384]{3,2,1,0:T(8,128)(2,1)}, bf16[2,4,128,384]{3,2,1,0:T(8,128)(2,1)}, u32[]{:S(2)}, u32[]{:S(2)}) collective-permute-start(bf16[2,4,128,384]{3,2,1,0:T(8,128)(2,1)} %get-tuple-element.177), channel_id=1, source_target_pairs={{0,16},{16,0},{1,17},{17,1},{2,18},{18,2},{3,19},{19,3},{4,20},{20... | collective-permute-start | bytes 2359304 | tf_op jit(solution)/shard_map/ppermute | solution.py:126
  374.6 72.1 %collective-permute-start.73 = (bf16[2,4,128,512]{3,2,1,0:T(8,128)(2,1)}, bf16[2,4,128,512]{3,2,1,0:T(8,128)(2,1)}, u32[]{:S(2)}, u32[]{:S(2)}) collective-permute-start(bf16[2,4,128,512]{3,2,1,0:T(8,128)(2,1)} %get-tuple-element.168), channel_id=1, source_target_pairs={{0,4},{4,0},{1,5},{5,1},{2,6},{6,2},{3,7},{7,3},{8,12},{12,8},{9,1... | collective-permute-start | bytes 3145736 | tf_op jit(solution)/shard_map/ppermute | solution.py:126
  376.3 74.1 %collective-permute-start.75 = (bf16[2,4,128,512]{3,2,1,0:T(8,128)(2,1)}, bf16[2,4,128,512]{3,2,1,0:T(8,128)(2,1)}, u32[]{:S(2)}, u32[]{:S(2)}) collective-permute-start(bf16[2,4,128,512]{3,2,1,0:T(8,128)(2,1)} %get-tuple-element.170), channel_id=1, source_target_pairs={{0,16},{16,0},{1,17},{17,1},{2,18},{18,2},{3,19},{19,3},{4,20},{20... | collective-permute-start | bytes 3145736 | tf_op jit(solution)/shard_map/ppermute | solution.py:126
  379.8 37.5 %collective-permute-start.81 = (bf16[1,4,128,384]{3,2,1,0:T(8,128)(2,1)}, bf16[1,4,128,384]{3,2,1,0:T(8,128)(2,1)}, u32[]{:S(2)}, u32[]{:S(2)}) collective-permute-start(bf16[1,4,128,384]{3,2,1,0:T(8,128)(2,1)} %slice.1583), channel_id=1, source_target_pairs={{0,16},{16,0},{1,17},{17,1},{2,18},{18,2},{3,19},{19,3},{4,20},{20... | collective-permute-start | bytes 1179656 | tf_op jit(solution)/shard_map/ppermute | solution.py:126
  383.0 36.1 %collective-permute-start.83 = (bf16[1,4,128,384]{3,2,1,0:T(8,128)(2,1)}, bf16[1,4,128,384]{3,2,1,0:T(8,128)(2,1)}, u32[]{:S(2)}, u32[]{:S(2)}) collective-permute-start(bf16[1,4,128,384]{3,2,1,0:T(8,128)(2,1)} %slice.1582), channel_id=1, source_target_pairs={{0,4},{4,0},{1,5},{5,1},{2,6},{6,2},{3,7},{7,3},{8,12},{12,8},{9,1... | collective-permute-start | bytes 1179656 | tf_op jit(solution)/shard_map/ppermute | solution.py:126
  408.8 59.4 %all-to-all-start.3 = ((bf16[4,96,1024]{2,1,0:T(8,128)(2,1)}), bf16[4,96,1024]{2,1,0:T(8,128)(2,1)S(1)}, u32[]{:S(2)}, u32[]{:S(2)}) async-start(bf16[4,96,1024]{2,1,0:T(8,128)(2,1)} %bitcast.50), calls=%async_computation.3 | async-start | bytes 1572864 | tf_op jit(solution)/shard_map/all_to_all | solution.py:252
  417.1 43.1 %collective-permute-start.55 = (bf16[2,128,1024]{2,1,0:T(8,128)(2,1)}, bf16[2,128,1024]{2,1,0:T(8,128)(2,1)S(1)}, u32[]{:S(2)}, u32[]{:S(2)}) collective-permute-start(bf16[2,128,1024]{2,1,0:T(8,128)(2,1)} %get-tuple-element.149), channel_id=1, source_target_pairs={{0,8},{8,0},{1,9},{9,1},{2,10},{10,2},{3,11},{11,3},{4,12},{12,4},... | collective-permute-start | bytes 1572872 | tf_op jit(solution)/shard_map/ppermute | solution.py:126
  420.4 25.7 %collective-permute-start.84 = (bf16[2,2,128,384]{3,2,1,0:T(8,128)(2,1)S(1)}, bf16[2,2,128,384]{3,2,1,0:T(8,128)(2,1)S(1)}, u32[]{:S(2)}, u32[]{:S(2)}) collective-permute-start(bf16[2,2,128,384]{3,2,1,0:T(8,128)(2,1)S(1)} %select_convert_fusion.1), channel_id=1, source_target_pairs={{0,2},{1,3},{2,0},{3,1},{4,6},{5,7},{6,4},{7,5},{8,10},{9,11},{10,... | collective-permute-start | bytes 1179656 | tf_op jit(solution)/shard_map/ppermute | solution.py:126
  424.3 40.8 %collective-permute-start.59 = (bf16[2,128,1024]{2,1,0:T(8,128)(2,1)}, bf16[2,128,1024]{2,1,0:T(8,128)(2,1)}, u32[]{:S(2)}, u32[]{:S(2)}) collective-permute-start(bf16[2,128,1024]{2,1,0:T(8,128)(2,1)} %get-tuple-element.153), channel_id=1, source_target_pairs={{0,8},{8,0},{1,9},{9,1},{2,10},{10,2},{3,11},{11,3},{4,12},{12,4},... | collective-permute-start | bytes 1572872 | tf_op jit(solution)/shard_map/ppermute | solution.py:126
  457.5 26.3 %collective-permute-start.74 = (bf16[1,4,128,512]{3,2,1,0:T(8,128)(2,1)}, bf16[1,4,128,512]{3,2,1,0:T(8,128)(2,1)S(1)}, u32[]{:S(2)}, u32[]{:S(2)}) collective-permute-start(bf16[1,4,128,512]{3,2,1,0:T(8,128)(2,1)} %slice.1581), channel_id=1, source_target_pairs={{0,16},{16,0},{1,17},{17,1},{2,18},{18,2},{3,19},{19,3},{4,20},{20... | collective-permute-start | bytes 1572872 | tf_op jit(solution)/shard_map/ppermute | solution.py:126
  460.2 25.0 %collective-permute-start.76 = (bf16[1,4,128,512]{3,2,1,0:T(8,128)(2,1)}, bf16[1,4,128,512]{3,2,1,0:T(8,128)(2,1)}, u32[]{:S(2)}, u32[]{:S(2)}) collective-permute-start(bf16[1,4,128,512]{3,2,1,0:T(8,128)(2,1)} %slice.1580), channel_id=1, source_target_pairs={{0,4},{4,0},{1,5},{5,1},{2,6},{6,2},{3,7},{7,3},{8,12},{12,8},{9,1... | collective-permute-start | bytes 1572872 | tf_op jit(solution)/shard_map/ppermute | solution.py:126
  463.9 50.4 %collective-permute-start.58 = (bf16[1,128,1024]{2,1,0:T(8,128)(2,1)}, bf16[1,128,1024]{2,1,0:T(8,128)(2,1)S(1)}, u32[]{:S(2)}, u32[]{:S(2)}) collective-permute-start(bf16[1,128,1024]{2,1,0:T(8,128)(2,1)} %slice.1587), channel_id=1, source_target_pairs={{0,16},{16,0},{1,17},{17,1},{2,18},{18,2},{3,19},{19,3},{4,20},{20... | collective-permute-start | bytes 786440 | tf_op jit(solution)/shard_map/ppermute | solution.py:126
  467.7 48.3 %collective-permute-start.62 = (bf16[1,128,1024]{2,1,0:T(8,128)(2,1)}, bf16[1,128,1024]{2,1,0:T(8,128)(2,1)}, u32[]{:S(2)}, u32[]{:S(2)}) collective-permute-start(bf16[1,128,1024]{2,1,0:T(8,128)(2,1)} %slice.1586), channel_id=1, source_target_pairs={{0,4},{4,0},{1,5},{5,1},{2,6},{6,2},{3,7},{7,3},{8,12},{12,8},{9,1... | collective-permute-start | bytes 786440 | tf_op jit(solution)/shard_map/ppermute | solution.py:126
  487.4 26.5 %collective-permute-start.77 = (bf16[2,2,128,512]{3,2,1,0:T(8,128)(2,1)}, bf16[2,2,128,512]{3,2,1,0:T(8,128)(2,1)S(1)}, u32[]{:S(2)}, u32[]{:S(2)}) collective-permute-start(bf16[2,2,128,512]{3,2,1,0:T(8,128)(2,1)} %select_convert_fusion), channel_id=1, source_target_pairs={{0,2},{1,3},{2,0},{3,1},{4,6},{5,7},{6,4},{7,5},{8,10},{9,11},{10,... | collective-permute-start | bytes 1572872 | tf_op jit(solution)/shard_map/ppermute | solution.py:126
  (254 other events, 2263.2 us)

commit v4 on v3

--- a/solution.py
+++ b/solution.py
@@ -99,26 +99,8 @@
     return [(c, b, a) for a in range(rows) for c in range(2) for b in range(ctxs)]
 
 
-def from_natural(value):
-    rows, ctxs = lax.axis_size("row"), lax.axis_size("ctx")
-    grid = [(c, b, a) for c in range(2) for b in range(ctxs) for a in range(rows)]
-    value = reorder(value, natural_places(), grid)
-    width = value.shape[-1] // len(grid)
-    blocks = [value[..., k * width : (k + 1) * width] for k in range(len(grid))]
-    half = len(grid) // 2
-    value = jnp.concatenate(crossed(blocks[:half]) + crossed(blocks[half:]), -1)
-    return reorder(value, grid, stream_places())
-
-
-def to_natural(value):
-    rows, ctxs = lax.axis_size("row"), lax.axis_size("ctx")
-    grid = [(c, b, a) for c in range(2) for b in range(ctxs) for a in range(rows)]
-    value = reorder(value, stream_places(), grid)
-    width = value.shape[-1] // len(grid)
-    blocks = [value[..., k * width : (k + 1) * width] for k in range(len(grid))]
-    half = len(grid) // 2
-    value = jnp.concatenate(crossed(blocks[:half]) + crossed(blocks[half:]), -1)
-    return reorder(value, grid, natural_places())
+def tied(*groups):
+    return lax.optimization_barrier(groups)
 
 
 def partner(value, axis, mask):
@@ -134,37 +116,55 @@
     return [(axis, mask) for axis in axes for mask in bits_of(axis)]
 
 
-def cube_pair(value, axes):
-    value = value[None]
-    stages = stages_of(axes)
-    for axis, mask in stages[:-1]:
-        value = jnp.concatenate([value, partner(value, axis, mask)], 0)
-    return value, partner(value, *stages[-1])
-
-
-def cube_settle(near, far, axes):
-    stages = stages_of(axes)[::-1]
-    total = near.astype(F32) + partner(far, *stages[0]).astype(F32)
-    for axis, mask in stages[1:]:
-        half = total.shape[0] // 2
-        arrived = partner(total[half:].astype(BF16), axis, mask)
-        total = total[:half] + arrived.astype(F32)
-    return total[0]
-
-
-def ffn_weight(weight, axes):
-    near, far = cube_pair(weight, axes)
-    return [near, far, swap_core(near), swap_core(far)]
-
-
-def ffn_settle(chunks, axes):
-    near = chunks[0].astype(F32) + swap_core(chunks[2]).astype(F32)
-    far = chunks[1].astype(F32) + swap_core(chunks[3]).astype(F32)
-    return cube_settle(near, far.astype(BF16), axes)
-
-
 A_AXES = ("row", "ctx")
 B_AXES = ("ctx", "row")
+
+
+def gather_first(weights):
+    values = [w[None] for w in weights]
+    rounds = [stages_of(axes)[:-1] for axes in (A_AXES, B_AXES)]
+    for k in range(len(rounds[0])):
+        values = join_pairs(values, [partner(v, *stages[k]) for v, stages in zip(values, rounds)])
+    return values
+
+
+def gather_last(values):
+    far = [
+        partner(values[0], *stages_of(A_AXES)[-1]),
+        partner(values[1], *stages_of(B_AXES)[-1]),
+    ]
+    return [values[0], far[0], values[1], far[1]]
+
+
+def ffn_weights(halves):
+    other = [swap_core(h) for h in halves]
+    return [*halves[:2], *other[:2]], [*halves[2:], *other[2:]]
+
+
+def settle_open(chunks):
+    near_a, far_a, near_b, far_b = chunks
+    arrived = [
+        partner(far_a, *stages_of(A_AXES)[-1]),
+        partner(far_b, *stages_of(B_AXES)[-1]),
+    ]
+    return [near_a, near_b], arrived
+
+
+def settle_close(own, far):
+    halves = sum_halves(own, far)
+    rounds = [stages_of(axes)[:-1][::-1] for axes in (A_AXES, B_AXES)]
+    for k in range(len(rounds[0])):
+        kept, sent = halves[:2], halves[2:]
+        arrived = [partner(s, *stages[k]) for s, stages in zip(sent, rounds)]
+        if k < len(rounds[0]) - 1:
+            halves = sum_halves(kept, arrived)
+    return kept, arrived
+
+
+def ffn_halves(grads_in, grads_out):
+    own = [*grads_in[:2], *grads_out[:2]]
+    far = [swap_core(g) for g in (*grads_in[2:], *grads_out[2:])]
+    return sum_pairs(own, far, BF16)
 
 
 def tp_joined(own, arrived, mask, axis):
@@ -174,14 +174,6 @@
     )
 
 
-def tp_halves(value, mask, axis):
-    upper = (lax.axis_index("tp") & mask) != 0
-    half = value.shape[axis] // 2
-    low = lax.slice_in_dim(value, 0, half, axis=axis)
-    high = lax.slice_in_dim(value, half, 2 * half, axis=axis)
-    return jnp.where(upper, high, low), jnp.where(upper, low, high)
-
-
 def core_shares(matrices, second):
     halves = jnp.concatenate(
         [m.reshape(m.shape[0], 2, 1, m.shape[1] // 2) for m in matrices], 2
@@ -190,36 +182,27 @@
     own, other = jnp.where(second, other, own), jnp.where(second, own, other)
     own = own.reshape(own.shape[0], -1)
     other = swap_core(other.reshape(own.shape))
-    value = jnp.stack([jnp.where(second, other, own), jnp.where(second, own, other)], 0)[:, None]
-    for mask in bits_of("tp"):
-        value = tp_joined(value, partner(value, "tp", mask), mask, 1)
-    return value
-
-
-def core_weight(value):
-    return [*cube_pair(value[0], A_AXES), *cube_pair(value[1], B_AXES)]
-
-
-def core_settle(chunks, second, count):
-    total = jnp.stack(
-        [
-            cube_settle(chunks[0], chunks[1], A_AXES),
-            cube_settle(chunks[2], chunks[3], B_AXES),
-        ],
-        0,
-    )
+    return jnp.stack([jnp.where(second, other, own), jnp.where(second, own, other)], 0)
+
+
+def tp_first(value):
+    steps = lax.axis_size("tp").bit_length() - 1
+    value = value.reshape((2,) + (1,) * steps + value.shape[1:])
+    mask = bits_of("tp")[-1]
+    return tp_joined(value, partner(value, "tp", mask), mask, 1)
+
+
+def tp_rest(value):
+    for k, mask in enumerate(bits_of("tp")[:-1][::-1]):
+        value = tp_joined(value, partner(value, "tp", mask), mask, 2 + k)
+    return value.reshape((2, -1) + value.shape[-2:])
+
+
+def core_finish(ids, kept, arrived, count):
+    own, sent = tp_open(ids, kept, arrived)
     for mask in bits_of("tp")[::-1]:
-        kept, sent = tp_halves(total, mask, 1)
-        total = kept + partner(sent.astype(BF16), "tp", mask).astype(F32)
-    total = total[:, 0]
-    own = jnp.where(second, total[1], total[0])
-    other = swap_core(jnp.where(second, total[0], total[1]).astype(BF16)).astype(F32)
-    own = own.reshape(own.shape[0], count, -1)
-    other = other.reshape(own.shape)
-    whole = jnp.concatenate(
-        [jnp.where(second, other, own), jnp.where(second, own, other)], 2
-    )
-    return [whole[:, m] for m in range(count)]
+        own, sent = tp_next(ids, own, partner(sent, "tp", mask))
+    return core_last(ids, own, swap_core(sent), count)
 
 
 def along(value, step):
@@ -232,18 +215,6 @@
     return lax.all_gather(rows, "tp", axis=0, tiled=True)
 
 
-def widen_early(rows):
-    count = lax.axis_size("tp")
-    index = lax.axis_index("tp")
-    parts = [rows] + [
-        lax.ppermute(rows, "tp", [(i, i ^ k) for i in range(count)]) for k in range(1, count)
-    ]
-    for mask in bits_of("tp"):
-        flag = (index & mask) != 0
-        parts = [jnp.where(flag, parts[k ^ mask], parts[k]) for k in range(count)]
-    return jnp.concatenate(parts, 0)
-
-
 def exchange_tp(partial_value):
     count = lax.axis_size("tp")
     pieces = partial_value.reshape(
@@ -261,16 +232,20 @@
     return [partial_value[:half], swap_core(partial_value[half:])]
 
 
-PARAMS = pltpu.CompilerParams(vmem_limit_bytes=48 << 20)
-VMEM = pl.BlockSpec(memory_space=pltpu.VMEM)
+PARAMS = pltpu.CompilerParams(vmem_limit_bytes=24 << 20)
 SMEM = pl.BlockSpec(memory_space=pltpu.SMEM)
+
+
+def whole(shape):
+    return pl.BlockSpec(shape, lambda step: (0,) * len(shape))
 
 
 def run(kernel, name, outs, *args, smem=0, scratch=()):
     return pl.pallas_call(
         kernel,
-        in_specs=[SMEM] * smem + [VMEM] * (len(args) - smem),
-        out_specs=[VMEM] * len(outs),
+        grid=(1,),
+        in_specs=[SMEM] * smem + [whole(a.shape) for a in args[smem:]],
+        out_specs=[whole(shape) for shape, _ in outs],
         out_shape=[jax.ShapeDtypeStruct(shape, dtype) for shape, dtype in outs],
         scratch_shapes=list(scratch),
         compiler_params=PARAMS,
@@ -278,8 +253,101 @@
     )(*args)
 
 
+def join_kernel(count, *refs):
+    for own, far, out_ref in zip(refs[:count], refs[count : 2 * count], refs[2 * count :]):
+        half = own.shape[0]
+        out_ref[:half] = own[...]
+        out_ref[half:] = far[...]
+
+
+def join_pairs(own, far):
+    outs = [((2 * v.shape[0], *v.shape[1:]), v.dtype) for v in own]
+    return list(run(functools.partial(join_kernel, len(own)), "join_pairs", outs, *own, *far))
+
+
+def sum_kernel(count, *refs):
+    for own, far, out_ref in zip(refs[:count], refs[count : 2 * count], refs[2 * count :]):
+        total = own[...].astype(F32) + far[...].astype(F32)
+        out_ref[...] = total.reshape(out_ref.shape).astype(out_ref.dtype)
+
+
+def sum_pairs(own, far, dtype, shape=None):
+    outs = [(shape or v.shape, dtype) for v in own]
+    return list(run(functools.partial(sum_kernel, len(own)), "sum_pairs", outs, *own, *far))
+
+
+def halves_kernel(*refs):
+    for k in range(2):
+        own, far, kept_ref, sent_ref = refs[k::2]
+        total = (own[...].astype(F32) + far[...].astype(F32)).astype(BF16)
+        half = total.shape[0] // 2
+        kept_ref[...] = total[:half]
+        sent_ref[...] = total[half:]
+
+
+def sum_halves(own, far):
+    outs = [((v.shape[0] // 2, *v.shape[1:]), BF16) for v in own] * 2
+    return list(run(halves_kernel, "sum_halves", outs, *own, *far))
+
+
+def tp_open_kernel(ids_ref, *refs):
+    own_ref, sent_ref = refs[4:]
+    half = own_ref.shape[1]
+    upper = lax.rem(ids_ref[3] // half, 2)
+    for c in range(2):
+        for ref, at in ((own_ref, upper), (sent_ref, 1 - upper)):
+            rows = pl.ds(at * half, half)
+            total = refs[c][0, rows].astype(F32) + refs[2 + c][0, rows].astype(F32)
+            ref[c] = total.astype(BF16)
+
+
+def tp_open(ids, kept, arrived):
+    _, tp, rows, width = kept[0].shape
+    outs = [((2, tp // 2, rows, width), BF16)] * 2
+    return run(tp_open_kernel, "tp_open", outs, ids, *kept, *arrived, smem=1)
+
+
+def tp_next_kernel(ids_ref, own_ref, far_ref, kept_ref, sent_ref):
+    half = own_ref.shape[1] // 2
+    if half:
+        upper = lax.rem(ids_ref[3] // half, 2)
+        for c in range(2):
+            for ref, at in ((kept_ref, upper), (sent_ref, 1 - upper)):
+                rows = pl.ds(at * half, half)
+                total = own_ref[c, rows].astype(F32) + far_ref[c, rows].astype(F32)
+                ref[c] = total.astype(BF16)
+    else:
+        for ref, at in ((kept_ref, ids_ref[0]), (sent_ref, 1 - ids_ref[0])):
+            total = own_ref[at, 0].astype(F32) + far_ref[at, 0].astype(F32)
+            ref[...] = total.astype(ref.dtype)
+
+
+def tp_next(ids, own, far):
+    _, tp, rows, width = own.shape
+    outs = [((2, tp // 2, rows, width), BF16)] * 2
+    if tp == 1:
+        outs = [((rows, width), F32), ((rows, width), BF16)]
+    return run(tp_next_kernel, "tp_next", outs, ids, own, far, smem=1)
+
+
+def core_last_kernel(ids_ref, own_ref, far_ref, *outs):
+    second = ids_ref[0] == 1
+    half = own_ref.shape[1] // len(outs)
+    for m, out_ref in enumerate(outs):
+        lanes = slice(m * half, (m + 1) * half)
+        own, far = own_ref[:, lanes], far_ref[:, lanes].astype(F32)
+        out_ref[:, :half] = jnp.where(second, far, own)
+        out_ref[:, half:] = jnp.where(second, own, far)
+
+
+def core_last(ids, own, far, count):
+    outs = [((own.shape[0], 2 * own.shape[1] // count), F32)] * count
+    return run(core_last_kernel, "core_last", outs, ids, own, far, smem=1)
+
+
 def stacked(refs):
-    return jnp.concatenate([r[...].reshape(-1, r.shape[-1]) for r in refs], 0)
+    local = D // (4 * refs[0].shape[0])
+    return jnp.concatenate([r[:, :local].reshape(-1, r.shape[-1]) for r in refs], 0)
 
 
 def heads_of(refs, start, stop):
@@ -314,6 +382,88 @@
     return jnp.where(second, options[1], options[0])
 
 
+def grid_places():
+    rows, ctxs = lax.axis_size("row"), lax.axis_size("ctx")
+    return [(c, b, a) for c in range(2) for b in range(ctxs) for a in range(rows)]
+
+
+def across(value, ids_ref, source, target):
+    grid, rows = grid_places(), lax.axis_size("row")
+    width = D // len(grid)
+    value = block_order(value, source, grid, width)
+    blocks = [value[:, k * width : (k + 1) * width] for k in range(len(grid))]
+    flags = [((ids_ref[1] & m) != 0, m) for m in bits_of("row")]
+    flags += [((ids_ref[2] & m) != 0, m * rows) for m in bits_of("ctx")]
+    for flag, mask in flags:
+        blocks = [jnp.where(flag, blocks[i ^ mask], blocks[i]) for i in range(len(blocks))]
+    return block_order(jnp.concatenate(blocks, 1), grid, target, width)
+
+
+def arrive_kernel(ids_ref, inputs_ref, near_ref, wide_ref):
+    near = across(inputs_ref[0].astype(F32), ids_ref, natural_places(), stream_places())
+    near_ref[...] = near.astype(BF16)
+    wide_ref[...] = by_core(near, "in", ids_ref[0] == 1).astype(BF16)
+
+
+def arrive(ids, inputs):
+    shape = inputs.shape[1:]
+    return run(arrive_kernel, "arrive", [(shape, BF16), (shape, BF16)], ids, inputs, smem=1)
+
+
+SMALL = 64
+
+
+def pack_kernel(count, weight_ref, *refs):
+    out_ref, wide = refs[count:]
+    local = weight_ref.shape[0]
+    out_ref[:local] = weight_ref[...]
+    wide[...] = jnp.zeros(wide.shape, F32)
+    start = 0
+    for ref in refs[:count]:
+        rows, width = ref.shape
+        wide[start : start + rows, :width] = ref[...].astype(F32)
+        start += rows
+    for k in range(out_ref.shape[1] // PAIR):
+        lanes = slice(k * PAIR, (k + 1) * PAIR)
+        out_ref[local:, lanes] = wide[8 * k : 8 * k + 8].astype(BF16)
+
+
+def pack_below(weight, values):
+    shape = (weight.shape[0] + 8, weight.shape[1])
+    return run(
+        functools.partial(pack_kernel, len(values)), "pack_below", [(shape, BF16)],
+        weight, *values,
+        scratch=[pltpu.VMEM((SMALL, PAIR), F32)],
+    )[0]
+
+
+def unpack_kernel(ids_ref, *refs):
+    chunks, out_ref = refs[:4], refs[4]
+    second = ids_ref[0] == 1
+    half = out_ref.shape[0] // 2
+    for k in range(out_ref.shape[0]):
+        for c in range(2):
+            own, other = chunks[2 * c + k // half], chunks[2 * (1 - c) + k // half]
+            value = jnp.where(second, other[k % half], own[k % half])
+            for m in range(SMALL // 8):
+                out_ref[k, c, 8 * m : 8 * m + 8] = value[:, m * PAIR : (m + 1) * PAIR]
+
+
+def unpack_below(ids, chunks, local):
+    blocks, _, width = chunks[0].shape
+    spec = pl.BlockSpec((blocks, 8, width), lambda step: (0, local // 8, 0))
+    shape = (2 * blocks, 2, SMALL, PAIR)
+    return pl.pallas_call(
+        unpack_kernel,
+        grid=(1,),
+        in_specs=[SMEM, *[spec] * 4],
+        out_specs=whole(shape),
+        out_shape=jax.ShapeDtypeStruct(shape, BF16),
+        compiler_params=PARAMS,
+        name="unpack_below",
+    )(ids, *chunks)
+
+
 def normal_of(stream):
     centre = stream - jnp.mean(stream, axis=-1, keepdims=True)
     inverse = lax.rsqrt(jnp.mean(centre * centre, axis=-1, keepdims=True) + EPSILON)
@@ -329,10 +479,16 @@
     return total
 
 
-def back_through(upstream, normal, inverse, gain, grads_ref):
+def back_through(upstream, normal, inverse, gain, ids_ref, grads_ref):
     scaled = upstream * gain
-    grads_ref[0:1] = jnp.sum(upstream * normal, axis=0, keepdims=True)
-    grads_ref[1:2] = jnp.sum(upstream, axis=0, keepdims=True)
+    grads = jnp.concatenate(
+        [
+            jnp.sum(upstream * normal, axis=0, keepdims=True),
+            jnp.sum(upstream, axis=0, keepdims=True),
+        ],
+        0,
+    )
+    grads_ref[...] = across(grads, ids_ref, stream_places(), natural_places())
     return inverse * (
         scaled
         - jnp.mean(scaled, axis=-1, keepdims=True)
@@ -372,10 +528,13 @@
     pieces, stream_ref, up_ref, norm_ref = refs[:count], *refs[count : count + 3]
     result_ref, back_ref, branch_ref, grads_ref = refs[count + 3 :]
     second = core_ref[0] == 1
+    upstream = across(up_ref[0].astype(F32), core_ref, natural_places(), stream_places())
     total = by_core(summed(pieces), "out", second, inverse=True)
     normal, inverse = normal_of(stream_ref[...] + 0.5 * total)
-    result_ref[...] = (normal * norm_ref[0:1] + norm_ref[1:2]).astype(BF16)
-    back = back_through(up_ref[...].astype(F32), normal, inverse, norm_ref[0:1], grads_ref)
+    result = normal * norm_ref[0:1] + norm_ref[1:2]
+    result = across(result, core_ref, stream_places(), natural_places())
+    result_ref[0] = result.astype(BF16)
+    back = back_through(upstream, normal, inverse, norm_ref[0:1], core_ref, grads_ref)
     back_ref[...] = back
     branch_ref[...] = by_core(0.5 * back, "out", second).astype(BF16)
 
@@ -385,7 +544,7 @@
     return run(
         functools.partial(turn_kernel, len(pieces)),
         "turn",
-        [(shape, BF16), (shape, F32), (shape, BF16), ((2, D), F32)],
+        [((1, *shape), BF16), (shape, F32), (shape, BF16), ((2, D), F32)],
         core,
         *pieces,
         stream,
@@ -397,13 +556,17 @@
 
 def return_kernel(count, scale, source, target, core_ref, *refs):
     pieces, stream_ref, up_ref, norm_ref = refs[:count], *refs[count : count + 3]
-    back_ref, branch_ref, grads_ref = refs[count + 3 :]
+    back_ref, grads_ref = refs[count + 3 : count + 5]
+    branch_ref = refs[-1]
     second = core_ref[0] == 1
     total = summed(pieces)
     if source:
         total = by_core(total, source, second, inverse=True)
     normal, inverse = normal_of(stream_ref[...].astype(F32))
-    back = up_ref[...] + back_through(total, normal, inverse, norm_ref[0:1], grads_ref)
+    back = up_ref[...] + back_through(total, normal, inverse, norm_ref[0:1], core_ref, grads_ref)
+    if scale is None:
+        back_ref[0] = across(back, core_ref, stream_places(), natural_places())
+        return
     back_ref[...] = back
     branch = scale * back
     if target:
@@ -413,10 +576,13 @@
 
 def returning(core, pieces, stream, upstream, norm, scale, source, target):
     shape = stream.shape
+    outs = [(shape, F32), ((2, D), F32), (shape, BF16)]
+    if scale is None:
+        outs = [((1, *shape), F32), ((2, D), F32)]
     return run(
         functools.partial(return_kernel, len(pieces), scale, source, target),
         "returning",
-        [(shape, F32), (shape, BF16), ((2, D), F32)],
+        outs,
         core,
         *pieces,
         stream,
@@ -437,14 +603,14 @@
     ins, outs = refs[:4], refs[4:8]
     before_ref, active_ref, branch_ref = refs[8:]
     before = product(rows_ref[...], stacked(ins))
-    before_ref[...] = before
+    before_ref[...] = before.astype(BF16)
     active = (before * jax.nn.sigmoid(before)).astype(BF16)
     active_ref[...] = active
     branch_ref[...] = product_nt(active, stacked(outs)).astype(BF16)
 
 
 def ffn_outs(height, width):
-    return [((height, width), F32), ((height, width), BF16), ((height, D), BF16)]
+    return [((height, width), BF16), ((height, width), BF16), ((height, D), BF16)]
 
 
 def ffn_first(wide, norm, ins, outs):
@@ -466,7 +632,7 @@
     ins, outs = refs[:4], refs[4:8]
     d_before_ref, branch_ref = refs[8:]
     d_active = product(rows_ref[...], stacked(outs))
-    d_before = (d_active * silu_slope(before_ref[...])).astype(BF16)
+    d_before = (d_active * silu_slope(before_ref[...].astype(F32))).astype(BF16)
     d_before_ref[...] = d_before
     branch_ref[...] = product_nt(d_before, stacked(ins)).astype(BF16)
 
@@ -921,21 +1087,6 @@
     )[0]
 
 
-def norm_grads_settle(grads, second):
-    rows = lax.axis_size("row")
-    width = grads.shape[1] // len(stream_places())
-    where = {place: k for k, place in enumerate(stream_places())}
-    cut = lambda p: grads[:, where[p] * width : (where[p] + 1) * width]
-    order = [(b, a) for b in range(lax.axis_size("ctx")) for a in range(rows)]
-    halves = [jnp.stack([cut((c, b, a)) for b, a in order], 0) for c in range(2)]
-    own = jnp.where(second, halves[1], halves[0])
-    total = own + swap_core(jnp.where(second, halves[0], halves[1]))
-    for axis, mask in stages_of(A_AXES)[::-1]:
-        count = total.shape[0] // 2
-        total = total[:count] + partner(total[count:], axis, mask)
-    return total[0]
-
-
 def body(
     inputs,
     cotangent,
@@ -958,35 +1109,38 @@
 ):
     rows, ctxs, tp = lax.axis_size("row"), lax.axis_size("ctx"), lax.axis_size("tp")
     second = lax.axis_index("core") == 1
-    core = lax.axis_index("core").reshape(1).astype(jnp.int32)
+    core = jnp.stack([lax.axis_index(axis) for axis in ("core", "row", "ctx", "tp")])
+    core = core.astype(jnp.int32)
     local = ffn1_in.shape[0]
     height = inputs.shape[1]
     first = (lax.axis_index("ctx") * tp + lax.axis_index("tp")) * height
+    attn_shares = core_shares(
+        [qkv_weight[:, 0], qkv_weight[:, 1], qkv_weight[:, 2], attn_out], second
+    )
+    near, rows_in = arrive(core, inputs)
+    small = [norm_gains.T, norm_biases.T, depthwise.T, conv_gain[None], conv_bias[None], distance]
+    joined = gather_first([pack_below(ffn1_in, small), ffn1_out])
+    attn_half = tp_first(attn_shares)
+    joined, attn_half, wide_inputs = tied(joined, attn_half, widen_tp(rows_in))
+    halves = gather_last(joined)
+    attn_rows = tp_rest(attn_half)
+    conv_shares = core_shares([glu_in[:, 0], glu_in[:, 1], conv_out], second)
+    conv_shares, attn_rows, halves = tied(conv_shares, attn_rows, halves)
+    one_in, one_out = ffn_weights(halves)
+    conv_half = tp_first(conv_shares)
+    w_attn = gather_last(gather_first(attn_rows))
+    conv_rows, w_attn = tied(tp_rest(conv_half), w_attn)
+    w_conv = gather_last(gather_first(conv_rows))
+    two_rows, w_conv = tied([ffn2_in, ffn2_out], w_conv)
+    two_in, two_out = ffn_weights(gather_last(gather_first(two_rows)))
+
     lens = widen_core(lengths)
     frame_ids = first + jnp.arange(height, dtype=jnp.int32)
     live = (frame_ids[None, :] < lens[:, None]).astype(F32).reshape(2 * height, 1)
 
-    near = from_natural(inputs[0])
-    wide_inputs = widen_early(to_ffn(near, "in", second))
-    one_in, one_out = ffn_weight(ffn1_in, A_AXES), ffn_weight(ffn1_out, B_AXES)
-
-    padded = lambda v: jnp.pad(v, ((0, 0), (0, PAIR - v.shape[1])))
     table_rows, width = distance.shape[0], conv_gain.shape[0]
-    small = jnp.concatenate(
-        [
-            padded(norm_gains.T),
-            padded(norm_biases.T),
-            padded(depthwise.T),
-            padded(conv_gain[None]),
-            padded(conv_bias[None]),
-            padded(distance),
-        ],
-        0,
-    )
-    cube = jnp.stack([small, swap_core(small)], 0)[None]
-    for axis, mask in stages_of(A_AXES):
-        cube = jnp.concatenate([cube, partner(cube, axis, mask)], 0)
-    take = lambda c, k: jnp.where(second, cube[k, 1 - c], cube[k, c])
+    cube = unpack_below(core, one_in, local)
+    take = lambda c, k: cube[k, c]
     norms = jnp.concatenate(
         [take(c, b * rows + a)[:10, :local] for c, b, a in stream_places()], 1
     ).astype(F32)
@@ -995,7 +1149,9 @@
         crossed([take(c, k)[10:] for k in range(rows * ctxs)]) for c in range(2)
     ]
     natural = [blocks[c][b * rows + a] for c, b, a in natural_places()]
-    table_all = jnp.concatenate([n[KERNEL + 2 :, :SPAN] for n in natural], 0)
+    table_all = jnp.concatenate(
+        [n[KERNEL + 2 : KERNEL + 2 + table_rows, :SPAN] for n in natural], 0
+    )
     conv_small = jnp.concatenate([n[: KERNEL + 2, :width] for n in natural], 1)
     half = conv_small.shape[1] // 2
     conv_small = jnp.where(second, conv_small[:, half:], conv_small[:, :half])
@@ -1003,12 +1159,6 @@
         conv_small = tp_joined(conv_small, partner(conv_small, "tp", mask), mask, 1)
     conv_small = conv_small.astype(F32)
     taps, affine = conv_small[:KERNEL], conv_small[KERNEL:]
-
-    w_attn = core_weight(
-        core_shares([qkv_weight[:, 0], qkv_weight[:, 1], qkv_weight[:, 2], attn_out], second)
-    )
-    w_conv = core_weight(core_shares([glu_in[:, 0], glu_in[:, 1], conv_out], second))
-    two_in, two_out = ffn_weight(ffn2_in, A_AXES), ffn_weight(ffn2_out, B_AXES)
 
     selector = (jnp.arange(SPAN, dtype=jnp.int32)[:, None] == buckets[None, :]).astype(BF16)
     rel = product(table_all, selector).astype(BF16)
@@ -1042,14 +1192,15 @@
     hidden3 = widen_tp(hidden3)
     before3, active3, branch = ffn_forward(hidden3, two_in, two_out)
     result, d_stream, d_branch, grads4 = turn(
-        core, [exchange_tp(branch)], stream3, from_natural(cotangent[0]), norm[4]
+        core, [exchange_tp(branch)], stream3, cotangent, norm[4]
     )
 
     d_branch = widen_tp(d_branch)
     d_before, branch = ffn_backward(d_branch, before3, two_in, two_out)
-    grad_in, grad_out = ffn_grads(hidden3, d_before, d_branch, active3, two_in[0])
-    grad_two_in, grad_two_out = ffn_settle(grad_in, A_AXES), ffn_settle(grad_out, B_AXES)
-    d_stream, d_branch, grads3 = returning(
+    two_own, two_far = settle_open(
+        ffn_halves(*ffn_grads(hidden3, d_before, d_branch, active3, two_in[0]))
+    )
+    d_stream, grads3, d_branch = returning(
         core, [exchange_tp(branch)], stream3, d_stream, norm[3], 1.0, "in", None
     )
 
@@ -1058,67 +1209,90 @@
     d_mixed, d_own, d_earlier = unmix_channels(
         scaled, totals, swap_core(totals), mixed, sums, other, taps
     )
+    two_own, two_far = settle_close(two_own, two_far)
     later = along(d_earlier, -1)
     d_value, d_gate, branch = gate_back(d_own, later, value_half, logistic, live, w_conv)
-    grads = core_grads(hidden2, d_branch, (d_value, d_gate), active_conv, w_conv[0])
-    tap_grads = tap_grads_of(d_mixed, gated, earlier)
-    grad_value, grad_gate, grad_w_conv = core_settle(grads, second, 3)
-    d_stream, d_branch, grads2 = returning(
+    conv_grads = core_grads(hidden2, d_branch, (d_value, d_gate), active_conv, w_conv[0])
+    conv_own, conv_far = settle_open(conv_grads)
+    d_stream, grads2, d_branch = returning(
         core, exchange_core(branch), stream2, d_stream, norm[2], 1.0, None, None
     )
 
     d_branch = widen_core(d_branch)
+    grad_two_in, grad_two_out = sum_pairs(two_own, two_far, F32, ffn2_in.shape)
     d_query, d_own, d_left, d_right, d_table = attend_back(
         first_ref, lens, d_branch, heads, left, right, rel, w_attn, chance
     )
-    d_key, d_val, branch = heads_in(d_query, d_own, along(d_left, -1), along(d_right, 1), w_attn)
-    grads = core_grads(hidden1, d_branch, (d_query, d_key, d_val), context, w_attn[0])
-    grad_q, grad_k, grad_v, grad_w_attn = core_settle(grads, second, 4)
-    d_stream, d_branch, grads1 = returning(
+    from_next = along(d_left, -1)
+    d_key, d_val, branch = heads_in(d_query, d_own, from_next, along(d_right, 1), w_attn)
+    conv_own, conv_far = settle_close(conv_own, conv_far)
+    attn_grads = core_grads(hidden1, d_branch, (d_query, d_key, d_val), context, w_attn[0])
+    d_stream, grads1, d_branch = returning(
         core, exchange_core(branch), stream1, d_stream, norm[1], 0.5, None, "out"
     )
-
-    d_branch = widen_tp(d_branch)
+    d_branch, attn_grads = tied(d_branch, attn_grads)
+    attn_own, attn_far = settle_open(attn_grads)
+
+    d_branch, attn_far = tied(widen_tp(d_branch), attn_far)
+    grad_value, grad_gate, grad_w_conv = core_finish(core, conv_own, conv_far, 3)
     d_before, branch = ffn_backward(d_branch, before0, one_in, one_out)
-    grad_in, grad_out = ffn_grads(hidden0, d_before, d_branch, active0, one_in[0])
-    grad_one_in, grad_one_out = ffn_settle(grad_in, A_AXES), ffn_settle(grad_out, B_AXES)
-    d_stream, _, grads0 = returning(
-        core, [exchange_tp(branch)], near, d_stream, norm[0], 1.0, "in", None
-    )
+    one_grads = ffn_grads(hidden0, d_before, d_branch, active0, one_out[0])
+    one_grads, attn_far = tied(one_grads, attn_far)
+    attn_own, attn_far = settle_close(attn_own, attn_far)
+    one_own, one_far = settle_open(ffn_halves(*one_grads))
+    pieces = exchange_tp(branch)
+    grad_q, grad_k, grad_v, grad_w_attn = core_finish(core, attn_own, attn_far, 4)
+    input_grad, grads0 = returning(
+        core, [pieces], near, d_stream, norm[0], None, "in", None
+    )
+    one_own, one_far = settle_close(one_own, one_far)
+    grad_one_in, grad_one_out = sum_pairs(one_own, one_far, F32, ffn1_in.shape)
 
     d_rel = (d_table[:HD] + d_table[HD:])[:, :SPAN]
     grad_table = jnp.dot(d_rel, selector.astype(F32).T, precision=lax.Precision.HIGHEST)
-    early = jnp.concatenate([tap_grads, affine_grads], 0)
-    for mask in bits_of("tp")[::-1]:
-        kept, sent = tp_halves(early, mask, 1)
-        early = kept + partner(sent, "tp", mask)
-    early = jnp.concatenate([early, padded(grad_table)], 0)
-    for axis, mask in stages_of(A_AXES):
-        early = early + partner(early, axis, mask)
-    far_early = swap_core(early)
-    grad_table = (early + far_early)[KERNEL + 2 :, :SPAN]
+    grad_table = jnp.pad(grad_table, ((0, 0), (0, PAIR - SPAN)))
+    wide = tp * half
+    fold_rows = lambda v: jnp.concatenate(
+        [v[:, k : k + wide] for k in range(0, v.shape[1], wide)], 0
+    )
+    tap_grads = tap_grads_of(d_mixed, gated, earlier)
+    packed = jnp.concatenate(
+        [
+            tap_grads,
+            affine_grads,
+            grad_table.reshape(-1, wide),
+            *[fold_rows(g) for g in (grads4, grads3, grads2, grads1, grads0)],
+        ],
+        0,
+    )
+    for axis, mask in [*stages_of(A_AXES), *stages_of(("tp",))]:
+        packed = packed + partner(packed, axis, mask)
+    far_packed = swap_core(packed)
+    total = (packed + far_packed)[KERNEL + 2 :]
+    table_size = grad_table.size // wide
+    grad_table = total[:table_size].reshape(HD, PAIR)[:, :SPAN]
+    norm_grads = total[table_size:].reshape(5, D // wide, 2, wide)
+    norm_grads = norm_grads.transpose(0, 2, 1, 3).reshape(10, D)[::-1]
     conv_cut = jnp.concatenate(
-        [jnp.where(second, far_early, early), jnp.where(second, early, far_early)], 1
-    )[: KERNEL + 2]
+        [
+            jnp.where(second, far_packed, packed)[: KERNEL + 2].reshape(-1, tp, half),
+            jnp.where(second, packed, far_packed)[: KERNEL + 2].reshape(-1, tp, half),
+        ],
+        2,
+    )
     place = (lax.axis_index("row") * 2 + lax.axis_index("core")) * ctxs + lax.axis_index("ctx")
+    conv_cut = lax.dynamic_index_in_dim(conv_cut, lax.axis_index("tp"), 1, keepdims=False)
     conv_cut = lax.dynamic_slice_in_dim(conv_cut, place * width, width, 1)
     grad_table = lax.dynamic_slice_in_dim(grad_table, place * table_rows, table_rows, 0)
-
-    norm_grads = jnp.concatenate([grads0, grads1, grads2, grads3, grads4], 0)
-    norm_grads = norm_grads_settle(norm_grads, second)
-    final = jnp.concatenate([padded(norm_grads), padded(grad_table)], 0)
-    for mask in bits_of("tp"):
-        final = final + partner(final, "tp", mask)
-    norm_grads = final[:10, :local].reshape(5, 2, local)
-    grad_table = final[10:, :SPAN]
+    norm_grads = lax.dynamic_slice_in_dim(norm_grads, place * local, local, 1)
 
     return (
-        to_natural(result)[None],
-        to_natural(d_stream)[None],
+        result,
+        input_grad,
         grad_one_in,
         grad_one_out,
-        norm_grads[:, 0].T,
-        norm_grads[:, 1].T,
+        norm_grads[1::2].T,
+        norm_grads[::2].T,
         jnp.stack([grad_q, grad_k, grad_v], 1),
         grad_w_attn,
         grad_table,

time: 535 us -> 483 us (0.903)
  waiting for transfers between devices: 183 us -> 111 us
  other arithmetic: 60.4 us -> 13.8 us
  blocking collectives: 60.4 us -> 104 us
  local copies, waits for them, and re-layouts: 50.1 us -> 64.9 us
  Pallas kernels: 64.1 us -> 78.2 us
    ppermute x86 -> x78, waiting for transfers between devices: 150 us -> 75.4 us  [partner(): return lax.ppermute(value, axis, [(i, i ^ mask) for i in range(count)])]
    all_gather x3 -> x4, blocking collectives: 60.4 us -> 84.9 us  [widen_tp(): return lax.all_gather(rows, 'tp', axis=0, tiled=True)]
    all_to_all x0 -> x1, blocking collectives: none -> 19.5 us  [exchange_tp(): return lax.all_to_all(pieces, 'tp', 0, 0)]
    add x25 -> x5, other arithmetic: 16.2 us -> 1.75 us  [the longest x4 1.73 us: body(): packed = packed + partner(packed, axis, mask)]
    unnamed x31 -> x4, other arithmetic: 14.5 us -> 0.05 us
    pallas_call x27 -> x50, Pallas kernels: 64.1 us -> 78.2 us  [the longest x49 77.3 us: run(): pl.pallas_call(kernel, grid=(1,), in_specs=[SMEM] * smem + [whole(a.shape...]
    ppermute x3 -> x0, starting transfers between devices: 8.15 us -> none  [widen_early(): lax.ppermute(rows, 'tp', [(i, i ^ k) for i in range(count)])]
    unnamed x409 -> x435, local copies, waits for them, and re-layouts: 37.6 us -> 45.1 us
  transfers between devices with their start and end apart: 99 -> 87, of which waited for: 34 -> 34; matrix products, arithmetic and copies ran while one was open for 13% -> 7% of each run, Pallas kernels for 10% -> 12%
where the time goes in v4:
time: 483 us; the launch traced here: 474 us
  waiting for transfers between devices  111 us (23%)
  blocking collectives  104 us (22%)
  starting transfers between devices  96.2 us (20%)
  Pallas kernels  78.2 us (16%)
  local copies, waits for them, and re-layouts  64.9 us (13%)
  other arithmetic  13.8 us (3%)
    all_gather x4, blocking collectives, widen_tp(): return lax.all_gather(rows, 'tp', axis=0, tiled=True)  84.9 us
    pallas_call x49, Pallas kernels, run(): pl.pallas_call(kernel, grid=(1,), in_specs=[SMEM] * smem + [whole(a.shape...  77.3 us
    ppermute x78, waiting for transfers between devices, partner(): return lax.ppermute(value, axis, [(i, i ^ mask) for i in range(count)])  75.4 us
    ppermute x78, starting transfers between devices, partner(): return lax.ppermute(value, axis, [(i, i ^ mask) for i in range(count)])  69.2 us
    unnamed x435, local copies, waits for them, and re-layouts  45.1 us
    all_to_all x3, waiting for transfers between devices, exchange_tp(): return lax.all_to_all(pieces, 'tp', 0, 0)  19.6 us
    all_to_all x1, blocking collectives, exchange_tp(): return lax.all_to_all(pieces, 'tp', 0, 0)  19.5 us
    ppermute x6, waiting for transfers between devices, along(): return lax.ppermute(value, ('ctx', 'tp'), pairs)  15.9 us
  transfers between devices with their start and end apart: 87, of which 34 were waited for; matrix products, arithmetic and copies ran while one was open for 7% of the time, Pallas kernels for 12%

profile of v4, /device:TPU:0, one launch (start us, length us, event | category | flops | bytes accessed | tf_op | source)
XLA Modules:
  0.0 473.9 jit_solution(12180546483352997056)
XLA Ops:
  13.5 2.7 collective-permute-start.4
  16.2 28.6 %all_gather.12.wide_ref = bf16[384,1024]{1,0:T(8,128)(2,1)} all-gather(bf16[96,1024]{1,0:T(8,128)(2,1)S(1)} %get-tuple-element.200), channel_id=1, replica_groups=mesh['row'=2,'core'=2,'ctx'=2,'tp'=4] {'tp'}, dimensions={0}, use_global_device_ids=true | all-gather | bytes 983040 | tf_op jit(solution)/shard_map/all_gather | solution.py:215
  48.2 10.1 %collective-permute-done.6 = bf16[2,2,1,128,512]{4,3,2,1,0:T(8,128)(2,1)S(1)} collective-permute-done((bf16[2,2,1,128,512]{4,3,2,1,0:T(8,128)(2,1)S(1)}, bf16[2,2,1,128,512]{4,3,2,1,0:T(8,128)(2,1)S(1)}, u32[]{:S(2)}, u32[]{:S(2)}) %collective-permute-start.6) | collective-permute-done | bytes 524320 | tf_op jit(solution)/shard_map/ppermute | solution.py:108
  65.3 5.0 %collective-permute-done.14 = bf16[2,1,1,128,384]{3,4,0,2,1:T(8,128)(2,1)} collective-permute-done((bf16[2,1,1,128,384]{3,4,0,2,1:T(8,128)(2,1)S(1)}, bf16[2,1,1,128,384]{3,4,0,2,1:T(8,128)(2,1)}, u32[]{:S(2)}, u32[]{:S(2)}) %collective-permute-start.14) | collective-permute-done | bytes 196640 | tf_op jit(solution)/shard_map/ppermute | solution.py:108
  86.4 4.0 ffn_first.1
  94.1 4.2 all-to-all-start
  115.8 2.9 all-to-all-done.refs_0_
  128.1 3.6 collective-permute-start.20
  134.2 6.2 %collective-permute-done.21.right_ref = bf16[2,16,1024]{2,1,0:T(8,128)(2,1)S(1)} collective-permute-done((bf16[2,16,1024]{2,1,0:T(8,128)(2,1)S(1)}, bf16[2,16,1024]{2,1,0:T(8,128)(2,1)S(1)}, u32[]{:S(2)}, u32[]{:S(2)}) %collective-permute-start.21) | collective-permute-done | bytes 65568 | tf_op jit(solution)/shard_map/ppermute | solution.py:211
  140.5 5.0 %attend.1 = (bf16[192,512]{1,0:T(8,128)(2,1)S(1)}, f32[2,4,192,256]{3,2,1,0:T(8,128)S(1)}, bf16[192,1024]{1,0:T(8,128)(2,1)S(1)}) custom-call(s32[1]{0:T(128)} %bitcast.4.first_ref, s32[2]{0:T(128)S(1)} %pad_add_fusion.1.lens_ref, bf16[192,512]{1,0:T(8,128)(2,1)S(1)} %get-tuple-element.220.q_ref, bf16[192,512]{1,0:T(8,128)(2,1)S(1)} %get-tuple-element.221.k_ref, ...), custom_call_target="tpu_custom_call" | custom-call | tf_op jit(solution)/shard_map/attend/pallas_call | solution.py:244
  172.0 20.5 %all_gather.13.rows_ref.hidden_ref = bf16[384,1024]{1,0:T(8,128)(2,1)S(1)} all-gather(bf16[96,1024]{1,0:T(8,128)(2,1)S(1)} %get-tuple-element.238), channel_id=1, replica_groups=mesh['row'=2,'core'=2,'ctx'=2,'tp'=4] {'tp'}, dimensions={0}, use_global_device_ids=true | all-gather | bytes 983040 | tf_op jit(solution)/shard_map/all_gather | solution.py:215
  197.2 4.2 all-to-all-start.1
  202.7 16.8 %all-to-all-done.1.refs_0_ = bf16[4,96,1024]{2,1,0:T(8,128)(2,1)} async-done(((bf16[4,96,1024]{2,1,0:T(8,128)(2,1)}), bf16[4,96,1024]{2,1,0:T(8,128)(2,1)}, u32[]{:S(2)}, u32[]{:S(2)}) %all-to-all-start.1) | async-done | bytes 786464 | tf_op jit(solution)/shard_map/all_to_all | solution.py:223
  225.1 17.7 %all_gather.14.rows_ref.up_ref = bf16[384,1024]{1,0:T(8,128)(2,1)S(1)} all-gather(bf16[96,1024]{1,0:T(8,128)(2,1)S(1)} %get-tuple-element.246), channel_id=1, replica_groups=mesh['row'=2,'core'=2,'ctx'=2,'tp'=4] {'tp'}, dimensions={0}, use_global_device_ids=true | all-gather | bytes 983040 | tf_op jit(solution)/shard_map/all_gather | solution.py:215
  250.1 19.5 %all_to_all.20.refs_0_ = bf16[4,96,1024]{2,1,0:T(8,128)(2,1)S(1)} all-to-all(bf16[4,96,1024]{2,1,0:T(8,128)(2,1)S(1)} %bitcast.146), channel_id=1, replica_groups=mesh['row'=2,'core'=2,'ctx'=2,'tp'=4] {'tp'}, dimensions={0} | all-to-all | bytes 1572864 | tf_op jit(solution)/shard_map/all_to_all | solution.py:223
  278.5 6.1 %collective-permute-done.43.later_ref = f32[2,32,512]{2,1,0:T(8,128)S(1)} collective-permute-done((f32[2,32,512]{2,1,0:T(8,128)S(1)}, f32[2,32,512]{2,1,0:T(8,128)S(1)}, u32[]{:S(2)}, u32[]{:S(2)}) %collective-permute-start.43) | collective-permute-done | bytes 131104 | tf_op jit(solution)/shard_map/ppermute | solution.py:211
  289.8 7.5 %attend_back.1 = (bf16[192,512]{1,0:T(8,128)(2,1)S(1)}, f32[2,192,512]{2,1,0:T(8,128)S(1)}, bf16[2,2,64,512]{3,2,1,0:T(8,128)(2,1)S(1)}, bf16[2,2,16,512]{3,2,1,0:T(8,128)(2,1)S(1)}, f32[128,128]{1,0:T(8,128)S(1)}) custom-call(s32[1]{0:T(128)} %bitcast.4.first_ref, s32[2]{0:T(128)S(1)} %copy-done.162, ...), custom_call_target="tpu_custom_call" | custom-call | tf_op jit(solution)/shard_map/attend_back/pallas_call | solution.py:244
  298.5 4.8 %collective-permute-start.47 = (bf16[2,2,16,512]{3,2,1,0:T(8,128)(2,1)S(1)}, bf16[2,2,16,512]{3,2,1,0:T(8,128)(2,1)S(1)}, u32[]{:S(2)}, u32[]{:S(2)}) collective-permute-start(bf16[2,2,16,512]{3,2,1,0:T(8,128)(2,1)S(1)} %get-tuple-element.264), channel_id=1, source_target_pairs={{0,1},{1,2},{2,3},{3,4},{4,5},{5,6},{6,7},{8,9},{9,10},{10,11},{11... | collective-permute-start | bytes 196616 | tf_op jit(solution)/shard_map/ppermute | solution.py:211
  314.1 8.4 %collective-permute-start.49 = (bf16[2,4,128,512]{3,2,1,0:T(8,128)(2,1)S(1)}, bf16[2,4,128,512]{3,2,1,0:T(8,128)(2,1)S(1)}, u32[]{:S(2)}, u32[]{:S(2)}) collective-permute-start(bf16[2,4,128,512]{3,2,1,0:T(8,128)(2,1)S(1)} %get-tuple-element.276), channel_id=1, source_target_pairs={{0,4},{4,0},{1,5},{5,1},{2,6},{6,2},{3,7},{7,3},{8,12},{12,8},{9,1... | collective-permute-start | bytes 3145736 | tf_op jit(solution)/shard_map/ppermute | solution.py:108
  335.8 18.0 %all_gather.15.rows_ref.up_ref = bf16[384,1024]{1,0:T(8,128)(2,1)S(1)} all-gather(bf16[96,1024]{1,0:T(8,128)(2,1)S(1)} %get-tuple-element.275), channel_id=1, replica_groups=mesh['row'=2,'core'=2,'ctx'=2,'tp'=4] {'tp'}, dimensions={0}, use_global_device_ids=true | all-gather | bytes 983040 | tf_op jit(solution)/shard_map/all_gather | solution.py:215
  353.9 5.0 %ffn_backward.3 = (bf16[384,1024]{1,0:T(8,128)(2,1)S(1)}, bf16[384,1024]{1,0:T(8,128)(2,1)}) custom-call(bf16[384,1024]{1,0:T(8,128)(2,1)S(1)} %all_gather.15.rows_ref.up_ref, bf16[384,1024]{1,0:T(8,128)(2,1)S(1)} %copy-done.95, bf16[2,136,1024]{2,1,0:T(8,128)(2,1)S(1)} %copy-done.12, bf16[2,136,1024]{2,1,0:T(8,128)(2,1)} %collective-permute-done.7.refs_1_, ...), custom_call_target="tpu_custom_call" | custom-call | tf_op jit(solution)/shard_map/ffn_backward/pallas_call | solution.py:244
  359.9 3.9 all-to-all-start.3
  366.1 3.3 ffn_grads.2
  378.7 3.7 collective-permute-done.64.refs_2_
  396.0 2.6 collective-permute-start.66
  408.2 5.0 %collective-permute-done.59 = f32[69,512]{1,0:T(8,128)S(1)} collective-permute-done((f32[69,512]{1,0:T(8,128)S(1)}, f32[69,512]{1,0:T(8,128)S(1)}, u32[]{:S(2)}, u32[]{:S(2)}) %collective-permute-start.59) | collective-permute-done | bytes 141344 | tf_op jit(solution)/shard_map/ppermute | solution.py:108
  413.2 2.6 collective-permute-start.73
  418.2 13.4 %collective-permute-done.66.far_ref = bf16[2,2,128,512]{3,2,1,0:T(8,128)(2,1)S(1)} collective-permute-done((bf16[2,2,128,512]{3,2,1,0:T(8,128)(2,1)}, bf16[2,2,128,512]{3,2,1,0:T(8,128)(2,1)S(1)}, u32[]{:S(2)}, u32[]{:S(2)}) %collective-permute-start.66) | collective-permute-done | bytes 524320 | tf_op jit(solution)/shard_map/ppermute | solution.py:108
  433.3 5.4 %collective-permute-done.73.far_ref = bf16[2,2,128,384]{3,2,1,0:T(8,128)(2,1)S(1)} collective-permute-done((bf16[2,2,128,384]{3,2,1,0:T(8,128)(2,1)S(1)}, bf16[2,2,128,384]{3,2,1,0:T(8,128)(2,1)S(1)}, u32[]{:S(2)}, u32[]{:S(2)}) %collective-permute-start.73) | collective-permute-done | bytes 393248 | tf_op jit(solution)/shard_map/ppermute | solution.py:108
  444.1 9.2 %collective-permute-done.61 = f32[69,512]{1,0:T(8,128)S(1)} collective-permute-done((f32[69,512]{1,0:T(8,128)S(1)}, f32[69,512]{1,0:T(8,128)S(1)}, u32[]{:S(2)}, u32[]{:S(2)}) %collective-permute-start.61) | collective-permute-done | bytes 141344 | tf_op jit(solution)/shard_map/ppermute | solution.py:108
  454.7 3.4 collective-permute-start.62
  462.2 2.6 collective-permute-done.62
  (747 shorter events, 213.3 us)
Async XLA Ops:
  0.6 45.2 %collective-permute-start = (s32[1]{0:T(128)}, s32[1]{0:T(128)}, u32[]{:S(2)}, u32[]{:S(2)}) collective-permute-start(s32[1]{0:T(128)} %param.20), channel_id=1, source_target_pairs={{0,8},{8,0},{1,9},{9,1},{2,10},{10,2},{3,11},{11,3},{4,12},{12,4},... | collective-permute-start | bytes 20 | tf_op jit(solution)/shard_map/ppermute | solution.py:108
  5.7 41.4 %collective-permute-start.5 = (bf16[128,384]{0,1:T(8,128)(2,1)}, bf16[128,384]{0,1:T(8,128)(2,1)}, u32[]{:S(2)}, u32[]{:S(2)}) collective-permute-start(bf16[128,384]{0,1:T(8,128)(2,1)} %bitcast.18), channel_id=1, source_target_pairs={{0,8},{8,0},{1,9},{9,1},{2,10},{10,2},{3,11},{11,3},{4,12},{12,4},... | collective-permute-start | bytes 294920 | tf_op jit(solution)/shard_map/ppermute | solution.py:108
  6.2 38.6 %collective-permute-start.2 = (bf16[1,128,1024]{2,1,0:T(8,128)(2,1)S(1)}, bf16[1,128,1024]{2,1,0:T(8,128)(2,1)S(1)}, u32[]{:S(2)}, u32[]{:S(2)}) collective-permute-start(bf16[1,128,1024]{2,1,0:T(8,128)(2,1)S(1)} %bitcast.147), channel_id=1, source_target_pairs={{0,4},{4,0},{1,5},{5,1},{2,6},{6,2},{3,7},{7,3},{8,12},{12,8},{9,1... | collective-permute-start | bytes 786440 | tf_op jit(solution)/shard_map/ppermute | solution.py:108
  8.9 35.9 %collective-permute-start.1 = (bf16[1,136,1024]{2,1,0:T(8,128)(2,1)S(1)}, bf16[1,136,1024]{2,1,0:T(8,128)(2,1)S(1)}, u32[]{:S(2)}, u32[]{:S(2)}) collective-permute-start(bf16[1,136,1024]{2,1,0:T(8,128)(2,1)S(1)} %bitcast.141), channel_id=1, source_target_pairs={{0,16},{16,0},{1,17},{17,1},{2,18},{18,2},{3,19},{19,3},{4,20},{20... | collective-permute-start | bytes 835592 | tf_op jit(solution)/shard_map/ppermute | solution.py:108
  13.5 32.1 %collective-permute-start.4 = (bf16[2,1,1,128,512]{4,3,2,1,0:T(8,128)(2,1)S(1)}, bf16[2,1,1,128,512]{4,3,2,1,0:T(8,128)(2,1)S(1)}, u32[]{:S(2)}, u32[]{:S(2)}) collective-permute-start(bf16[2,1,1,128,512]{4,3,2,1,0:T(8,128)(2,1)S(1)} %maximum_bitcast_fusion), channel_id=1, source_target_pairs={{0,2},{1,3},{2,0},{3,1},{4,6},{5,7},{6,4},{7,5},{8,10},{9,11},{10,... | collective-permute-start | bytes 786440 | tf_op jit(solution)/shard_map/ppermute | solution.py:108
  63.9 19.0 %collective-permute-start.10 = (bf16[2,136,1024]{2,1,0:T(8,128)(2,1)}, bf16[2,136,1024]{2,1,0:T(8,128)(2,1)}, u32[]{:S(2)}, u32[]{:S(2)}) collective-permute-start(bf16[2,136,1024]{2,1,0:T(8,128)(2,1)} %collective-permute-done.7.refs_1_), channel_id=1, source_target_pairs={{0,8},{8,0},{1,9},{9,1},{2,10},{10,2},{3,11},{11,3},{4,12},{12,4},... | collective-permute-start | bytes 1671176 | tf_op jit(solution)/shard_map/ppermute | solution.py:108
  75.2 27.9 %collective-permute-start.15 = (bf16[2,2,1,128,384]{3,4,0,2,1:T(8,128)(2,1)}, bf16[2,2,1,128,384]{3,4,0,2,1:T(8,128)(2,1)}, u32[]{:S(2)}, u32[]{:S(2)}) collective-permute-start(bf16[2,2,1,128,384]{3,4,0,2,1:T(8,128)(2,1)} %pad_maximum_fusion.3), channel_id=1, source_target_pairs={{0,1},{1,0},{2,3},{3,2},{4,5},{5,4},{6,7},{7,6},{8,9},{9,8},{10,11... | collective-permute-start | bytes 1179656 | tf_op jit(solution)/shard_map/ppermute | solution.py:108
  81.8 25.9 %collective-permute-start.18 = (bf16[2,4,128,512]{3,2,1,0:T(8,128)(2,1)S(1)}, bf16[2,4,128,512]{3,2,1,0:T(8,128)(2,1)S(1)}, u32[]{:S(2)}, u32[]{:S(2)}) collective-permute-start(bf16[2,4,128,512]{3,2,1,0:T(8,128)(2,1)S(1)} %get-tuple-element.216.refs_0_.c0), channel_id=1, source_target_pairs={{0,4},{4,0},{1,5},{5,1},{2,6},{6,2},{3,7},{7,3},{8,12},{12,8},{9,1... | collective-permute-start | bytes 3145736 | tf_op jit(solution)/shard_map/ppermute | solution.py:108
  82.9 25.1 %collective-permute-start.19 = (bf16[2,4,128,512]{3,2,1,0:T(8,128)(2,1)S(1)}, bf16[2,4,128,512]{3,2,1,0:T(8,128)(2,1)}, u32[]{:S(2)}, u32[]{:S(2)}) collective-permute-start(bf16[2,4,128,512]{3,2,1,0:T(8,128)(2,1)S(1)} %get-tuple-element.218.refs_2_.c2), channel_id=1, source_target_pairs={{0,16},{16,0},{1,17},{17,1},{2,18},{18,2},{3,19},{19,3},{4,20},{20... | collective-permute-start | bytes 3145736 | tf_op jit(solution)/shard_map/ppermute | solution.py:108
  94.1 24.6 %all-to-all-start = ((bf16[4,96,1024]{2,1,0:T(8,128)(2,1)}), bf16[4,96,1024]{2,1,0:T(8,128)(2,1)}, u32[]{:S(2)}, u32[]{:S(2)}) async-start(bf16[4,96,1024]{2,1,0:T(8,128)(2,1)} %bitcast.144), calls=%async_computation | async-start | bytes 1572864 | tf_op jit(solution)/shard_map/all_to_all | solution.py:223
  113.0 20.4 %collective-permute-start.29 = (bf16[33,128]{1,0:T(8,128)(2,1)}, bf16[33,128]{1,0:T(8,128)(2,1)}, u32[]{:S(2)}, u32[]{:S(2)}) collective-permute-start(bf16[33,128]{1,0:T(8,128)(2,1)} %maximum_select_fusion), channel_id=1, source_target_pairs={{0,1},{1,0},{2,3},{3,2},{4,5},{5,4},{6,7},{7,6},{8,9},{9,8},{10,11... | collective-permute-start | bytes 25352 | tf_op jit(solution)/shard_map/ppermute | solution.py:108
  122.6 23.6 %collective-permute-start.26 = (bf16[2,4,128,384]{3,2,1,0:T(8,128)(2,1)S(1)}, bf16[2,4,128,384]{3,2,1,0:T(8,128)(2,1)S(1)}, u32[]{:S(2)}, u32[]{:S(2)}) collective-permute-start(bf16[2,4,128,384]{3,2,1,0:T(8,128)(2,1)S(1)} %get-tuple-element.229.refs_0_), channel_id=1, source_target_pairs={{0,4},{4,0},{1,5},{5,1},{2,6},{6,2},{3,7},{7,3},{8,12},{12,8},{9,1... | collective-permute-start | bytes 2359304 | tf_op jit(solution)/shard_map/ppermute | solution.py:108
  124.2 22.0 %collective-permute-start.27 = (bf16[2,4,128,384]{3,2,1,0:T(8,128)(2,1)S(1)}, bf16[2,4,128,384]{3,2,1,0:T(8,128)(2,1)S(1)}, u32[]{:S(2)}, u32[]{:S(2)}) collective-permute-start(bf16[2,4,128,384]{3,2,1,0:T(8,128)(2,1)S(1)} %get-tuple-element.231.refs_2_), channel_id=1, source_target_pairs={{0,16},{16,0},{1,17},{17,1},{2,18},{18,2},{3,19},{19,3},{4,20},{20... | collective-permute-start | bytes 2359304 | tf_op jit(solution)/shard_map/ppermute | solution.py:108
  166.7 25.9 %collective-permute-start.36 = (bf16[2,128,1024]{2,1,0:T(8,128)(2,1)S(1)}, bf16[2,128,1024]{2,1,0:T(8,128)(2,1)S(1)}, u32[]{:S(2)}, u32[]{:S(2)}) collective-permute-start(bf16[2,128,1024]{2,1,0:T(8,128)(2,1)S(1)} %get-tuple-element.241.refs_0_), channel_id=1, source_target_pairs={{0,8},{8,0},{1,9},{9,1},{2,10},{10,2},{3,11},{11,3},{4,12},{12,4},... | collective-permute-start | bytes 1572872 | tf_op jit(solution)/shard_map/ppermute | solution.py:108
  166.9 25.6 %collective-permute-start.39 = (bf16[2,128,1024]{2,1,0:T(8,128)(2,1)S(1)}, bf16[2,128,1024]{2,1,0:T(8,128)(2,1)S(1)}, u32[]{:S(2)}, u32[]{:S(2)}) collective-permute-start(bf16[2,128,1024]{2,1,0:T(8,128)(2,1)S(1)} %get-tuple-element.242.refs_4_), channel_id=1, source_target_pairs={{0,8},{8,0},{1,9},{9,1},{2,10},{10,2},{3,11},{11,3},{4,12},{12,4},... | collective-permute-start | bytes 1572872 | tf_op jit(solution)/shard_map/ppermute | solution.py:108
  167.9 24.6 %collective-permute-start.37 = (bf16[2,128,1024]{2,1,0:T(8,128)(2,1)S(1)}, bf16[2,128,1024]{2,1,0:T(8,128)(2,1)S(1)}, u32[]{:S(2)}, u32[]{:S(2)}) collective-permute-start(bf16[2,128,1024]{2,1,0:T(8,128)(2,1)S(1)} %collective-permute-done.35.refs_1_), channel_id=1, source_target_pairs={{0,8},{8,0},{1,9},{9,1},{2,10},{10,2},{3,11},{11,3},{4,12},{12,4},... | collective-permute-start | bytes 1572872 | tf_op jit(solution)/shard_map/ppermute | solution.py:108
  168.7 23.9 %collective-permute-start.40 = (bf16[2,128,1024]{2,1,0:T(8,128)(2,1)S(1)}, bf16[2,128,1024]{2,1,0:T(8,128)(2,1)S(1)}, u32[]{:S(2)}, u32[]{:S(2)}) collective-permute-start(bf16[2,128,1024]{2,1,0:T(8,128)(2,1)S(1)} %collective-permute-done.38.refs_5_), channel_id=1, source_target_pairs={{0,8},{8,0},{1,9},{9,1},{2,10},{10,2},{3,11},{11,3},{4,12},{12,4},... | collective-permute-start | bytes 1572872 | tf_op jit(solution)/shard_map/ppermute | solution.py:108
  197.2 22.3 %all-to-all-start.1 = ((bf16[4,96,1024]{2,1,0:T(8,128)(2,1)}), bf16[4,96,1024]{2,1,0:T(8,128)(2,1)}, u32[]{:S(2)}, u32[]{:S(2)}) async-start(bf16[4,96,1024]{2,1,0:T(8,128)(2,1)} %bitcast.145), calls=%async_computation.1 | async-start | bytes 1572864 | tf_op jit(solution)/shard_map/all_to_all | solution.py:223
  314.1 39.8 %collective-permute-start.49 = (bf16[2,4,128,512]{3,2,1,0:T(8,128)(2,1)S(1)}, bf16[2,4,128,512]{3,2,1,0:T(8,128)(2,1)S(1)}, u32[]{:S(2)}, u32[]{:S(2)}) collective-permute-start(bf16[2,4,128,512]{3,2,1,0:T(8,128)(2,1)S(1)} %get-tuple-element.276), channel_id=1, source_target_pairs={{0,4},{4,0},{1,5},{5,1},{2,6},{6,2},{3,7},{7,3},{8,12},{12,8},{9,1... | collective-permute-start | bytes 3145736 | tf_op jit(solution)/shard_map/ppermute | solution.py:108
  322.5 31.4 %collective-permute-start.50 = (bf16[2,4,128,512]{3,2,1,0:T(8,128)(2,1)S(1)}, bf16[2,4,128,512]{3,2,1,0:T(8,128)(2,1)S(1)}, u32[]{:S(2)}, u32[]{:S(2)}) collective-permute-start(bf16[2,4,128,512]{3,2,1,0:T(8,128)(2,1)S(1)} %get-tuple-element.277), channel_id=1, source_target_pairs={{0,16},{16,0},{1,17},{17,1},{2,18},{18,2},{3,19},{19,3},{4,20},{20... | collective-permute-start | bytes 3145736 | tf_op jit(solution)/shard_map/ppermute | solution.py:108
  329.5 45.6 %collective-permute-start.80 = (bf16[2,128,1024]{2,1,0:T(8,128)(2,1)}, bf16[2,128,1024]{2,1,0:T(8,128)(2,1)}, u32[]{:S(2)}, u32[]{:S(2)}) collective-permute-start(bf16[2,128,1024]{2,1,0:T(8,128)(2,1)} %get-tuple-element.372), channel_id=1, source_target_pairs={{0,4},{4,0},{1,5},{5,1},{2,6},{6,2},{3,7},{7,3},{8,12},{12,8},{9,1... | collective-permute-start | bytes 1572872 | tf_op jit(solution)/shard_map/ppermute | solution.py:108
  332.5 44.9 %collective-permute-start.69 = (bf16[2,4,128,384]{3,2,1,0:T(8,128)(2,1)}, bf16[2,4,128,384]{3,2,1,0:T(8,128)(2,1)}, u32[]{:S(2)}, u32[]{:S(2)}) collective-permute-start(bf16[2,4,128,384]{3,2,1,0:T(8,128)(2,1)} %get-tuple-element.345), channel_id=1, source_target_pairs={{0,4},{4,0},{1,5},{5,1},{2,6},{6,2},{3,7},{7,3},{8,12},{12,8},{9,1... | collective-permute-start | bytes 2359304 | tf_op jit(solution)/shard_map/ppermute | solution.py:108
  334.5 43.5 %collective-permute-start.70 = (bf16[2,4,128,384]{3,2,1,0:T(8,128)(2,1)}, bf16[2,4,128,384]{3,2,1,0:T(8,128)(2,1)}, u32[]{:S(2)}, u32[]{:S(2)}) collective-permute-start(bf16[2,4,128,384]{3,2,1,0:T(8,128)(2,1)} %get-tuple-element.346), channel_id=1, source_target_pairs={{0,16},{16,0},{1,17},{17,1},{2,18},{18,2},{3,19},{19,3},{4,20},{20... | collective-permute-start | bytes 2359304 | tf_op jit(solution)/shard_map/ppermute | solution.py:108
  359.9 32.2 %all-to-all-start.3 = ((bf16[4,96,1024]{2,1,0:T(8,128)(2,1)}), bf16[4,96,1024]{2,1,0:T(8,128)(2,1)S(1)}, u32[]{:S(2)}, u32[]{:S(2)}) async-start(bf16[4,96,1024]{2,1,0:T(8,128)(2,1)} %bitcast.49), calls=%async_computation.3 | async-start | bytes 1572864 | tf_op jit(solution)/shard_map/all_to_all | solution.py:223
  395.0 20.8 %collective-permute-start.81 = (bf16[2,128,1024]{2,1,0:T(8,128)(2,1)}, bf16[2,128,1024]{2,1,0:T(8,128)(2,1)S(1)}, u32[]{:S(2)}, u32[]{:S(2)}) collective-permute-start(bf16[2,128,1024]{2,1,0:T(8,128)(2,1)} %copy-done.170), channel_id=1, source_target_pairs={{0,16},{16,0},{1,17},{17,1},{2,18},{18,2},{3,19},{19,3},{4,20},{20... | collective-permute-start | bytes 1572872 | tf_op jit(solution)/shard_map/ppermute | solution.py:108
  396.0 35.6 %collective-permute-start.66 = (bf16[2,2,128,512]{3,2,1,0:T(8,128)(2,1)}, bf16[2,2,128,512]{3,2,1,0:T(8,128)(2,1)S(1)}, u32[]{:S(2)}, u32[]{:S(2)}) collective-permute-start(bf16[2,2,128,512]{3,2,1,0:T(8,128)(2,1)} %copy-done.171), channel_id=1, source_target_pairs={{0,2},{1,3},{2,0},{3,1},{4,6},{5,7},{6,4},{7,5},{8,10},{9,11},{10,... | collective-permute-start | bytes 1572872 | tf_op jit(solution)/shard_map/ppermute | solution.py:108
  405.0 36.5 %collective-permute-start.55 = (bf16[2,128,1024]{2,1,0:T(8,128)(2,1)S(1)}, bf16[2,128,1024]{2,1,0:T(8,128)(2,1)S(1)}, u32[]{:S(2)}, u32[]{:S(2)}) collective-permute-start(bf16[2,128,1024]{2,1,0:T(8,128)(2,1)S(1)} %get-tuple-element.306), channel_id=1, source_target_pairs={{0,4},{4,0},{1,5},{5,1},{2,6},{6,2},{3,7},{7,3},{8,12},{12,8},{9,1... | collective-permute-start | bytes 1572872 | tf_op jit(solution)/shard_map/ppermute | solution.py:108
  405.5 36.8 %collective-permute-start.56 = (bf16[2,128,1024]{2,1,0:T(8,128)(2,1)S(1)}, bf16[2,128,1024]{2,1,0:T(8,128)(2,1)S(1)}, u32[]{:S(2)}, u32[]{:S(2)}) collective-permute-start(bf16[2,128,1024]{2,1,0:T(8,128)(2,1)S(1)} %get-tuple-element.307), channel_id=1, source_target_pairs={{0,16},{16,0},{1,17},{17,1},{2,18},{18,2},{3,19},{19,3},{4,20},{20... | collective-permute-start | bytes 1572872 | tf_op jit(solution)/shard_map/ppermute | solution.py:108
  413.2 25.5 %collective-permute-start.73 = (bf16[2,2,128,384]{3,2,1,0:T(8,128)(2,1)S(1)}, bf16[2,2,128,384]{3,2,1,0:T(8,128)(2,1)S(1)}, u32[]{:S(2)}, u32[]{:S(2)}) collective-permute-start(bf16[2,2,128,384]{3,2,1,0:T(8,128)(2,1)S(1)} %get-tuple-element.352), channel_id=1, source_target_pairs={{0,2},{1,3},{2,0},{3,1},{4,6},{5,7},{6,4},{7,5},{8,10},{9,11},{10,... | collective-permute-start | bytes 1179656 | tf_op jit(solution)/shard_map/ppermute | solution.py:108
  415.9 24.2 %collective-permute-start.60 = (f32[69,512]{1,0:T(8,128)S(1)}, f32[69,512]{1,0:T(8,128)S(1)}, u32[]{:S(2)}, u32[]{:S(2)}) collective-permute-start(f32[69,512]{1,0:T(8,128)S(1)} %add.61), channel_id=1, source_target_pairs={{0,4},{4,0},{1,5},{5,1},{2,6},{6,2},{3,7},{7,3},{8,12},{12,8},{9,1... | collective-permute-start | bytes 423944 | tf_op jit(solution)/shard_map/ppermute | solution.py:108
  438.7 20.0 %collective-permute-start.67 = (bf16[2,1,128,512]{3,2,1,0:T(8,128)(2,1)S(1)}, bf16[2,1,128,512]{3,2,1,0:T(8,128)(2,1)S(1)}, u32[]{:S(2)}, u32[]{:S(2)}) collective-permute-start(bf16[2,1,128,512]{3,2,1,0:T(8,128)(2,1)S(1)} %get-tuple-element.333), channel_id=1, source_target_pairs={{0,1},{1,0},{2,3},{3,2},{4,5},{5,4},{6,7},{7,6},{8,9},{9,8},{10,11... | collective-permute-start | bytes 786440 | tf_op jit(solution)/shard_map/ppermute | solution.py:108
  443.3 23.5 %collective-permute-start.57 = (bf16[1,128,1024]{2,1,0:T(8,128)(2,1)S(1)}, bf16[1,128,1024]{2,1,0:T(8,128)(2,1)S(1)}, u32[]{:S(2)}, u32[]{:S(2)}) collective-permute-start(bf16[1,128,1024]{2,1,0:T(8,128)(2,1)S(1)} %get-tuple-element.310), channel_id=1, source_target_pairs={{0,16},{16,0},{1,17},{17,1},{2,18},{18,2},{3,19},{19,3},{4,20},{20... | collective-permute-start | bytes 786440 | tf_op jit(solution)/shard_map/ppermute | solution.py:108
  (258 other events, 2213.5 us)
